TPU v7x, 32 devices: a whole 2x2x4 slice. The times are simulated.
32 devices in a mesh: groups: 2 (over y), ep: 8 (over z, x), tp: 2 (over core).
Axes of the slice: x: 2, y: 2, z: 4, core: 2. Of those that a mesh axis runs over, the one named last changes fastest.
Arguments:
- partials: bfloat16 [2, 1024, 3840], P('tp', ('groups', 'ep')), parts along dimension 1, may hold values from -6 to 6
- residual: bfloat16 [1024, 3840], P(('groups', 'ep')), parts along dimension 0, may hold values from -6 to 6
- norm_gain: float32 [3840], replicated, may hold values from 0.1 to 1.9
- router_logits: float32 [1024, 8], P(('groups', 'ep')), parts along dimension 0, may hold values from -8 to 8
- expert_ids: int32 [1024, 8], P(('groups', 'ep')), parts along dimension 0, may hold values from 0 to 7, as said below
- gate_packed: float32 [8, 640, 1024], P('ep', None, 'tp'), may hold values from 0 to 16777215
- up_packed: float32 [8, 640, 1024], P('ep', None, 'tp'), may hold values from 0 to 16777215, as said below
- down_packed: float32 [8, 640, 1024], P('ep', 'tp'), may hold values from 0 to 16777215, as said below
- gate_scale: float32 [8, 1024], P('ep', 'tp'), may hold values from 0.5 to 2
- up_scale: float32 [8, 1024], P('ep', 'tp'), may hold values from 0.5 to 2
- down_scale: float32 [8, 3840], P('ep', 'tp'), may hold values from 1 to 6
Outputs:
- mixed: bfloat16 [1024, 3840], P(('groups', 'ep', 'tp')), parts along dimension 0
There are 2 independent parts, one for each index of `groups`. A program takes and returns all parts, laid end to end along the dimension named above; an argument that names none is the same for every part. Nothing has to cross between parts.
Inputs may be any that keep to these rules, and one draw needn't show every extreme that they name: `expert_ids`: the 8 experts of a row differ. In each aligned block of 32 rows every expert that the block names is named by exactly 32 of its rows, and one expert, drawn afresh for each part, is named in every block. `up_packed`: whole numbers. `down_packed`: whole numbers.
All inputs are finite; a program needn't handle non-finite values.
Results may differ from a plain program's by a relative error of at most 0.017.
Values may be sent and summed in bfloat16 or wider, within the bound.
No kernel may reach another device: no remote copies, remote signals or barrier semaphores. Data moves between devices by JAX's collectives and lax.ppermute only.
A program may use at most 128 MiB of HBM per device.

v0:
```python
import math

import jax
import jax.numpy as jnp
import numpy as np
from jax import lax
from jax.experimental import pallas as pl
from jax.experimental.pallas import tpu as pltpu
from jax.sharding import PartitionSpec as P

HB = 128


level_variance = 21.25
digit_powers = [1.0, 16.0, 256.0, 4096.0, 65536.0, 1048576.0]


def hadamard(table_order):
    indices = jnp.arange(table_order, dtype=jnp.int32)
    common_bits = jnp.bitwise_and(indices[:, None], indices[None, :])
    parity = jnp.zeros((table_order, table_order), jnp.int32)
    for bit_pos in range(table_order.bit_length() - 1):
        parity = parity + jnp.bitwise_and(jnp.right_shift(common_bits, bit_pos), 1)
    sign_table = 1 - 2 * (parity % 2)
    return sign_table.astype(jnp.float32) * (1.0 / math.sqrt(table_order))


def rotate_blocks(values, hadamard_table):
    feature_count = values.shape[-1]
    block_size = hadamard_table.shape[0]
    shaped = values.reshape(values.shape[:-1] + (feature_count // block_size, block_size))
    turned = jnp.einsum("rij,jk->rik", shaped, hadamard_table, precision=lax.Precision.HIGHEST)
    return turned.reshape(values.shape)


def unpack_levels(packed):
    pieces = []
    for power in digit_powers:
        digit = jnp.mod(jnp.floor(packed / power), 16.0) - 7.5
        pieces.append(digit.astype(jnp.bfloat16))
    levels = jnp.stack(pieces, axis=1)
    return levels.reshape((packed.shape[0] * 6, packed.shape[1]))


def prepare(stream, norm_gain, hadamard_table):
    mean_square = jnp.mean(stream * stream, axis=-1, keepdims=True)
    normed = stream * lax.rsqrt(mean_square + 1e-06) * norm_gain
    return rotate_blocks(normed, hadamard_table).astype(jnp.bfloat16)


def route_weights(router_logits):
    lifted = jax.nn.sigmoid(router_logits)
    return lifted / jnp.sum(lifted, axis=-1, keepdims=True)


def block_slots(expert_ids, block_rows, expert_count):
    expert_range = jnp.arange(expert_count, dtype=jnp.int32)
    member = jnp.sum(
        (expert_ids[:, :, None] == expert_range[None, None, :]).astype(jnp.int32), axis=1
    )
    blocks = member.reshape(-1, block_rows, expert_count)
    before = (jnp.cumsum(blocks, axis=1) - blocks).reshape(-1, expert_count)
    return jnp.take_along_axis(before, expert_ids, axis=1)


def place_rows(rotated, target, slot_count):
    slot_ids = jnp.arange(slot_count, dtype=jnp.int32)
    hits = (target[:, :, None] == slot_ids[None, None, :]).astype(jnp.bfloat16)
    placement = jnp.sum(hits, axis=1)
    return jnp.dot(placement.T, rotated, preferred_element_type=jnp.float32).astype(jnp.bfloat16)


def expert_rows(
    row_block, gate_levels, up_levels, down_levels, gate_row, up_row, down_row, hadamard_table
):
    feature_count = row_block.shape[1]
    gate_proj = jnp.dot(row_block, gate_levels, preferred_element_type=jnp.float32) * (
        gate_row * (1.0 / math.sqrt(level_variance * feature_count))
    )
    up_proj = jnp.dot(row_block, up_levels, preferred_element_type=jnp.float32) * (
        up_row * (1.0 / math.sqrt(level_variance * feature_count))
    )
    hidden = rotate_blocks(jax.nn.silu(gate_proj) * up_proj, hadamard_table).astype(jnp.bfloat16)
    whole_hidden = lax.all_gather(hidden, "tp", axis=1, tiled=True)
    hidden_count = whole_hidden.shape[1]
    expert_out = lax.dot_general(
        whole_hidden, down_levels, (((1,), (1,)), ((), ())), preferred_element_type=jnp.float32
    ) * (down_row * (1.0 / math.sqrt(level_variance * hidden_count)))
    return expert_out.astype(jnp.bfloat16)


def routed_shards(
    partials,
    residual,
    norm_gain,
    router_logits,
    expert_ids,
    gate_packed,
    up_packed,
    down_packed,
    gate_scale,
    up_scale,
    down_scale,
):
    tp_count = lax.axis_size("tp")
    ep_count = lax.axis_size("ep")
    tp_index = lax.axis_index("tp")
    block_tokens = residual.shape[0]
    half_rows = block_tokens // tp_count
    pick_count = expert_ids.shape[1]
    experts = ep_count * gate_packed.shape[0]
    capacity = max(2, half_rows * pick_count // experts)
    hadamard_table = hadamard(HB)
    gate_levels = unpack_levels(gate_packed[0])
    up_levels = unpack_levels(up_packed[0])
    down_levels = unpack_levels(down_packed[0])
    weights = route_weights(router_logits)
    slot_rank = block_slots(expert_ids, half_rows, experts)
    half_of_row = (jnp.arange(block_tokens, dtype=jnp.int32) // half_rows)[:, None]
    summed_rows = lax.psum_scatter(partials, "tp", scatter_dimension=1, tiled=True).astype(
        jnp.float32
    )
    own_resid = lax.dynamic_slice_in_dim(residual, tp_index * half_rows, half_rows, 0)
    stream = own_resid.astype(jnp.float32) + summed_rows[0]
    rotated = prepare(stream, norm_gain, hadamard_table)
    own_ids = lax.dynamic_slice_in_dim(expert_ids, tp_index * half_rows, half_rows, 0)
    own_slots = lax.dynamic_slice_in_dim(slot_rank, tp_index * half_rows, half_rows, 0)
    outgoing = place_rows(rotated, own_ids * capacity + own_slots, experts * capacity)
    outgoing = outgoing.reshape(experts, capacity, -1)
    arrived = lax.all_to_all(outgoing, "ep", split_axis=0, concat_axis=0, tiled=True)
    paired = lax.all_gather(arrived, "tp", axis=0, tiled=True)
    produced = expert_rows(
        paired.reshape(-1, paired.shape[2]),
        gate_levels,
        up_levels,
        down_levels,
        gate_scale[0],
        up_scale[0],
        down_scale[0],
        hadamard_table,
    )
    served = produced.reshape(tp_count, ep_count, arrived.shape[1], -1)
    returned = lax.all_to_all(served, "ep", split_axis=1, concat_axis=1, tiled=True)
    position = half_of_row * (experts * capacity) + expert_ids * capacity + slot_rank
    flat_back = returned.reshape(-1, returned.shape[-1])
    mixture = jnp.zeros((block_tokens, flat_back.shape[1]), jnp.float32)
    for pick in range(pick_count):
        fetched = jnp.take(flat_back, position[:, pick], axis=0)
        mixture = mixture + weights[:, pick : pick + 1] * fetched.astype(jnp.float32)
    arranged = mixture.reshape(tp_count, half_rows, -1)
    mixed = lax.all_to_all(
        arranged.astype(jnp.bfloat16), "tp", split_axis=0, concat_axis=2, tiled=True
    ).astype(arranged.dtype)
    return mixed[0].astype(jnp.bfloat16)


UNIT = 64
SPAN = 6 * UNIT
ALONE = ((0, None, 1), (0, None, 0))
ROUND = ((0, 0, 1), (0, 1, 0), (0, 0, 0), (0, 1, 1))
NEAR = ALONE + tuple((slot + 1, place, half) for slot, place, half in ROUND)
EXTRA = 128


def level_order():
    order = np.zeros((SPAN, SPAN), np.float32)
    for plane in range(6):
        for row in range(UNIT):
            order[6 * row + plane, plane * UNIT + row] = 1.0
    return order


def sign_blocks(count):
    indices = np.arange(HB)
    common = indices[:, None] & indices[None, :]
    parity = np.zeros((HB, HB), np.int64)
    for bit_pos in range(HB.bit_length() - 1):
        parity += (common >> bit_pos) & 1
    return np.kron(np.eye(count), 1.0 - 2.0 * (parity % 2)).astype(np.float32)


def fold(values, span):
    return jnp.concatenate(
        [values[:, i * span : (i + 1) * span] for i in range(values.shape[1] // span)], axis=0
    )


def unfold(values, rows):
    return jnp.concatenate(
        [values[i * rows : (i + 1) * rows] for i in range(values.shape[0] // rows)], axis=1
    )


def signed_product(values, signs):
    high = values.astype(jnp.bfloat16)
    low = (values - high.astype(jnp.float32)).astype(jnp.bfloat16)
    both = jnp.concatenate([high, low], axis=0)
    product = jnp.dot(both, signs, preferred_element_type=jnp.float32)
    rows = values.shape[0]
    return (product[:rows] + product[rows:]) * (1.0 / math.sqrt(HB))


def core_of(side):
    core = lax.axis_index("tp")
    return core if side == 0 else 1 - core


def own_rows(half, core):
    return pl.ds(pl.multiple_of(core * half, half), half)


def first_kernel(
    partial,
    resid,
    gain,
    signs,
    all_logits,
    all_ids,
    words,
    base,
    gain_out,
    signs_out,
    tail,
    words_out,
    rows_in,
    logits,
    ids,
    sems,
):
    copies = [
        pltpu.make_async_copy(partial, rows_in.at[0], sems.at[0]),
        pltpu.make_async_copy(resid, rows_in.at[1], sems.at[1]),
        pltpu.make_async_copy(gain, gain_out, sems.at[2]),
        pltpu.make_async_copy(signs, signs_out, sems.at[3]),
    ]
    small = [
        pltpu.make_async_copy(all_logits, logits, sems.at[4]),
        pltpu.make_async_copy(all_ids, ids, sems.at[5]),
    ]
    later = pltpu.make_async_copy(words, words_out, sems.at[6])
    for copy in small + copies + [later]:
        copy.start()
    for copy in small:
        copy.wait()
    lifted = jax.nn.sigmoid(logits[...])
    route = lifted / jnp.sum(lifted, axis=0, keepdims=True)
    picks, rows = route.shape
    expert = lax.broadcasted_iota(jnp.int32, (picks, rows), 0)
    spread = jnp.zeros((picks, rows), jnp.float32)
    for pick in range(picks):
        hit = expert == ids[pick : pick + 1, :]
        spread = spread + jnp.where(hit, route[pick : pick + 1, :], 0.0)
    high = spread.astype(jnp.bfloat16).astype(jnp.float32)
    blank = jnp.zeros((EXTRA - 2 * picks, rows), jnp.float32)
    columns = jnp.concatenate([high, spread - high, blank], axis=0)
    tail[...] = columns.T.astype(jnp.bfloat16)
    for copy in copies:
        copy.wait()
    base[...] = rows_in[1].astype(jnp.float32) + rows_in[0].astype(jnp.float32)
    later.wait()


def prep_kernel(side, base, other, gain, signs, tail, out):
    rows, features = out.shape[0], base.shape[1]
    at = own_rows(rows, core_of(side))
    stream = base[at, :] + other[at, :].astype(jnp.float32)
    mean_square = jnp.mean(stream * stream, axis=-1, keepdims=True)
    normed = stream * lax.rsqrt(mean_square + 1e-06) * gain[...].reshape(1, features)
    turned = signed_product(fold(normed, SPAN), signs[...])
    out[:, :features] = unfold(turned, rows).astype(jnp.bfloat16)
    out[:, features:] = tail[at, :]


def unpack_unit(words, out, at, columns):
    whole = words.astype(jnp.int32)
    for plane in range(6):
        digit = jnp.bitwise_and(jnp.right_shift(whole, 4 * plane), 15)
        level = digit.astype(jnp.float32) - 7.5
        out[pl.ds(at + plane * UNIT, UNIT), columns] = level.astype(jnp.bfloat16)


def unpack_all(packed, out, parts):
    def unit(index, carry):
        for source, columns in parts:
            words = packed[pl.ds(pl.multiple_of(index * UNIT, UNIT), UNIT), source]
            unpack_unit(words, out, pl.multiple_of(index * SPAN, SPAN), columns)
        return carry

    lax.fori_loop(0, packed.shape[0] // UNIT, unit, 0)


def unpack_gate_kernel(up, down, gate, out, up_out, down_out, sems):
    copies = [
        pltpu.make_async_copy(up, up_out, sems.at[0]),
        pltpu.make_async_copy(down, down_out, sems.at[1]),
    ]
    for copy in copies:
        copy.start()
    unpack_all(gate, out, ((slice(None), slice(None)),))
    for copy in copies:
        copy.wait()


def unpack_up_kernel(up, out):
    unpack_all(up, out, ((slice(None), slice(None)),))


def unpack_down_kernel(down, scale, order, out, row):
    half = down.shape[1] // 2
    core = lax.axis_index("tp")
    mine = pl.ds(pl.multiple_of(core * half, half), half)
    theirs = pl.ds(pl.multiple_of((1 - core) * half, half), half)
    unpack_all(down, out, ((mine, slice(0, half)), (theirs, slice(half, 2 * half))))
    rest = fold(jnp.broadcast_to(scale[...], (8, scale.shape[1])), SPAN)
    total = jnp.zeros(rest.shape, jnp.float32)
    for _ in range(3):
        term = rest.astype(jnp.bfloat16)
        rest = rest - term.astype(jnp.float32)
        total = total + jnp.dot(term, order[...], preferred_element_type=jnp.float32)
    row[...] = unfold(total, 8)


def slot_row(count, slot, side, part):
    at = slot if side is None else slot + core_of(side)
    return (2 * at + core_of(part)) * count


def hidden_kernel(slots, *refs):
    pieces, (gate, up, gate_row, up_row, signs, hidden, weight, rows_ref) = (
        refs[: len(slots)],
        refs[len(slots) :],
    )
    features = gate.shape[0]
    picks = lax.axis_size("ep")
    for piece, (slot, side, part) in zip(pieces, slots):
        count = piece.shape[0]
        lane = lax.broadcasted_iota(jnp.int32, (count, EXTRA), 1)
        picked = (lane < 2 * picks) & ((lane & (picks - 1)) == lax.axis_index("ep"))
        row = slot_row(count, slot, side, part)
        at = pl.ds(pl.multiple_of(row, count), count)
        rows_ref[at, :] = piece[:, :features]
        tail = jnp.where(picked, piece[:, features:].astype(jnp.float32), 0.0)
        total = jnp.sum(tail, axis=-1, keepdims=True)
        weight[at, :] = jnp.broadcast_to(total, (count, EXTRA))
    scale = 1.0 / math.sqrt(level_variance * features)
    rows = rows_ref[...]
    gate_proj = jnp.dot(rows, gate[...], preferred_element_type=jnp.float32)
    up_proj = jnp.dot(rows, up[...], preferred_element_type=jnp.float32)
    gate_proj, up_proj = gate_proj[: hidden.shape[0]], up_proj[: hidden.shape[0]]
    mixed = jax.nn.silu(gate_proj * (gate_row[...] * scale)) * (up_proj * (up_row[...] * scale))
    turned = signed_product(fold(mixed, 2 * HB), signs[...])
    hidden[...] = unfold(turned, mixed.shape[0])[: hidden.shape[0]].astype(jnp.bfloat16)


def down_kernel(mine, theirs, levels, down_row, weight, *outs):
    half = mine.shape[1]
    contract = (((1,), (1,)), ((), ()))
    produced = lax.dot_general(
        mine[...], levels[:, :half], contract, preferred_element_type=jnp.float32
    ) + lax.dot_general(
        theirs[...], levels[:, half:], contract, preferred_element_type=jnp.float32
    )
    scale = 1.0 / math.sqrt(level_variance * 2 * half)
    produced = produced * (down_row[:1, :] * scale) * weight[:, :1]
    rows = outs[0].shape[0]
    for index, out in enumerate(outs):
        out[...] = produced[index * rows : (index + 1) * rows]


def close_kernel(own, ahead, behind, order, out):
    total = own[...] + (ahead[...].astype(jnp.float32) + behind[...].astype(jnp.float32))
    folded = fold(total.astype(jnp.bfloat16), SPAN)
    placed = jnp.dot(folded, order[...], preferred_element_type=jnp.float32)
    out[...] = unfold(placed, total.shape[0]).astype(jnp.bfloat16)


def on_chip(values):
    return pltpu.with_memory_space_constraint(values, pltpu.VMEM)


def whole_call(
    kernel, outs, name, *args, scratch=(), work=0, after=None, fetched=0, plain=False
):
    vmem = pl.BlockSpec(memory_space=pltpu.VMEM)
    specs = [pl.BlockSpec(memory_space=pltpu.HBM)] * fetched + [vmem] * (len(args) - fetched)
    stay = [pltpu.with_memory_space_constraint(a, pltpu.HBM) for a in args[:fetched]]
    args = (*stay, *args[fetched:])
    body = kernel
    if after is not None:
        specs, args = [pl.BlockSpec(memory_space=pl.ANY)] + specs, (after, *args)
        body = lambda first, *refs: kernel(*refs)
    return pl.pallas_call(
        body,
        in_specs=specs,
        out_specs=[vmem] * len(outs),
        out_shape=[(jax.ShapeDtypeStruct if plain else pltpu.VMEM)(*out) for out in outs],
        scratch_shapes=list(scratch),
        compiler_params=pltpu.CompilerParams(vmem_limit_bytes=12 << 20),
        cost_estimate=pl.CostEstimate(flops=work, bytes_accessed=0, transcendentals=0),
        name=name,
    )(*args)


def dense_shards(
    partials,
    residual,
    norm_gain,
    router_logits,
    expert_ids,
    gate_packed,
    up_packed,
    down_packed,
    gate_scale,
    up_scale,
    down_scale,
):
    ep_count = lax.axis_size("ep")
    tp_index = lax.axis_index("tp")
    block_rows, features = residual.shape
    half = block_rows // 2
    around = list(range(0, ep_count, 2)) + list(range(ep_count - 1, 0, -2))

    def device(spot, core):
        return around[spot % ep_count] * 2 + core

    def hop(values):
        spots = range(ep_count)
        pairs = [(device(s, 0), device(s + 1, 0)) for s in spots]
        pairs += [(device(s, 1), device(s - 1, 1)) for s in spots]
        return lax.ppermute(values, ("ep", "tp"), pairs)

    def turn_hop(values, step):
        pairs = [(device(s, c), device(s + step, c)) for s in range(ep_count) for c in range(2)]
        return lax.ppermute(values, ("ep", "tp"), pairs)

    def swap(values):
        return lax.ppermute(values, "tp", [(0, 1), (1, 0)])

    def own_half(values, other=False):
        at = (1 - tp_index if other else tp_index) * half
        return lax.dynamic_slice_in_dim(values, at, half, 0)

    turn = sign_blocks(SPAN // HB) @ level_order()
    turn = jnp.asarray(turn, jnp.bfloat16)
    turn_hidden = jnp.asarray(sign_blocks(2), jnp.bfloat16)
    order = jnp.asarray(level_order(), jnp.bfloat16)
    back = jnp.asarray(level_order().T, jnp.bfloat16)

    wide = features + EXTRA
    first = whole_call(
        first_kernel,
        [
            ((block_rows, features), jnp.float32),
            (norm_gain.shape, jnp.float32),
            (turn.shape, turn.dtype),
            ((block_rows, EXTRA), jnp.bfloat16),
            (gate_packed.shape[1:], jnp.float32),
        ],
        "first",
        partials[0],
        residual,
        norm_gain,
        turn,
        router_logits.T,
        expert_ids.T,
        gate_packed[0],
        fetched=7,
        scratch=[
            pltpu.VMEM((2, block_rows, features), jnp.bfloat16),
            pltpu.VMEM(router_logits.T.shape, jnp.float32),
            pltpu.VMEM(expert_ids.T.shape, jnp.int32),
            pltpu.SemaphoreType.DMA((7,)),
        ],
    )
    base, gain, turn, tail, gate_words = first
    other_partial = swap(partials[0])

    def prepared(side, after=None):
        (rows,) = whole_call(
            lambda *refs: prep_kernel(side, *refs),
            [((half, wide), jnp.bfloat16)],
            "prep",
            base,
            other_partial,
            gain,
            turn,
            tail,
            after=after,
        )
        return rows

    lead = [prepared(1)]
    follow = [prepared(0, after=lead[0])]

    packed_rows, columns = gate_packed.shape[1:]

    levels = ((6 * packed_rows, columns), jnp.bfloat16)
    gate, up_words, down_words = whole_call(
        unpack_gate_kernel,
        [levels, (up_packed.shape[1:], jnp.float32), (down_packed.shape[1:], jnp.float32)],
        "unpack_gate",
        up_packed[0],
        down_packed[0],
        on_chip(gate_words),
        fetched=2,
        scratch=[pltpu.SemaphoreType.DMA((2,))],
        after=follow[0],
        work=10**10,
    )
    down_rows, hidden_count = down_packed.shape[1:]
    down_features = 6 * down_rows

    def hold(values, *done):
        return lax.optimization_barrier((values, done))[0]

    def expert_hidden(pieces, slots, count, work=10**9):
        hidden, weight = whole_call(
            lambda *refs: hidden_kernel(slots, *refs),
            [
                ((block_rows * count, columns), jnp.bfloat16),
                ((block_rows * count, EXTRA), jnp.float32),
            ],
            "hidden_part",
            *pieces,
            on_chip(gate),
            on_chip(up),
            gate_scale,
            up_scale,
            turn_hidden,
            scratch=[pltpu.VMEM((max(2, count) * block_rows, features), jnp.bfloat16)],
            work=work,
        )
        return hidden, weight, swap(hidden)

    def expert_out(stage, after=None):
        hidden, weight, theirs = stage
        count = hidden.shape[0] // block_rows
        return whole_call(
            down_kernel,
            [((block_rows, down_features), jnp.float32)] * count,
            "down_part",
            hidden,
            theirs,
            on_chip(down),
            down_row,
            weight,
            work=2 * block_rows * count * hidden_count * down_features,
            after=after,
        )

    lead.append(hop(lead[0]))
    follow.append(hop(follow[0]))
    (up,) = whole_call(
        unpack_up_kernel, [levels], "unpack_up", on_chip(up_words), after=gate, work=10**10
    )
    lead[1] = hold(lead[1], gate)
    lead.append(hop(lead[1]))
    follow.append(hop(follow[1]))
    lead[2] = hold(lead[2], up)
    down, down_row = whole_call(
        unpack_down_kernel,
        [((down_features, hidden_count), jnp.bfloat16), ((8, down_features), jnp.float32)],
        "unpack_down",
        on_chip(down_words),
        down_scale,
        order,
        after=up,
        work=10**10,
    )
    lead.append(hop(lead[2]))
    follow.append(hop(follow[2]))
    lead[3] = hold(lead[3], down_row)
    lead.append(hop(lead[3]))

    def pieces(distance):
        ours = lead[distance], follow[distance]
        return [piece for own in ours for piece in (own, swap(own))]

    lead[2], follow[2] = hold(lead[2], down_row), hold(follow[2], down_row)
    lead.append(hop(lead[2]))
    follow.append(hop(follow[2]))
    beside = pieces(3)
    near = expert_hidden(hold([lead[0], follow[0]] + pieces(1), beside[1]), NEAR, 3, work=10**10)
    second = expert_hidden(hold(pieces(2), beside[1]), ROUND, 2, work=10**10)
    third = expert_hidden(beside, ROUND, 2, work=10**9)
    lead[4] = hold(lead[4], near[1], second[1])
    edge = expert_hidden(hold([lead[4], swap(lead[4])], third[1]), ALONE, 1, work=10**9)

    far = ep_count // 2

    def join(part, came):
        return (part + came.astype(jnp.float32)).astype(jnp.bfloat16)

    ahead, behind = {}, {}
    behind[3], ahead[3] = expert_out(third)
    (edge,) = expert_out(edge, after=ahead[3])
    went_ahead = turn_hop(edge[:half].astype(jnp.bfloat16), 1)
    went_behind = turn_hop(edge[half:].astype(jnp.bfloat16), -1)
    behind[2], ahead[2] = expert_out(second, after=went_behind)
    own, behind[1], ahead[1] = expert_out(near, after=went_behind)
    for distance in range(far - 1, 0, -1):
        if distance == far - 1:
            send_ahead = jnp.concatenate(
                [
                    join(ahead[distance][:half], went_ahead),
                    ahead[distance][half:].astype(jnp.bfloat16),
                ],
                axis=0,
            )
            send_behind = jnp.concatenate(
                [
                    behind[distance][:half].astype(jnp.bfloat16),
                    join(behind[distance][half:], went_behind),
                ],
                axis=0,
            )
        else:
            send_ahead = join(ahead[distance], went_ahead)
            send_behind = join(behind[distance], went_behind)
        went_ahead, went_behind = turn_hop(send_ahead, 1), turn_hop(send_behind, -1)
    (mixed,) = whole_call(
        close_kernel,
        [(own.shape, jnp.bfloat16)],
        "close",
        own,
        went_ahead,
        went_behind,
        back,
    )
    mine, theirs = own_half(mixed), swap(own_half(mixed, other=True))
    first = jnp.where(tp_index == 0, mine, theirs)
    second = jnp.where(tp_index == 0, theirs, mine)
    return jnp.concatenate([first, second], axis=1)


def solution(mesh):
    def shards(*args):
        experts = lax.axis_size("ep") * args[5].shape[0]
        every_row_everywhere = args[4].shape[1] == experts
        one_each = args[5].shape[0] == 1 and lax.axis_size("tp") == 2
        if every_row_everywhere and one_each and lax.axis_size("ep") == 8:
            return dense_shards(*args)
        return routed_shards(*args)

    return jax.shard_map(
        shards,
        mesh=mesh,
        in_specs=(
            P("tp", ("groups", "ep"), None),
            P(("groups", "ep"), None),
            P(),
            P(("groups", "ep"), None),
            P(("groups", "ep"), None),
            P("ep", None, "tp"),
            P("ep", None, "tp"),
            P("ep", "tp", None),
            P("ep", "tp"),
            P("ep", "tp"),
            P("ep", "tp"),
        ),
        out_specs=P(("groups", "ep", "tp"), None),
        check_vma=False,
    )
```

profile of v0, /device:TPU:0, one launch (start us, length us, event | category | flops | bytes accessed | tf_op | source)
XLA Modules:
  0.0 66.3 jit_solution(8810642835153147789)
XLA Ops:
  0.0 0.5 collective-permute-start
  0.5 1.8 %first.1 = (f32[64,3840]{1,0:T(8,128)S(1)}, f32[3840]{0:T(1024)S(1)}, bf16[384,384]{1,0:T(8,128)(2,1)S(1)}, bf16[64,128]{1,0:T(8,128)(2,1)S(1)}, f32[640,512]{1,0:T(8,128)S(1)}) custom-call(bf16[64,3840]{1,0:T(8,128)(2,1)} %bitcast.8, bf16[64,3840]{1,0:T(8,128)(2,1)} %resid.1, f32[3840]{0:T(1024)} %gain.1, bf16[384,384]{1,0:T(8,128)(2,1)} %constant.20.clone.signs, ...), custom_call_target="tpu_custom_call" | custom-call | tf_op jit(solution)/shard_map/first/pallas_call | solution.py:392
  2.3 0.6 prep.2.first.refs_0_
  2.9 2.9 %collective-permute-start.1 = (bf16[32,3968]{1,0:T(8,128)(2,1)S(1)}, bf16[32,3968]{1,0:T(8,128)(2,1)S(1)}, u32[]{:S(2)}, u32[]{:S(2)}) collective-permute-start(bf16[32,3968]{1,0:T(8,128)(2,1)S(1)} %prep.2.first.refs_0_), channel_id=1, source_target_pairs={{0,4},{4,8},{8,12},{12,14},{14,10},{10,6},{6,2},{2,0},{1,3},{5,1},... | collective-permute-start | bytes 761864 | tf_op jit(solution)/shard_map/ppermute | solution.py:430
  5.8 0.6 prep.3.first.refs_1_
  6.4 1.6 %collective-permute-start.5 = (bf16[32,3968]{1,0:T(8,128)(2,1)S(1)}, bf16[32,3968]{1,0:T(8,128)(2,1)S(1)}, u32[]{:S(2)}, u32[]{:S(2)}) collective-permute-start(bf16[32,3968]{1,0:T(8,128)(2,1)S(1)} %prep.3.first.refs_1_), channel_id=1, source_target_pairs={{0,4},{4,8},{8,12},{12,14},{14,10},{10,6},{6,2},{2,0},{1,3},{5,1},... | collective-permute-start | bytes 761864 | tf_op jit(solution)/shard_map/ppermute | solution.py:430
  8.1 1.7 %unpack_gate.1 = (bf16[3840,512]{1,0:T(8,128)(2,1)S(1)}, f32[640,512]{1,0:T(8,128)S(1)}, f32[320,1024]{1,0:T(8,128)S(1)}) custom-call(bf16[32,3968]{1,0:T(8,128)(2,1)S(1)} %prep.3.first.refs_1_, f32[640,512]{1,0:T(8,128)} %bitcast.11, f32[320,1024]{1,0:T(8,128)} %bitcast.12, f32[640,512]{1,0:T(8,128)S(1)} %get-tuple-element.52.refs_2_), custom_call_target="tpu_custom_call" | custom-call | flops 10000000000 | tf_op jit(solution)/shard_map/unpack_gate/pallas_call | solution.py:392
  10.0 2.1 %collective-permute-start.2 = (bf16[32,3968]{1,0:T(8,128)(2,1)S(1)}, bf16[32,3968]{1,0:T(8,128)(2,1)S(1)}, u32[]{:S(2)}, u32[]{:S(2)}) collective-permute-start(bf16[32,3968]{1,0:T(8,128)(2,1)S(1)} %collective-permute-done.1.refs_2_), channel_id=1, source_target_pairs={{0,4},{4,8},{8,12},{12,14},{14,10},{10,6},{6,2},{2,0},{1,3},{5,1},... | collective-permute-start | bytes 761864 | tf_op jit(solution)/shard_map/ppermute | solution.py:430
  12.1 1.4 %unpack_up.1.first.refs_5_.refs_7_.refs_3_ = bf16[3840,512]{1,0:T(8,128)(2,1)S(1)} custom-call(bf16[3840,512]{1,0:T(8,128)(2,1)S(1)} %get-tuple-element.53.first.refs_4_.refs_6_.refs_2_, f32[640,512]{1,0:T(8,128)S(1)} %get-tuple-element.55.refs_0_), custom_call_target="tpu_custom_call" | custom-call | flops 10000000000 | tf_op jit(solution)/shard_map/unpack_up/pallas_call | solution.py:392
  13.5 1.6 %collective-permute-start.6 = (bf16[32,3968]{1,0:T(8,128)(2,1)S(1)}, bf16[32,3968]{1,0:T(8,128)(2,1)S(1)}, u32[]{:S(2)}, u32[]{:S(2)}) collective-permute-start(bf16[32,3968]{1,0:T(8,128)(2,1)S(1)} %collective-permute-done.5.refs_4_), channel_id=1, source_target_pairs={{0,4},{4,8},{8,12},{12,14},{14,10},{10,6},{6,2},{2,0},{1,3},{5,1},... | collective-permute-start | bytes 761864 | tf_op jit(solution)/shard_map/ppermute | solution.py:430
  15.1 1.2 %collective-permute-done.2.refs_0_ = bf16[32,3968]{1,0:T(8,128)(2,1)S(1)} collective-permute-done((bf16[32,3968]{1,0:T(8,128)(2,1)S(1)}, bf16[32,3968]{1,0:T(8,128)(2,1)S(1)}, u32[]{:S(2)}, u32[]{:S(2)}) %collective-permute-start.2) | collective-permute-done | bytes 253984 | tf_op jit(solution)/shard_map/ppermute | solution.py:430
  16.3 2.1 %collective-permute-start.3 = (bf16[32,3968]{1,0:T(8,128)(2,1)S(1)}, bf16[32,3968]{1,0:T(8,128)(2,1)S(1)}, u32[]{:S(2)}, u32[]{:S(2)}) collective-permute-start(bf16[32,3968]{1,0:T(8,128)(2,1)S(1)} %collective-permute-done.2.refs_0_), channel_id=1, source_target_pairs={{0,4},{4,8},{8,12},{12,14},{14,10},{10,6},{6,2},{2,0},{1,3},{5,1},... | collective-permute-start | bytes 761864 | tf_op jit(solution)/shard_map/ppermute | solution.py:430
  18.4 1.6 %unpack_down.1 = (bf16[1920,1024]{1,0:T(8,128)(2,1)S(1)}, f32[8,1920]{1,0:T(8,128)S(1)}) custom-call(bf16[3840,512]{1,0:T(8,128)(2,1)S(1)} %unpack_up.1.first.refs_5_.refs_7_.refs_3_, f32[320,1024]{1,0:T(8,128)S(1)} %get-tuple-element.57.refs_0_, f32[1,1920]{1,0:T(1,128)S(1)} %copy-done.4, bf16[384,384]{1,0:T(8,128)(2,1)S(1)} %copy-done.5), custom_call_target="tpu_custom_call" | custom-call | flops 10000000000 | tf_op jit(solution)/shard_map/unpack_down/pallas_call | solution.py:392
  20.1 0.5 collective-permute-start.13
  20.6 1.6 %collective-permute-start.7 = (bf16[32,3968]{1,0:T(8,128)(2,1)S(1)}, bf16[32,3968]{1,0:T(8,128)(2,1)S(1)}, u32[]{:S(2)}, u32[]{:S(2)}) collective-permute-start(bf16[32,3968]{1,0:T(8,128)(2,1)S(1)} %collective-permute-done.6.refs_2_), channel_id=1, source_target_pairs={{0,4},{4,8},{8,12},{12,14},{14,10},{10,6},{6,2},{2,0},{1,3},{5,1},... | collective-permute-start | bytes 761864 | tf_op jit(solution)/shard_map/ppermute | solution.py:430
  22.1 0.4 collective-permute-done.3.refs_0_
  22.5 0.5 collective-permute-start.11
  23.1 2.2 %collective-permute-start.10 = (bf16[32,3968]{1,0:T(8,128)(2,1)S(1)}, bf16[32,3968]{1,0:T(8,128)(2,1)S(1)}, u32[]{:S(2)}, u32[]{:S(2)}) collective-permute-start(bf16[32,3968]{1,0:T(8,128)(2,1)S(1)} %collective-permute-done.3.refs_0_), channel_id=1, source_target_pairs={{0,4},{4,8},{8,12},{12,14},{14,10},{10,6},{6,2},{2,0},{1,3},{5,1},... | collective-permute-start | bytes 761864 | tf_op jit(solution)/shard_map/ppermute | solution.py:430
  25.2 1.6 %collective-permute-done.7.refs_2_ = bf16[32,3968]{1,0:T(8,128)(2,1)S(1)} collective-permute-done((bf16[32,3968]{1,0:T(8,128)(2,1)S(1)}, bf16[32,3968]{1,0:T(8,128)(2,1)S(1)}, u32[]{:S(2)}, u32[]{:S(2)}) %collective-permute-start.7) | collective-permute-done | bytes 253984 | tf_op jit(solution)/shard_map/ppermute | solution.py:430
  26.9 1.4 %hidden_part.6 = (bf16[128,512]{1,0:T(8,128)(2,1)S(1)}, f32[128,128]{1,0:T(8,128)S(1)}) custom-call(bf16[32,3968]{1,0:T(8,128)(2,1)S(1)} %collective-permute-done.2.refs_0_, bf16[32,3968]{1,0:T(8,128)(2,1)S(1)} %collective-permute-done.13.refs_1_, bf16[32,3968]{1,0:T(8,128)(2,1)S(1)} %collective-permute-done.6.refs_2_, ...), custom_call_target="tpu_custom_call" | custom-call | flops 10000000000 | tf_op jit(solution)/shard_map/hidden_part/pallas_call | solution.py:392
  28.3 1.9 %hidden_part.5 = (bf16[192,512]{1,0:T(8,128)(2,1)S(1)}, f32[192,128]{1,0:T(8,128)S(1)}) custom-call(bf16[32,3968]{1,0:T(8,128)(2,1)S(1)} %prep.2.first.refs_0_, bf16[32,3968]{1,0:T(8,128)(2,1)S(1)} %prep.3.first.refs_1_, bf16[32,3968]{1,0:T(8,128)(2,1)S(1)} %collective-permute-done.1.refs_2_, bf16[32,3968]{1,0:T(8,128)(2,1)S(1)} %collective-permute-done.11.refs_3_, ...), custom_call_target="tpu_custom_call" | custom-call | flops 10000000000 | tf_op jit(solution)/shard_map/hidden_part/pallas_call | solution.py:392
  30.2 0.6 collective-permute-start.15
  30.8 1.4 %hidden_part.4 = (bf16[128,512]{1,0:T(8,128)(2,1)S(1)}, f32[128,128]{1,0:T(8,128)S(1)}) custom-call(bf16[32,3968]{1,0:T(8,128)(2,1)S(1)} %collective-permute-done.3.refs_0_, bf16[32,3968]{1,0:T(8,128)(2,1)S(1)} %collective-permute-done.4.refs_1_, bf16[32,3968]{1,0:T(8,128)(2,1)S(1)} %collective-permute-done.7.refs_2_, ...), custom_call_target="tpu_custom_call" | custom-call | flops 1000000000 | tf_op jit(solution)/shard_map/hidden_part/pallas_call | solution.py:392
  32.3 1.4 %hidden_part.7 = (bf16[64,512]{1,0:T(8,128)(2,1)S(1)}, f32[64,128]{1,0:T(8,128)S(1)}) custom-call(bf16[32,3968]{1,0:T(8,128)(2,1)S(1)} %collective-permute-done.10.refs_0_, bf16[32,3968]{1,0:T(8,128)(2,1)S(1)} %collective-permute-done.15.refs_1_, bf16[3840,512]{1,0:T(8,128)(2,1)S(1)} %get-tuple-element.53.first.refs_4_.refs_6_.refs_2_, ...), custom_call_target="tpu_custom_call" | custom-call | flops 1000000000 | tf_op jit(solution)/shard_map/hidden_part/pallas_call | solution.py:392
  33.7 0.6 collective-permute-start.16
  34.2 1.4 %down_part.4 = (f32[64,1920]{1,0:T(8,128)S(1)}, f32[64,1920]{1,0:T(8,128)S(1)}) custom-call(bf16[128,512]{1,0:T(8,128)(2,1)S(1)} %get-tuple-element.60.mine, bf16[128,512]{1,0:T(8,128)(2,1)S(1)} %collective-permute-done.9.theirs, bf16[1920,1024]{1,0:T(8,128)(2,1)S(1)} %get-tuple-element.61.levels.refs_2_, f32[8,1920]{1,0:T(8,128)S(1)} %get-tuple-element.58.down_row.refs_3_, ...), custom_call_target="tpu_custom_call" | custom-call | flops 503316480 | tf_op jit(solution)/shard_map/down_part/pallas_call | solution.py:392
  35.6 1.3 %down_part.5 = f32[64,1920]{1,0:T(8,128)S(1)} custom-call(f32[64,1920]{1,0:T(8,128)S(1)} %get-tuple-element.63.first, bf16[64,512]{1,0:T(8,128)(2,1)S(1)} %get-tuple-element.81.refs_0_, bf16[64,512]{1,0:T(8,128)(2,1)S(1)} %collective-permute-done.16.refs_1_, bf16[1920,1024]{1,0:T(8,128)(2,1)S(1)} %get-tuple-element.61.levels.refs_2_, ...), custom_call_target="tpu_custom_call" | custom-call | flops 251658240 | tf_op jit(solution)/shard_map/down_part/pallas_call | solution.py:392
  37.0 1.0 %collective-permute-start.17 = (bf16[32,1920]{1,0:T(8,128)(2,1)S(1)}, bf16[32,1920]{1,0:T(8,128)(2,1)S(1)}, u32[]{:S(2)}, u32[]{:S(2)}) collective-permute-start(bf16[32,1920]{1,0:T(8,128)(2,1)S(1)} %get-tuple-element.94), channel_id=1, source_target_pairs={{0,2},{1,3},{4,0},{5,1},{8,4},{9,5},{12,8},{13,9},{14,12},{15,13},... | collective-permute-start | bytes 368648 | tf_op jit(solution)/shard_map/ppermute | solution.py:434
  38.0 0.5 collective-permute-start.18
  38.5 1.2 %collective-permute-start.20 = (bf16[32,1920]{1,0:T(8,128)(2,1)S(1)}, bf16[32,1920]{1,0:T(8,128)(2,1)S(1)}, u32[]{:S(2)}, u32[]{:S(2)}) collective-permute-start(bf16[32,1920]{1,0:T(8,128)(2,1)S(1)} %get-tuple-element.93), channel_id=1, source_target_pairs={{0,4},{1,5},{4,8},{5,9},{8,12},{9,13},{12,14},{13,15},{14,10},{15,... | collective-permute-start | bytes 368648 | tf_op jit(solution)/shard_map/ppermute | solution.py:434
  39.7 2.6 %collective-permute-done.17.first = bf16[32,1920]{1,0:T(8,128)(2,1)S(1)} collective-permute-done((bf16[32,1920]{1,0:T(8,128)(2,1)S(1)}, bf16[32,1920]{1,0:T(8,128)(2,1)S(1)}, u32[]{:S(2)}, u32[]{:S(2)}) %collective-permute-start.17) | collective-permute-done | bytes 122912 | tf_op jit(solution)/shard_map/ppermute | solution.py:434
  42.4 1.2 %collective-permute-start.24 = (bf16[64,1920]{1,0:T(8,128)(2,1)S(1)}, bf16[64,1920]{1,0:T(8,128)(2,1)S(1)}, u32[]{:S(2)}, u32[]{:S(2)}) collective-permute-start(bf16[64,1920]{1,0:T(8,128)(2,1)S(1)} %pad_maximum_fusion.1), channel_id=1, source_target_pairs={{0,2},{1,3},{4,0},{5,1},{8,4},{9,5},{12,8},{13,9},{14,12},{15,13},... | collective-permute-start | bytes 737288 | tf_op jit(solution)/shard_map/ppermute | solution.py:434
  43.5 0.3 collective-permute-done.20
  43.9 1.3 %collective-permute-start.21 = (bf16[64,1920]{1,0:T(8,128)(2,1)S(1)}, bf16[64,1920]{1,0:T(8,128)(2,1)S(1)}, u32[]{:S(2)}, u32[]{:S(2)}) collective-permute-start(bf16[64,1920]{1,0:T(8,128)(2,1)S(1)} %pad_maximum_fusion), channel_id=1, source_target_pairs={{0,4},{1,5},{4,8},{5,9},{8,12},{9,13},{12,14},{13,15},{14,10},{15,... | collective-permute-start | bytes 737288 | tf_op jit(solution)/shard_map/ppermute | solution.py:434
  45.2 1.4 %down_part.7 = (f32[64,1920]{1,0:T(8,128)S(1)}, f32[64,1920]{1,0:T(8,128)S(1)}) custom-call(bf16[32,1920]{1,0:T(8,128)(2,1)S(1)} %collective-permute-done.17.first, bf16[128,512]{1,0:T(8,128)(2,1)S(1)} %get-tuple-element.86.refs_0_, bf16[128,512]{1,0:T(8,128)(2,1)S(1)} %collective-permute-done.19.refs_1_, ...), custom_call_target="tpu_custom_call" | custom-call | flops 503316480 | tf_op jit(solution)/shard_map/down_part/pallas_call | solution.py:392
  46.6 1.4 %down_part.6 = (f32[64,1920]{1,0:T(8,128)S(1)}, f32[64,1920]{1,0:T(8,128)S(1)}, f32[64,1920]{1,0:T(8,128)S(1)}) custom-call(bf16[32,1920]{1,0:T(8,128)(2,1)S(1)} %collective-permute-done.17.first, bf16[192,512]{1,0:T(8,128)(2,1)S(1)} %get-tuple-element.83.refs_0_, bf16[192,512]{1,0:T(8,128)(2,1)S(1)} %collective-permute-done.18.refs_1_, ...), custom_call_target="tpu_custom_call" | custom-call | flops 754974720 | tf_op jit(solution)/shard_map/down_part/pallas_call | solution.py:392
  48.0 1.4 %collective-permute-done.24 = bf16[64,1920]{1,0:T(8,128)(2,1)S(1)} collective-permute-done((bf16[64,1920]{1,0:T(8,128)(2,1)S(1)}, bf16[64,1920]{1,0:T(8,128)(2,1)S(1)}, u32[]{:S(2)}, u32[]{:S(2)}) %collective-permute-start.24) | collective-permute-done | bytes 245792 | tf_op jit(solution)/shard_map/ppermute | solution.py:434
  49.5 1.4 %collective-permute-start.25 = (bf16[64,1920]{1,0:T(8,128)(2,1)S(1)}, bf16[64,1920]{1,0:T(8,128)(2,1)S(1)}, u32[]{:S(2)}, u32[]{:S(2)}) collective-permute-start(bf16[64,1920]{1,0:T(8,128)(2,1)S(1)} %add_convert_fusion.1), channel_id=1, source_target_pairs={{0,2},{1,3},{4,0},{5,1},{8,4},{9,5},{12,8},{13,9},{14,12},{15,13},... | collective-permute-start | bytes 737288 | tf_op jit(solution)/shard_map/ppermute | solution.py:434
  50.9 0.2 collective-permute-done.21
  51.2 1.2 %collective-permute-start.22 = (bf16[64,1920]{1,0:T(8,128)(2,1)S(1)}, bf16[64,1920]{1,0:T(8,128)(2,1)S(1)}, u32[]{:S(2)}, u32[]{:S(2)}) collective-permute-start(bf16[64,1920]{1,0:T(8,128)(2,1)S(1)} %add_convert_fusion.3), channel_id=1, source_target_pairs={{0,4},{1,5},{4,8},{5,9},{8,12},{9,13},{12,14},{13,15},{14,10},{15,... | collective-permute-start | bytes 737288 | tf_op jit(solution)/shard_map/ppermute | solution.py:434
  52.3 3.5 %collective-permute-done.25 = bf16[64,1920]{1,0:T(8,128)(2,1)S(1)} collective-permute-done((bf16[64,1920]{1,0:T(8,128)(2,1)S(1)}, bf16[64,1920]{1,0:T(8,128)(2,1)S(1)}, u32[]{:S(2)}, u32[]{:S(2)}) %collective-permute-start.25) | collective-permute-done | bytes 245792 | tf_op jit(solution)/shard_map/ppermute | solution.py:434
  55.9 1.4 %collective-permute-start.26 = (bf16[64,1920]{1,0:T(8,128)(2,1)S(1)}, bf16[64,1920]{1,0:T(8,128)(2,1)S(1)}, u32[]{:S(2)}, u32[]{:S(2)}) collective-permute-start(bf16[64,1920]{1,0:T(8,128)(2,1)S(1)} %add_convert_fusion), channel_id=1, source_target_pairs={{0,2},{1,3},{4,0},{5,1},{8,4},{9,5},{12,8},{13,9},{14,12},{15,13},... | collective-permute-start | bytes 737288 | tf_op jit(solution)/shard_map/ppermute | solution.py:434
  57.5 1.2 %collective-permute-start.23 = (bf16[64,1920]{1,0:T(8,128)(2,1)S(1)}, bf16[64,1920]{1,0:T(8,128)(2,1)S(1)}, u32[]{:S(2)}, u32[]{:S(2)}) collective-permute-start(bf16[64,1920]{1,0:T(8,128)(2,1)S(1)} %add_convert_fusion.2), channel_id=1, source_target_pairs={{0,4},{1,5},{4,8},{5,9},{8,12},{9,13},{12,14},{13,15},{14,10},{15,... | collective-permute-start | bytes 737288 | tf_op jit(solution)/shard_map/ppermute | solution.py:434
  58.6 3.5 %collective-permute-done.26.behind = bf16[64,1920]{1,0:T(8,128)(2,1)S(1)} collective-permute-done((bf16[64,1920]{1,0:T(8,128)(2,1)S(1)}, bf16[64,1920]{1,0:T(8,128)(2,1)S(1)}, u32[]{:S(2)}, u32[]{:S(2)}) %collective-permute-start.26) | collective-permute-done | bytes 245792 | tf_op jit(solution)/shard_map/ppermute | solution.py:434
  62.2 1.5 %collective-permute-done.23.ahead = bf16[64,1920]{1,0:T(8,128)(2,1)S(1)} collective-permute-done((bf16[64,1920]{1,0:T(8,128)(2,1)S(1)}, bf16[64,1920]{1,0:T(8,128)(2,1)S(1)}, u32[]{:S(2)}, u32[]{:S(2)}) %collective-permute-start.23) | collective-permute-done | bytes 245792 | tf_op jit(solution)/shard_map/ppermute | solution.py:434
  63.7 0.3 close.1
  64.2 1.3 %collective-permute-done.27 = bf16[32,1920]{1,0:T(8,128)(2,1)S(1)} collective-permute-done((bf16[32,1920]{1,0:T(8,128)(2,1)S(1)}, bf16[32,1920]{1,0:T(8,128)(2,1)S(1)}, u32[]{:S(2)}, u32[]{:S(2)}) %collective-permute-start.27) | collective-permute-done | bytes 122912 | tf_op jit(solution)/shard_map/ppermute | solution.py:437
  65.6 0.7 %pad_maximum_fusion.2 = bf16[32,3840]{1,0:T(8,128)(2,1)} fusion(bf16[32,1920]{1,0:T(8,128)(2,1)S(1)} %get-tuple-element.92, bf16[32,1920]{1,0:T(8,128)(2,1)S(1)} %get-tuple-element.91), kind=kLoop, calls=%fused_computation.8 | loop fusion | flops 491520 | bytes 491520 | tf_op jit(solution)/shard_map/concatenate | solution.py:633
  (50 shorter events, 1.0 us)
Async XLA Ops:
  0.0 2.3 %collective-permute-start = (bf16[64,3840]{1,0:T(8,128)(2,1)}, bf16[64,3840]{1,0:T(8,128)(2,1)S(1)}, u32[]{:S(2)}, u32[]{:S(2)}) collective-permute-start(bf16[64,3840]{1,0:T(8,128)(2,1)} %bitcast.7), channel_id=1, source_target_pairs={{0,1},{1,0},{2,3},{3,2},{4,5},{5,4},{6,7},{7,6},{8,9},{9,8},{10,11... | collective-permute-start | bytes 1474568 | tf_op jit(solution)/shard_map/ppermute | solution.py:437
  2.9 7.0 %collective-permute-start.1 = (bf16[32,3968]{1,0:T(8,128)(2,1)S(1)}, bf16[32,3968]{1,0:T(8,128)(2,1)S(1)}, u32[]{:S(2)}, u32[]{:S(2)}) collective-permute-start(bf16[32,3968]{1,0:T(8,128)(2,1)S(1)} %prep.2.first.refs_0_), channel_id=1, source_target_pairs={{0,4},{4,8},{8,12},{12,14},{14,10},{10,6},{6,2},{2,0},{1,3},{5,1},... | collective-permute-start | bytes 761864 | tf_op jit(solution)/shard_map/ppermute | solution.py:430
  6.4 7.0 %collective-permute-start.5 = (bf16[32,3968]{1,0:T(8,128)(2,1)S(1)}, bf16[32,3968]{1,0:T(8,128)(2,1)S(1)}, u32[]{:S(2)}, u32[]{:S(2)}) collective-permute-start(bf16[32,3968]{1,0:T(8,128)(2,1)S(1)} %prep.3.first.refs_1_), channel_id=1, source_target_pairs={{0,4},{4,8},{8,12},{12,14},{14,10},{10,6},{6,2},{2,0},{1,3},{5,1},... | collective-permute-start | bytes 761864 | tf_op jit(solution)/shard_map/ppermute | solution.py:430
  10.0 6.3 %collective-permute-start.2 = (bf16[32,3968]{1,0:T(8,128)(2,1)S(1)}, bf16[32,3968]{1,0:T(8,128)(2,1)S(1)}, u32[]{:S(2)}, u32[]{:S(2)}) collective-permute-start(bf16[32,3968]{1,0:T(8,128)(2,1)S(1)} %collective-permute-done.1.refs_2_), channel_id=1, source_target_pairs={{0,4},{4,8},{8,12},{12,14},{14,10},{10,6},{6,2},{2,0},{1,3},{5,1},... | collective-permute-start | bytes 761864 | tf_op jit(solution)/shard_map/ppermute | solution.py:430
  12.1 6.3 %copy-start.4 = (f32[1,1920]{1,0:T(1,128)S(1)}, f32[1,1920]{1,0:T(1,128)}, u32[]{:S(2)}) copy-start(f32[1,1920]{1,0:T(1,128)} %refs_1_.1) | copy-start | bytes 23044
  12.1 6.3 %copy-start.5 = (bf16[384,384]{1,0:T(8,128)(2,1)S(1)}, bf16[384,384]{1,0:T(8,128)(2,1)}, u32[]{:S(2)}) copy-start(bf16[384,384]{1,0:T(8,128)(2,1)} %constant.22.clone.refs_2_) | copy-start | bytes 884740
  13.5 6.5 %collective-permute-start.6 = (bf16[32,3968]{1,0:T(8,128)(2,1)S(1)}, bf16[32,3968]{1,0:T(8,128)(2,1)S(1)}, u32[]{:S(2)}, u32[]{:S(2)}) collective-permute-start(bf16[32,3968]{1,0:T(8,128)(2,1)S(1)} %collective-permute-done.5.refs_4_), channel_id=1, source_target_pairs={{0,4},{4,8},{8,12},{12,14},{14,10},{10,6},{6,2},{2,0},{1,3},{5,1},... | collective-permute-start | bytes 761864 | tf_op jit(solution)/shard_map/ppermute | solution.py:430
  16.3 6.3 %collective-permute-start.3 = (bf16[32,3968]{1,0:T(8,128)(2,1)S(1)}, bf16[32,3968]{1,0:T(8,128)(2,1)S(1)}, u32[]{:S(2)}, u32[]{:S(2)}) collective-permute-start(bf16[32,3968]{1,0:T(8,128)(2,1)S(1)} %collective-permute-done.2.refs_0_), channel_id=1, source_target_pairs={{0,4},{4,8},{8,12},{12,14},{14,10},{10,6},{6,2},{2,0},{1,3},{5,1},... | collective-permute-start | bytes 761864 | tf_op jit(solution)/shard_map/ppermute | solution.py:430
  18.4 8.5 %copy-start = (bf16[256,256]{1,0:T(8,128)(2,1)S(1)}, bf16[256,256]{1,0:T(8,128)(2,1)}, u32[]{:S(2)}) copy-start(bf16[256,256]{1,0:T(8,128)(2,1)} %constant.21.clone.refs_8_.refs_10_.refs_6_) | copy-start | bytes 393220
  18.4 8.5 %copy-start.2 = (f32[1,512]{1,0:T(1,128)S(1)}, f32[1,512]{1,0:T(1,128)}, u32[]{:S(2)}) copy-start(f32[1,512]{1,0:T(1,128)} %refs_4_.1) | copy-start | bytes 6148
  18.4 8.5 %copy-start.3 = (f32[1,512]{1,0:T(1,128)S(1)}, f32[1,512]{1,0:T(1,128)}, u32[]{:S(2)}) copy-start(f32[1,512]{1,0:T(1,128)} %refs_5_.1) | copy-start | bytes 6148
  20.0 3.1 %collective-permute-start.14 = (bf16[32,3968]{1,0:T(8,128)(2,1)S(1)}, bf16[32,3968]{1,0:T(8,128)(2,1)S(1)}, u32[]{:S(2)}, u32[]{:S(2)}) collective-permute-start(bf16[32,3968]{1,0:T(8,128)(2,1)S(1)} %collective-permute-done.6.refs_2_), channel_id=1, source_target_pairs={{0,1},{1,0},{2,3},{3,2},{4,5},{5,4},{6,7},{7,6},{8,9},{9,8},{10,11... | collective-permute-start | bytes 761864 | tf_op jit(solution)/shard_map/ppermute | solution.py:437
  20.1 3.0 %collective-permute-start.13 = (bf16[32,3968]{1,0:T(8,128)(2,1)S(1)}, bf16[32,3968]{1,0:T(8,128)(2,1)S(1)}, u32[]{:S(2)}, u32[]{:S(2)}) collective-permute-start(bf16[32,3968]{1,0:T(8,128)(2,1)S(1)} %collective-permute-done.2.refs_0_), channel_id=1, source_target_pairs={{0,1},{1,0},{2,3},{3,2},{4,5},{5,4},{6,7},{7,6},{8,9},{9,8},{10,11... | collective-permute-start | bytes 761864 | tf_op jit(solution)/shard_map/ppermute | solution.py:437
  20.6 6.3 %collective-permute-start.7 = (bf16[32,3968]{1,0:T(8,128)(2,1)S(1)}, bf16[32,3968]{1,0:T(8,128)(2,1)S(1)}, u32[]{:S(2)}, u32[]{:S(2)}) collective-permute-start(bf16[32,3968]{1,0:T(8,128)(2,1)S(1)} %collective-permute-done.6.refs_2_), channel_id=1, source_target_pairs={{0,4},{4,8},{8,12},{12,14},{14,10},{10,6},{6,2},{2,0},{1,3},{5,1},... | collective-permute-start | bytes 761864 | tf_op jit(solution)/shard_map/ppermute | solution.py:430
  22.5 4.3 %collective-permute-start.4 = (bf16[32,3968]{1,0:T(8,128)(2,1)S(1)}, bf16[32,3968]{1,0:T(8,128)(2,1)S(1)}, u32[]{:S(2)}, u32[]{:S(2)}) collective-permute-start(bf16[32,3968]{1,0:T(8,128)(2,1)S(1)} %collective-permute-done.3.refs_0_), channel_id=1, source_target_pairs={{0,1},{1,0},{2,3},{3,2},{4,5},{5,4},{6,7},{7,6},{8,9},{9,8},{10,11... | collective-permute-start | bytes 761864 | tf_op jit(solution)/shard_map/ppermute | solution.py:437
  22.5 4.3 %collective-permute-start.11 = (bf16[32,3968]{1,0:T(8,128)(2,1)S(1)}, bf16[32,3968]{1,0:T(8,128)(2,1)S(1)}, u32[]{:S(2)}, u32[]{:S(2)}) collective-permute-start(bf16[32,3968]{1,0:T(8,128)(2,1)S(1)} %collective-permute-done.1.refs_2_), channel_id=1, source_target_pairs={{0,1},{1,0},{2,3},{3,2},{4,5},{5,4},{6,7},{7,6},{8,9},{9,8},{10,11... | collective-permute-start | bytes 761864 | tf_op jit(solution)/shard_map/ppermute | solution.py:437
  23.1 3.8 %collective-permute-start.12 = (bf16[32,3968]{1,0:T(8,128)(2,1)S(1)}, bf16[32,3968]{1,0:T(8,128)(2,1)S(1)}, u32[]{:S(2)}, u32[]{:S(2)}) collective-permute-start(bf16[32,3968]{1,0:T(8,128)(2,1)S(1)} %collective-permute-done.5.refs_4_), channel_id=1, source_target_pairs={{0,1},{1,0},{2,3},{3,2},{4,5},{5,4},{6,7},{7,6},{8,9},{9,8},{10,11... | collective-permute-start | bytes 761864 | tf_op jit(solution)/shard_map/ppermute | solution.py:437
  23.1 7.1 %collective-permute-start.10 = (bf16[32,3968]{1,0:T(8,128)(2,1)S(1)}, bf16[32,3968]{1,0:T(8,128)(2,1)S(1)}, u32[]{:S(2)}, u32[]{:S(2)}) collective-permute-start(bf16[32,3968]{1,0:T(8,128)(2,1)S(1)} %collective-permute-done.3.refs_0_), channel_id=1, source_target_pairs={{0,4},{4,8},{8,12},{12,14},{14,10},{10,6},{6,2},{2,0},{1,3},{5,1},... | collective-permute-start | bytes 761864 | tf_op jit(solution)/shard_map/ppermute | solution.py:430
  26.9 3.9 %collective-permute-start.8 = (bf16[32,3968]{1,0:T(8,128)(2,1)S(1)}, bf16[32,3968]{1,0:T(8,128)(2,1)S(1)}, u32[]{:S(2)}, u32[]{:S(2)}) collective-permute-start(bf16[32,3968]{1,0:T(8,128)(2,1)S(1)} %collective-permute-done.7.refs_2_), channel_id=1, source_target_pairs={{0,1},{1,0},{2,3},{3,2},{4,5},{5,4},{6,7},{7,6},{8,9},{9,8},{10,11... | collective-permute-start | bytes 761864 | tf_op jit(solution)/shard_map/ppermute | solution.py:437
  30.2 2.1 %collective-permute-start.15 = (bf16[32,3968]{1,0:T(8,128)(2,1)S(1)}, bf16[32,3968]{1,0:T(8,128)(2,1)S(1)}, u32[]{:S(2)}, u32[]{:S(2)}) collective-permute-start(bf16[32,3968]{1,0:T(8,128)(2,1)S(1)} %collective-permute-done.10.refs_0_), channel_id=1, source_target_pairs={{0,1},{1,0},{2,3},{3,2},{4,5},{5,4},{6,7},{7,6},{8,9},{9,8},{10,11... | collective-permute-start | bytes 761864 | tf_op jit(solution)/shard_map/ppermute | solution.py:437
  32.2 2.0 %collective-permute-start.9 = (bf16[128,512]{1,0:T(8,128)(2,1)S(1)}, bf16[128,512]{1,0:T(8,128)(2,1)S(1)}, u32[]{:S(2)}, u32[]{:S(2)}) collective-permute-start(bf16[128,512]{1,0:T(8,128)(2,1)S(1)} %get-tuple-element.60.mine), channel_id=1, source_target_pairs={{0,1},{1,0},{2,3},{3,2},{4,5},{5,4},{6,7},{7,6},{8,9},{9,8},{10,11... | collective-permute-start | bytes 393224 | tf_op jit(solution)/shard_map/ppermute | solution.py:437
  33.7 1.9 %collective-permute-start.16 = (bf16[64,512]{1,0:T(8,128)(2,1)S(1)}, bf16[64,512]{1,0:T(8,128)(2,1)S(1)}, u32[]{:S(2)}, u32[]{:S(2)}) collective-permute-start(bf16[64,512]{1,0:T(8,128)(2,1)S(1)} %get-tuple-element.81.refs_0_), channel_id=1, source_target_pairs={{0,1},{1,0},{2,3},{3,2},{4,5},{5,4},{6,7},{7,6},{8,9},{9,8},{10,11... | collective-permute-start | bytes 196616 | tf_op jit(solution)/shard_map/ppermute | solution.py:437
  37.0 5.3 %collective-permute-start.17 = (bf16[32,1920]{1,0:T(8,128)(2,1)S(1)}, bf16[32,1920]{1,0:T(8,128)(2,1)S(1)}, u32[]{:S(2)}, u32[]{:S(2)}) collective-permute-start(bf16[32,1920]{1,0:T(8,128)(2,1)S(1)} %get-tuple-element.94), channel_id=1, source_target_pairs={{0,2},{1,3},{4,0},{5,1},{8,4},{9,5},{12,8},{13,9},{14,12},{15,13},... | collective-permute-start | bytes 368648 | tf_op jit(solution)/shard_map/ppermute | solution.py:434
  38.0 7.2 %collective-permute-start.19 = (bf16[128,512]{1,0:T(8,128)(2,1)S(1)}, bf16[128,512]{1,0:T(8,128)(2,1)S(1)}, u32[]{:S(2)}, u32[]{:S(2)}) collective-permute-start(bf16[128,512]{1,0:T(8,128)(2,1)S(1)} %get-tuple-element.86.refs_0_), channel_id=1, source_target_pairs={{0,1},{1,0},{2,3},{3,2},{4,5},{5,4},{6,7},{7,6},{8,9},{9,8},{10,11... | collective-permute-start | bytes 393224 | tf_op jit(solution)/shard_map/ppermute | solution.py:437
  38.0 8.6 %collective-permute-start.18 = (bf16[192,512]{1,0:T(8,128)(2,1)S(1)}, bf16[192,512]{1,0:T(8,128)(2,1)S(1)}, u32[]{:S(2)}, u32[]{:S(2)}) collective-permute-start(bf16[192,512]{1,0:T(8,128)(2,1)S(1)} %get-tuple-element.83.refs_0_), channel_id=1, source_target_pairs={{0,1},{1,0},{2,3},{3,2},{4,5},{5,4},{6,7},{7,6},{8,9},{9,8},{10,11... | collective-permute-start | bytes 589832 | tf_op jit(solution)/shard_map/ppermute | solution.py:437
  38.5 5.3 %collective-permute-start.20 = (bf16[32,1920]{1,0:T(8,128)(2,1)S(1)}, bf16[32,1920]{1,0:T(8,128)(2,1)S(1)}, u32[]{:S(2)}, u32[]{:S(2)}) collective-permute-start(bf16[32,1920]{1,0:T(8,128)(2,1)S(1)} %get-tuple-element.93), channel_id=1, source_target_pairs={{0,4},{1,5},{4,8},{5,9},{8,12},{9,13},{12,14},{13,15},{14,10},{15,... | collective-permute-start | bytes 368648 | tf_op jit(solution)/shard_map/ppermute | solution.py:434
  42.4 7.1 %collective-permute-start.24 = (bf16[64,1920]{1,0:T(8,128)(2,1)S(1)}, bf16[64,1920]{1,0:T(8,128)(2,1)S(1)}, u32[]{:S(2)}, u32[]{:S(2)}) collective-permute-start(bf16[64,1920]{1,0:T(8,128)(2,1)S(1)} %pad_maximum_fusion.1), channel_id=1, source_target_pairs={{0,2},{1,3},{4,0},{5,1},{8,4},{9,5},{12,8},{13,9},{14,12},{15,13},... | collective-permute-start | bytes 737288 | tf_op jit(solution)/shard_map/ppermute | solution.py:434
  43.9 7.2 %collective-permute-start.21 = (bf16[64,1920]{1,0:T(8,128)(2,1)S(1)}, bf16[64,1920]{1,0:T(8,128)(2,1)S(1)}, u32[]{:S(2)}, u32[]{:S(2)}) collective-permute-start(bf16[64,1920]{1,0:T(8,128)(2,1)S(1)} %pad_maximum_fusion), channel_id=1, source_target_pairs={{0,4},{1,5},{4,8},{5,9},{8,12},{9,13},{12,14},{13,15},{14,10},{15,... | collective-permute-start | bytes 737288 | tf_op jit(solution)/shard_map/ppermute | solution.py:434
  49.5 6.4 %collective-permute-start.25 = (bf16[64,1920]{1,0:T(8,128)(2,1)S(1)}, bf16[64,1920]{1,0:T(8,128)(2,1)S(1)}, u32[]{:S(2)}, u32[]{:S(2)}) collective-permute-start(bf16[64,1920]{1,0:T(8,128)(2,1)S(1)} %add_convert_fusion.1), channel_id=1, source_target_pairs={{0,2},{1,3},{4,0},{5,1},{8,4},{9,5},{12,8},{13,9},{14,12},{15,13},... | collective-permute-start | bytes 737288 | tf_op jit(solution)/shard_map/ppermute | solution.py:434
  51.1 12.6 %copy-start.1 = (bf16[384,384]{1,0:T(8,128)(2,1)S(1)}, bf16[384,384]{1,0:T(8,128)(2,1)}, u32[]{:S(2)}) copy-start(bf16[384,384]{1,0:T(8,128)(2,1)} %constant.23.clone.order) | copy-start | bytes 884740
  51.2 6.2 %collective-permute-start.22 = (bf16[64,1920]{1,0:T(8,128)(2,1)S(1)}, bf16[64,1920]{1,0:T(8,128)(2,1)S(1)}, u32[]{:S(2)}, u32[]{:S(2)}) collective-permute-start(bf16[64,1920]{1,0:T(8,128)(2,1)S(1)} %add_convert_fusion.3), channel_id=1, source_target_pairs={{0,4},{1,5},{4,8},{5,9},{8,12},{9,13},{12,14},{13,15},{14,10},{15,... | collective-permute-start | bytes 737288 | tf_op jit(solution)/shard_map/ppermute | solution.py:434
  55.9 6.2 %collective-permute-start.26 = (bf16[64,1920]{1,0:T(8,128)(2,1)S(1)}, bf16[64,1920]{1,0:T(8,128)(2,1)S(1)}, u32[]{:S(2)}, u32[]{:S(2)}) collective-permute-start(bf16[64,1920]{1,0:T(8,128)(2,1)S(1)} %add_convert_fusion), channel_id=1, source_target_pairs={{0,2},{1,3},{4,0},{5,1},{8,4},{9,5},{12,8},{13,9},{14,12},{15,13},... | collective-permute-start | bytes 737288 | tf_op jit(solution)/shard_map/ppermute | solution.py:434
  57.5 6.2 %collective-permute-start.23 = (bf16[64,1920]{1,0:T(8,128)(2,1)S(1)}, bf16[64,1920]{1,0:T(8,128)(2,1)S(1)}, u32[]{:S(2)}, u32[]{:S(2)}) collective-permute-start(bf16[64,1920]{1,0:T(8,128)(2,1)S(1)} %add_convert_fusion.2), channel_id=1, source_target_pairs={{0,4},{1,5},{4,8},{5,9},{8,12},{9,13},{12,14},{13,15},{14,10},{15,... | collective-permute-start | bytes 737288 | tf_op jit(solution)/shard_map/ppermute | solution.py:434
  64.1 1.4 %collective-permute-start.27 = (bf16[32,1920]{1,0:T(8,128)(2,1)S(1)}, bf16[32,1920]{1,0:T(8,128)(2,1)S(1)}, u32[]{:S(2)}, u32[]{:S(2)}) collective-permute-start(bf16[32,1920]{1,0:T(8,128)(2,1)S(1)} %constant_dynamic-slice_fusion), channel_id=1, source_target_pairs={{0,1},{1,0},{2,3},{3,2},{4,5},{5,4},{6,7},{7,6},{8,9},{9,8},{10,11... | collective-permute-start | bytes 368648 | tf_op jit(solution)/shard_map/ppermute | solution.py:437
where the time goes:
time: 66.5 us; the launch traced here: 66.3 us
  starting transfers between devices  27.2 us (41%)
  Pallas kernels  19.6 us (29%)
  waiting for transfers between devices  17.9 us (27%)
  other arithmetic  1.13 us (2%)
    pallas_call x15, Pallas kernels, whole_call(): pl.pallas_call(body, in_specs=specs, out_specs=[vmem] * len(outs), out_sh...  19.6 us
    ppermute x7, starting transfers between devices, hop(): return lax.ppermute(values, ('ep', 'tp'), pairs)  14.1 us
    ppermute x8, waiting for transfers between devices, turn_hop(): return lax.ppermute(values, ('ep', 'tp'), pairs)  13.2 us
    ppermute x8, starting transfers between devices, turn_hop(): return lax.ppermute(values, ('ep', 'tp'), pairs)  9.79 us
    ppermute x7, waiting for transfers between devices, hop(): return lax.ppermute(values, ('ep', 'tp'), pairs)  3.38 us
    ppermute x13, starting transfers between devices, swap(): return lax.ppermute(values, 'tp', [(0, 1), (1, 0)])  3.33 us
    ppermute x13, waiting for transfers between devices, swap(): return lax.ppermute(values, 'tp', [(0, 1), (1, 0)])  1.35 us
  transfers between devices with their start and end apart: 28, of which 13 were waited for; matrix products, arithmetic and copies ran while one was open for 1% of the time, Pallas kernels for 26%

commit v1 on v0

--- a/solution.py
+++ b/solution.py
@@ -156,9 +156,8 @@
 
 UNIT = 64
 SPAN = 6 * UNIT
-ALONE = ((0, None, 1), (0, None, 0))
+APART = ((0, None, 1), (0, None, 0), (1, None, 1), (1, None, 0))
 ROUND = ((0, 0, 1), (0, 1, 0), (0, 0, 0), (0, 1, 1))
-NEAR = ALONE + tuple((slot + 1, place, half) for slot, place, half in ROUND)
 EXTRA = 128
 
 
@@ -569,22 +568,20 @@
     )
     lead.append(hop(lead[2]))
     follow.append(hop(follow[2]))
-    lead[3] = hold(lead[3], down_row)
-    lead.append(hop(lead[3]))
 
     def pieces(distance):
         ours = lead[distance], follow[distance]
         return [piece for own in ours for piece in (own, swap(own))]
 
-    lead[2], follow[2] = hold(lead[2], down_row), hold(follow[2], down_row)
-    lead.append(hop(lead[2]))
-    follow.append(hop(follow[2]))
+    near = expert_hidden(pieces(1), ROUND, 2, work=10**9)
+    lead[3] = hold(lead[3], near[1], down_row)
+    lead.append(hop(lead[3]))
     beside = pieces(3)
-    near = expert_hidden(hold([lead[0], follow[0]] + pieces(1), beside[1]), NEAR, 3, work=10**10)
     second = expert_hidden(hold(pieces(2), beside[1]), ROUND, 2, work=10**10)
     third = expert_hidden(beside, ROUND, 2, work=10**9)
-    lead[4] = hold(lead[4], near[1], second[1])
-    edge = expert_hidden(hold([lead[4], swap(lead[4])], third[1]), ALONE, 1, work=10**9)
+    lead[4] = hold(lead[4], second[1], third[1])
+    rows = [lead[4], swap(lead[4]), lead[0], follow[0]]
+    edge = expert_hidden(hold(rows, third[1]), APART, 2, work=10**9)
 
     far = ep_count // 2
 
@@ -593,11 +590,11 @@
 
     ahead, behind = {}, {}
     behind[3], ahead[3] = expert_out(third)
-    (edge,) = expert_out(edge, after=ahead[3])
+    edge, own = expert_out(edge, after=ahead[3])
     went_ahead = turn_hop(edge[:half].astype(jnp.bfloat16), 1)
     went_behind = turn_hop(edge[half:].astype(jnp.bfloat16), -1)
     behind[2], ahead[2] = expert_out(second, after=went_behind)
-    own, behind[1], ahead[1] = expert_out(near, after=went_behind)
+    behind[1], ahead[1] = expert_out(near, after=went_behind)
     for distance in range(far - 1, 0, -1):
         if distance == far - 1:
             send_ahead = jnp.concatenate(

time: 66.5 us -> 65.8 us (0.989)
  starting transfers between devices: 27.2 us -> 25.6 us
  waiting for transfers between devices: 17.9 us -> 19.2 us
    ppermute x13, waiting for transfers between devices: 1.35 us -> 2.42 us  [swap(): return lax.ppermute(values, 'tp', [(0, 1), (1, 0)])]
    ppermute x8, waiting for transfers between devices: 13.2 us -> 14 us  [turn_hop(): return lax.ppermute(values, ('ep', 'tp'), pairs)]
  transfers between devices with their start and end apart: 28 -> 28, of which waited for: 13 -> 15; matrix products, arithmetic and copies ran while one was open for 1% -> 0% of each run, Pallas kernels for 26% -> 26%
where the time goes in v1:
time: 65.8 us; the launch traced here: 65.6 us
  starting transfers between devices  25.6 us (39%)
  Pallas kernels  19.3 us (29%)
  waiting for transfers between devices  19.2 us (29%)
  other arithmetic  1.09 us (2%)
    pallas_call x15, Pallas kernels, whole_call(): pl.pallas_call(body, in_specs=specs, out_specs=[vmem] * len(outs), out_sh...  19.3 us
    ppermute x8, waiting for transfers between devices, turn_hop(): return lax.ppermute(values, ('ep', 'tp'), pairs)  14 us
    ppermute x7, starting transfers between devices, hop(): return lax.ppermute(values, ('ep', 'tp'), pairs)  13.5 us
    ppermute x8, starting transfers between devices, turn_hop(): return lax.ppermute(values, ('ep', 'tp'), pairs)  9.19 us
    ppermute x13, starting transfers between devices, swap(): return lax.ppermute(values, 'tp', [(0, 1), (1, 0)])  2.88 us
    ppermute x7, waiting for transfers between devices, hop(): return lax.ppermute(values, ('ep', 'tp'), pairs)  2.82 us
    ppermute x13, waiting for transfers between devices, swap(): return lax.ppermute(values, 'tp', [(0, 1), (1, 0)])  2.42 us
  transfers between devices with their start and end apart: 28, of which 15 were waited for; matrix products, arithmetic and copies ran while one was open for 0% of the time, Pallas kernels for 26%

profile of v1, /device:TPU:0, one launch (start us, length us, event | category | flops | bytes accessed | tf_op | source)
XLA Modules:
  0.0 65.6 jit_solution(9937283649593165739)
XLA Ops:
  0.0 0.5 collective-permute-start
  0.5 1.8 %first.1 = (f32[64,3840]{1,0:T(8,128)S(1)}, f32[3840]{0:T(1024)S(1)}, bf16[384,384]{1,0:T(8,128)(2,1)S(1)}, bf16[64,128]{1,0:T(8,128)(2,1)S(1)}, f32[640,512]{1,0:T(8,128)S(1)}) custom-call(bf16[64,3840]{1,0:T(8,128)(2,1)} %bitcast.8, bf16[64,3840]{1,0:T(8,128)(2,1)} %resid.1, f32[3840]{0:T(1024)} %gain.1, bf16[384,384]{1,0:T(8,128)(2,1)} %constant.20.clone.signs, ...), custom_call_target="tpu_custom_call" | custom-call | tf_op jit(solution)/shard_map/first/pallas_call | solution.py:391
  2.3 0.6 prep.2.first.refs_2_
  2.9 2.9 %collective-permute-start.1 = (bf16[32,3968]{1,0:T(8,128)(2,1)S(1)}, bf16[32,3968]{1,0:T(8,128)(2,1)S(1)}, u32[]{:S(2)}, u32[]{:S(2)}) collective-permute-start(bf16[32,3968]{1,0:T(8,128)(2,1)S(1)} %prep.2.first.refs_2_), channel_id=1, source_target_pairs={{0,4},{4,8},{8,12},{12,14},{14,10},{10,6},{6,2},{2,0},{1,3},{5,1},... | collective-permute-start | bytes 761864 | tf_op jit(solution)/shard_map/ppermute | solution.py:429
  5.8 0.6 prep.3.first.refs_3_
  6.4 1.6 %collective-permute-start.5 = (bf16[32,3968]{1,0:T(8,128)(2,1)S(1)}, bf16[32,3968]{1,0:T(8,128)(2,1)S(1)}, u32[]{:S(2)}, u32[]{:S(2)}) collective-permute-start(bf16[32,3968]{1,0:T(8,128)(2,1)S(1)} %prep.3.first.refs_3_), channel_id=1, source_target_pairs={{0,4},{4,8},{8,12},{12,14},{14,10},{10,6},{6,2},{2,0},{1,3},{5,1},... | collective-permute-start | bytes 761864 | tf_op jit(solution)/shard_map/ppermute | solution.py:429
  8.1 1.7 %unpack_gate.1 = (bf16[3840,512]{1,0:T(8,128)(2,1)S(1)}, f32[640,512]{1,0:T(8,128)S(1)}, f32[320,1024]{1,0:T(8,128)S(1)}) custom-call(bf16[32,3968]{1,0:T(8,128)(2,1)S(1)} %prep.3.first.refs_3_, f32[640,512]{1,0:T(8,128)} %bitcast.11, f32[320,1024]{1,0:T(8,128)} %bitcast.12, f32[640,512]{1,0:T(8,128)S(1)} %get-tuple-element.47.refs_2_), custom_call_target="tpu_custom_call" | custom-call | flops 10000000000 | tf_op jit(solution)/shard_map/unpack_gate/pallas_call | solution.py:391
  10.0 2.1 %collective-permute-start.2 = (bf16[32,3968]{1,0:T(8,128)(2,1)S(1)}, bf16[32,3968]{1,0:T(8,128)(2,1)S(1)}, u32[]{:S(2)}, u32[]{:S(2)}) collective-permute-start(bf16[32,3968]{1,0:T(8,128)(2,1)S(1)} %collective-permute-done.1.refs_0_), channel_id=1, source_target_pairs={{0,4},{4,8},{8,12},{12,14},{14,10},{10,6},{6,2},{2,0},{1,3},{5,1},... | collective-permute-start | bytes 761864 | tf_op jit(solution)/shard_map/ppermute | solution.py:429
  12.1 1.4 %unpack_up.1.refs_5_.first = bf16[3840,512]{1,0:T(8,128)(2,1)S(1)} custom-call(bf16[3840,512]{1,0:T(8,128)(2,1)S(1)} %get-tuple-element.48.first.refs_4_, f32[640,512]{1,0:T(8,128)S(1)} %get-tuple-element.50.refs_0_), custom_call_target="tpu_custom_call" | custom-call | flops 10000000000 | tf_op jit(solution)/shard_map/unpack_up/pallas_call | solution.py:391
  13.5 0.5 collective-permute-start.6
  14.0 1.6 %collective-permute-start.8 = (bf16[32,3968]{1,0:T(8,128)(2,1)S(1)}, bf16[32,3968]{1,0:T(8,128)(2,1)S(1)}, u32[]{:S(2)}, u32[]{:S(2)}) collective-permute-start(bf16[32,3968]{1,0:T(8,128)(2,1)S(1)} %collective-permute-done.5.refs_2_), channel_id=1, source_target_pairs={{0,4},{4,8},{8,12},{12,14},{14,10},{10,6},{6,2},{2,0},{1,3},{5,1},... | collective-permute-start | bytes 761864 | tf_op jit(solution)/shard_map/ppermute | solution.py:429
  15.6 0.6 collective-permute-done.2.refs_0_
  16.3 2.1 %collective-permute-start.3 = (bf16[32,3968]{1,0:T(8,128)(2,1)S(1)}, bf16[32,3968]{1,0:T(8,128)(2,1)S(1)}, u32[]{:S(2)}, u32[]{:S(2)}) collective-permute-start(bf16[32,3968]{1,0:T(8,128)(2,1)S(1)} %collective-permute-done.2.refs_0_), channel_id=1, source_target_pairs={{0,4},{4,8},{8,12},{12,14},{14,10},{10,6},{6,2},{2,0},{1,3},{5,1},... | collective-permute-start | bytes 761864 | tf_op jit(solution)/shard_map/ppermute | solution.py:429
  18.4 1.6 %unpack_down.1 = (bf16[1920,1024]{1,0:T(8,128)(2,1)S(1)}, f32[8,1920]{1,0:T(8,128)S(1)}) custom-call(bf16[3840,512]{1,0:T(8,128)(2,1)S(1)} %unpack_up.1.refs_5_.first, f32[320,1024]{1,0:T(8,128)S(1)} %get-tuple-element.53.refs_0_, f32[1,1920]{1,0:T(1,128)S(1)} %copy-done.4, bf16[384,384]{1,0:T(8,128)(2,1)S(1)} %copy-done.5), custom_call_target="tpu_custom_call" | custom-call | flops 10000000000 | tf_op jit(solution)/shard_map/unpack_down/pallas_call | solution.py:391
  20.1 0.2 collective-permute-done.8.refs_2_
  20.3 0.3 collective-permute-start.14
  20.6 1.6 %collective-permute-start.9 = (bf16[32,3968]{1,0:T(8,128)(2,1)S(1)}, bf16[32,3968]{1,0:T(8,128)(2,1)S(1)}, u32[]{:S(2)}, u32[]{:S(2)}) collective-permute-start(bf16[32,3968]{1,0:T(8,128)(2,1)S(1)} %collective-permute-done.8.refs_2_), channel_id=1, source_target_pairs={{0,4},{4,8},{8,12},{12,14},{14,10},{10,6},{6,2},{2,0},{1,3},{5,1},... | collective-permute-start | bytes 761864 | tf_op jit(solution)/shard_map/ppermute | solution.py:429
  22.2 1.4 %hidden_part.4 = (bf16[128,512]{1,0:T(8,128)(2,1)S(1)}, f32[128,128]{1,0:T(8,128)S(1)}) custom-call(bf16[32,3968]{1,0:T(8,128)(2,1)S(1)} %collective-permute-done.1.refs_0_, bf16[32,3968]{1,0:T(8,128)(2,1)S(1)} %collective-permute-done.4.refs_1_, bf16[32,3968]{1,0:T(8,128)(2,1)S(1)} %collective-permute-done.5.refs_2_, ...), custom_call_target="tpu_custom_call" | custom-call | flops 1000000000 | tf_op jit(solution)/shard_map/hidden_part/pallas_call | solution.py:391
  23.7 1.6 %collective-permute-start.12 = (bf16[32,3968]{1,0:T(8,128)(2,1)S(1)}, bf16[32,3968]{1,0:T(8,128)(2,1)S(1)}, u32[]{:S(2)}, u32[]{:S(2)}) collective-permute-start(bf16[32,3968]{1,0:T(8,128)(2,1)S(1)} %collective-permute-done.3.refs_0_), channel_id=1, source_target_pairs={{0,4},{4,8},{8,12},{12,14},{14,10},{10,6},{6,2},{2,0},{1,3},{5,1},... | collective-permute-start | bytes 761864 | tf_op jit(solution)/shard_map/ppermute | solution.py:429
  25.3 1.5 %collective-permute-done.9.refs_2_ = bf16[32,3968]{1,0:T(8,128)(2,1)S(1)} collective-permute-done((bf16[32,3968]{1,0:T(8,128)(2,1)S(1)}, bf16[32,3968]{1,0:T(8,128)(2,1)S(1)}, u32[]{:S(2)}, u32[]{:S(2)}) %collective-permute-start.9) | collective-permute-done | bytes 253984 | tf_op jit(solution)/shard_map/ppermute | solution.py:429
  26.9 1.4 %hidden_part.6 = (bf16[128,512]{1,0:T(8,128)(2,1)S(1)}, f32[128,128]{1,0:T(8,128)S(1)}) custom-call(bf16[32,3968]{1,0:T(8,128)(2,1)S(1)} %collective-permute-done.2.refs_0_, bf16[32,3968]{1,0:T(8,128)(2,1)S(1)} %collective-permute-done.13.refs_1_, bf16[32,3968]{1,0:T(8,128)(2,1)S(1)} %collective-permute-done.8.refs_2_, ...), custom_call_target="tpu_custom_call" | custom-call | flops 10000000000 | tf_op jit(solution)/shard_map/hidden_part/pallas_call | solution.py:391
  28.4 1.4 %hidden_part.5 = (bf16[128,512]{1,0:T(8,128)(2,1)S(1)}, f32[128,128]{1,0:T(8,128)S(1)}) custom-call(bf16[32,3968]{1,0:T(8,128)(2,1)S(1)} %collective-permute-done.3.refs_0_, bf16[32,3968]{1,0:T(8,128)(2,1)S(1)} %collective-permute-done.7.refs_1_, bf16[32,3968]{1,0:T(8,128)(2,1)S(1)} %collective-permute-done.9.refs_2_, ...), custom_call_target="tpu_custom_call" | custom-call | flops 1000000000 | tf_op jit(solution)/shard_map/hidden_part/pallas_call | solution.py:391
  29.8 0.2 collective-permute-done.12.refs_0_
  30.0 0.3 collective-permute-start.15
  30.6 1.0 %collective-permute-done.15.refs_1_ = bf16[32,3968]{1,0:T(8,128)(2,1)S(1)} collective-permute-done((bf16[32,3968]{1,0:T(8,128)(2,1)S(1)}, bf16[32,3968]{1,0:T(8,128)(2,1)S(1)}, u32[]{:S(2)}, u32[]{:S(2)}) %collective-permute-start.15) | collective-permute-done | bytes 253984 | tf_op jit(solution)/shard_map/ppermute | solution.py:436
  31.6 1.4 %hidden_part.7 = (bf16[128,512]{1,0:T(8,128)(2,1)S(1)}, f32[128,128]{1,0:T(8,128)S(1)}) custom-call(bf16[32,3968]{1,0:T(8,128)(2,1)S(1)} %collective-permute-done.12.refs_0_, bf16[32,3968]{1,0:T(8,128)(2,1)S(1)} %collective-permute-done.15.refs_1_, bf16[32,3968]{1,0:T(8,128)(2,1)S(1)} %prep.2.first.refs_2_, bf16[32,3968]{1,0:T(8,128)(2,1)S(1)} %prep.3.first.refs_3_, ...), custom_call_target="tpu_custom_call" | custom-call | flops 1000000000 | tf_op jit(solution)/shard_map/hidden_part/pallas_call | solution.py:391
  33.0 0.4 collective-permute-start.16
  33.4 1.4 %down_part.4 = (f32[64,1920]{1,0:T(8,128)S(1)}, f32[64,1920]{1,0:T(8,128)S(1)}) custom-call(bf16[128,512]{1,0:T(8,128)(2,1)S(1)} %get-tuple-element.56.mine, bf16[128,512]{1,0:T(8,128)(2,1)S(1)} %collective-permute-done.11.theirs, bf16[1920,1024]{1,0:T(8,128)(2,1)S(1)} %get-tuple-element.57.levels.refs_2_, f32[8,1920]{1,0:T(8,128)S(1)} %get-tuple-element.54.down_row.refs_3_, ...), custom_call_target="tpu_custom_call" | custom-call | flops 503316480 | tf_op jit(solution)/shard_map/down_part/pallas_call | solution.py:391
  34.8 1.4 %down_part.5 = (f32[64,1920]{1,0:T(8,128)S(1)}, f32[64,1920]{1,0:T(8,128)S(1)}) custom-call(f32[64,1920]{1,0:T(8,128)S(1)} %get-tuple-element.59.first, bf16[128,512]{1,0:T(8,128)(2,1)S(1)} %get-tuple-element.70.refs_0_, bf16[128,512]{1,0:T(8,128)(2,1)S(1)} %collective-permute-done.16.refs_1_, bf16[1920,1024]{1,0:T(8,128)(2,1)S(1)} %get-tuple-element.57.levels.refs_2_, ...), custom_call_target="tpu_custom_call" | custom-call | flops 503316480 | tf_op jit(solution)/shard_map/down_part/pallas_call | solution.py:391
  36.2 0.7 %collective-permute-start.17 = (bf16[32,1920]{1,0:T(8,128)(2,1)S(1)}, bf16[32,1920]{1,0:T(8,128)(2,1)S(1)}, u32[]{:S(2)}, u32[]{:S(2)}) collective-permute-start(bf16[32,1920]{1,0:T(8,128)(2,1)S(1)} %get-tuple-element.84), channel_id=1, source_target_pairs={{0,2},{1,3},{4,0},{5,1},{8,4},{9,5},{12,8},{13,9},{14,12},{15,13},... | collective-permute-start | bytes 368648 | tf_op jit(solution)/shard_map/ppermute | solution.py:433
  37.0 0.4 collective-permute-start.19
  37.4 1.4 %collective-permute-start.20 = (bf16[32,1920]{1,0:T(8,128)(2,1)S(1)}, bf16[32,1920]{1,0:T(8,128)(2,1)S(1)}, u32[]{:S(2)}, u32[]{:S(2)}) collective-permute-start(bf16[32,1920]{1,0:T(8,128)(2,1)S(1)} %get-tuple-element.83), channel_id=1, source_target_pairs={{0,4},{1,5},{4,8},{5,9},{8,12},{9,13},{12,14},{13,15},{14,10},{15,... | collective-permute-start | bytes 368648 | tf_op jit(solution)/shard_map/ppermute | solution.py:433
  38.9 2.8 %collective-permute-done.17.first = bf16[32,1920]{1,0:T(8,128)(2,1)S(1)} collective-permute-done((bf16[32,1920]{1,0:T(8,128)(2,1)S(1)}, bf16[32,1920]{1,0:T(8,128)(2,1)S(1)}, u32[]{:S(2)}, u32[]{:S(2)}) %collective-permute-start.17) | collective-permute-done | bytes 122912 | tf_op jit(solution)/shard_map/ppermute | solution.py:433
  41.7 0.9 %collective-permute-start.24 = (bf16[64,1920]{1,0:T(8,128)(2,1)S(1)}, bf16[64,1920]{1,0:T(8,128)(2,1)S(1)}, u32[]{:S(2)}, u32[]{:S(2)}) collective-permute-start(bf16[64,1920]{1,0:T(8,128)(2,1)S(1)} %pad_maximum_fusion.1), channel_id=1, source_target_pairs={{0,2},{1,3},{4,0},{5,1},{8,4},{9,5},{12,8},{13,9},{14,12},{15,13},... | collective-permute-start | bytes 737288 | tf_op jit(solution)/shard_map/ppermute | solution.py:433
  42.9 1.5 %collective-permute-start.21 = (bf16[64,1920]{1,0:T(8,128)(2,1)S(1)}, bf16[64,1920]{1,0:T(8,128)(2,1)S(1)}, u32[]{:S(2)}, u32[]{:S(2)}) collective-permute-start(bf16[64,1920]{1,0:T(8,128)(2,1)S(1)} %pad_maximum_fusion), channel_id=1, source_target_pairs={{0,4},{1,5},{4,8},{5,9},{8,12},{9,13},{12,14},{13,15},{14,10},{15,... | collective-permute-start | bytes 737288 | tf_op jit(solution)/shard_map/ppermute | solution.py:433
  44.4 1.4 %down_part.7 = (f32[64,1920]{1,0:T(8,128)S(1)}, f32[64,1920]{1,0:T(8,128)S(1)}) custom-call(bf16[32,1920]{1,0:T(8,128)(2,1)S(1)} %collective-permute-done.17.first, bf16[128,512]{1,0:T(8,128)(2,1)S(1)} %get-tuple-element.76.refs_0_, bf16[128,512]{1,0:T(8,128)(2,1)S(1)} %collective-permute-done.19.refs_1_, ...), custom_call_target="tpu_custom_call" | custom-call | flops 503316480 | tf_op jit(solution)/shard_map/down_part/pallas_call | solution.py:391
  45.8 1.4 %down_part.6 = (f32[64,1920]{1,0:T(8,128)S(1)}, f32[64,1920]{1,0:T(8,128)S(1)}) custom-call(bf16[32,1920]{1,0:T(8,128)(2,1)S(1)} %collective-permute-done.17.first, bf16[128,512]{1,0:T(8,128)(2,1)S(1)} %get-tuple-element.74.refs_0_, bf16[128,512]{1,0:T(8,128)(2,1)S(1)} %collective-permute-done.18.refs_1_, ...), custom_call_target="tpu_custom_call" | custom-call | flops 503316480 | tf_op jit(solution)/shard_map/down_part/pallas_call | solution.py:391
  47.2 1.8 %collective-permute-done.24 = bf16[64,1920]{1,0:T(8,128)(2,1)S(1)} collective-permute-done((bf16[64,1920]{1,0:T(8,128)(2,1)S(1)}, bf16[64,1920]{1,0:T(8,128)(2,1)S(1)}, u32[]{:S(2)}, u32[]{:S(2)}) %collective-permute-start.24) | collective-permute-done | bytes 245792 | tf_op jit(solution)/shard_map/ppermute | solution.py:433
  49.0 1.1 %collective-permute-start.25 = (bf16[64,1920]{1,0:T(8,128)(2,1)S(1)}, bf16[64,1920]{1,0:T(8,128)(2,1)S(1)}, u32[]{:S(2)}, u32[]{:S(2)}) collective-permute-start(bf16[64,1920]{1,0:T(8,128)(2,1)S(1)} %add_convert_fusion.1), channel_id=1, source_target_pairs={{0,2},{1,3},{4,0},{5,1},{8,4},{9,5},{12,8},{13,9},{14,12},{15,13},... | collective-permute-start | bytes 737288 | tf_op jit(solution)/shard_map/ppermute | solution.py:433
  50.2 1.3 %collective-permute-start.22 = (bf16[64,1920]{1,0:T(8,128)(2,1)S(1)}, bf16[64,1920]{1,0:T(8,128)(2,1)S(1)}, u32[]{:S(2)}, u32[]{:S(2)}) collective-permute-start(bf16[64,1920]{1,0:T(8,128)(2,1)S(1)} %add_convert_fusion.3), channel_id=1, source_target_pairs={{0,4},{1,5},{4,8},{5,9},{8,12},{9,13},{12,14},{13,15},{14,10},{15,... | collective-permute-start | bytes 737288 | tf_op jit(solution)/shard_map/ppermute | solution.py:433
  51.5 3.9 %collective-permute-done.25 = bf16[64,1920]{1,0:T(8,128)(2,1)S(1)} collective-permute-done((bf16[64,1920]{1,0:T(8,128)(2,1)S(1)}, bf16[64,1920]{1,0:T(8,128)(2,1)S(1)}, u32[]{:S(2)}, u32[]{:S(2)}) %collective-permute-start.25) | collective-permute-done | bytes 245792 | tf_op jit(solution)/shard_map/ppermute | solution.py:433
  55.4 1.3 %collective-permute-start.26 = (bf16[64,1920]{1,0:T(8,128)(2,1)S(1)}, bf16[64,1920]{1,0:T(8,128)(2,1)S(1)}, u32[]{:S(2)}, u32[]{:S(2)}) collective-permute-start(bf16[64,1920]{1,0:T(8,128)(2,1)S(1)} %add_convert_fusion), channel_id=1, source_target_pairs={{0,2},{1,3},{4,0},{5,1},{8,4},{9,5},{12,8},{13,9},{14,12},{15,13},... | collective-permute-start | bytes 737288 | tf_op jit(solution)/shard_map/ppermute | solution.py:433
  56.8 1.1 %collective-permute-start.23 = (bf16[64,1920]{1,0:T(8,128)(2,1)S(1)}, bf16[64,1920]{1,0:T(8,128)(2,1)S(1)}, u32[]{:S(2)}, u32[]{:S(2)}) collective-permute-start(bf16[64,1920]{1,0:T(8,128)(2,1)S(1)} %add_convert_fusion.2), channel_id=1, source_target_pairs={{0,4},{1,5},{4,8},{5,9},{8,12},{9,13},{12,14},{13,15},{14,10},{15,... | collective-permute-start | bytes 737288 | tf_op jit(solution)/shard_map/ppermute | solution.py:433
  57.8 3.9 %collective-permute-done.26.behind = bf16[64,1920]{1,0:T(8,128)(2,1)S(1)} collective-permute-done((bf16[64,1920]{1,0:T(8,128)(2,1)S(1)}, bf16[64,1920]{1,0:T(8,128)(2,1)S(1)}, u32[]{:S(2)}, u32[]{:S(2)}) %collective-permute-start.26) | collective-permute-done | bytes 245792 | tf_op jit(solution)/shard_map/ppermute | solution.py:433
  61.7 1.3 %collective-permute-done.23.ahead = bf16[64,1920]{1,0:T(8,128)(2,1)S(1)} collective-permute-done((bf16[64,1920]{1,0:T(8,128)(2,1)S(1)}, bf16[64,1920]{1,0:T(8,128)(2,1)S(1)}, u32[]{:S(2)}, u32[]{:S(2)}) %collective-permute-start.23) | collective-permute-done | bytes 245792 | tf_op jit(solution)/shard_map/ppermute | solution.py:433
  63.0 0.3 close.1
  63.5 1.3 %collective-permute-done.27 = bf16[32,1920]{1,0:T(8,128)(2,1)S(1)} collective-permute-done((bf16[32,1920]{1,0:T(8,128)(2,1)S(1)}, bf16[32,1920]{1,0:T(8,128)(2,1)S(1)}, u32[]{:S(2)}, u32[]{:S(2)}) %collective-permute-start.27) | collective-permute-done | bytes 122912 | tf_op jit(solution)/shard_map/ppermute | solution.py:436
  64.9 0.7 %pad_maximum_fusion.2 = bf16[32,3840]{1,0:T(8,128)(2,1)} fusion(bf16[32,1920]{1,0:T(8,128)(2,1)S(1)} %get-tuple-element.82, bf16[32,1920]{1,0:T(8,128)(2,1)S(1)} %get-tuple-element.81), kind=kLoop, calls=%fused_computation.8 | loop fusion | flops 491520 | bytes 491520 | tf_op jit(solution)/shard_map/concatenate | solution.py:630
  (50 shorter events, 1.6 us)
Async XLA Ops:
  0.0 2.3 %collective-permute-start = (bf16[64,3840]{1,0:T(8,128)(2,1)}, bf16[64,3840]{1,0:T(8,128)(2,1)S(1)}, u32[]{:S(2)}, u32[]{:S(2)}) collective-permute-start(bf16[64,3840]{1,0:T(8,128)(2,1)} %bitcast.7), channel_id=1, source_target_pairs={{0,1},{1,0},{2,3},{3,2},{4,5},{5,4},{6,7},{7,6},{8,9},{9,8},{10,11... | collective-permute-start | bytes 1474568 | tf_op jit(solution)/shard_map/ppermute | solution.py:436
  2.9 7.0 %collective-permute-start.1 = (bf16[32,3968]{1,0:T(8,128)(2,1)S(1)}, bf16[32,3968]{1,0:T(8,128)(2,1)S(1)}, u32[]{:S(2)}, u32[]{:S(2)}) collective-permute-start(bf16[32,3968]{1,0:T(8,128)(2,1)S(1)} %prep.2.first.refs_2_), channel_id=1, source_target_pairs={{0,4},{4,8},{8,12},{12,14},{14,10},{10,6},{6,2},{2,0},{1,3},{5,1},... | collective-permute-start | bytes 761864 | tf_op jit(solution)/shard_map/ppermute | solution.py:429
  6.4 7.1 %collective-permute-start.5 = (bf16[32,3968]{1,0:T(8,128)(2,1)S(1)}, bf16[32,3968]{1,0:T(8,128)(2,1)S(1)}, u32[]{:S(2)}, u32[]{:S(2)}) collective-permute-start(bf16[32,3968]{1,0:T(8,128)(2,1)S(1)} %prep.3.first.refs_3_), channel_id=1, source_target_pairs={{0,4},{4,8},{8,12},{12,14},{14,10},{10,6},{6,2},{2,0},{1,3},{5,1},... | collective-permute-start | bytes 761864 | tf_op jit(solution)/shard_map/ppermute | solution.py:429
  10.0 6.3 %collective-permute-start.2 = (bf16[32,3968]{1,0:T(8,128)(2,1)S(1)}, bf16[32,3968]{1,0:T(8,128)(2,1)S(1)}, u32[]{:S(2)}, u32[]{:S(2)}) collective-permute-start(bf16[32,3968]{1,0:T(8,128)(2,1)S(1)} %collective-permute-done.1.refs_0_), channel_id=1, source_target_pairs={{0,4},{4,8},{8,12},{12,14},{14,10},{10,6},{6,2},{2,0},{1,3},{5,1},... | collective-permute-start | bytes 761864 | tf_op jit(solution)/shard_map/ppermute | solution.py:429
  12.1 6.3 %copy-start.4 = (f32[1,1920]{1,0:T(1,128)S(1)}, f32[1,1920]{1,0:T(1,128)}, u32[]{:S(2)}) copy-start(f32[1,1920]{1,0:T(1,128)} %refs_1_.1) | copy-start | bytes 23044
  12.1 6.3 %copy-start.5 = (bf16[384,384]{1,0:T(8,128)(2,1)S(1)}, bf16[384,384]{1,0:T(8,128)(2,1)}, u32[]{:S(2)}) copy-start(bf16[384,384]{1,0:T(8,128)(2,1)} %constant.22.clone.refs_2_) | copy-start | bytes 884740
  13.4 7.1 %collective-permute-start.4 = (bf16[32,3968]{1,0:T(8,128)(2,1)S(1)}, bf16[32,3968]{1,0:T(8,128)(2,1)S(1)}, u32[]{:S(2)}, u32[]{:S(2)}) collective-permute-start(bf16[32,3968]{1,0:T(8,128)(2,1)S(1)} %collective-permute-done.1.refs_0_), channel_id=1, source_target_pairs={{0,1},{1,0},{2,3},{3,2},{4,5},{5,4},{6,7},{7,6},{8,9},{9,8},{10,11... | collective-permute-start | bytes 761864 | tf_op jit(solution)/shard_map/ppermute | solution.py:436
  13.5 8.6 %collective-permute-start.6 = (bf16[32,3968]{1,0:T(8,128)(2,1)S(1)}, bf16[32,3968]{1,0:T(8,128)(2,1)S(1)}, u32[]{:S(2)}, u32[]{:S(2)}) collective-permute-start(bf16[32,3968]{1,0:T(8,128)(2,1)S(1)} %collective-permute-done.5.refs_2_), channel_id=1, source_target_pairs={{0,1},{1,0},{2,3},{3,2},{4,5},{5,4},{6,7},{7,6},{8,9},{9,8},{10,11... | collective-permute-start | bytes 761864 | tf_op jit(solution)/shard_map/ppermute | solution.py:436
  14.0 6.3 %collective-permute-start.8 = (bf16[32,3968]{1,0:T(8,128)(2,1)S(1)}, bf16[32,3968]{1,0:T(8,128)(2,1)S(1)}, u32[]{:S(2)}, u32[]{:S(2)}) collective-permute-start(bf16[32,3968]{1,0:T(8,128)(2,1)S(1)} %collective-permute-done.5.refs_2_), channel_id=1, source_target_pairs={{0,4},{4,8},{8,12},{12,14},{14,10},{10,6},{6,2},{2,0},{1,3},{5,1},... | collective-permute-start | bytes 761864 | tf_op jit(solution)/shard_map/ppermute | solution.py:429
  16.3 7.4 %collective-permute-start.3 = (bf16[32,3968]{1,0:T(8,128)(2,1)S(1)}, bf16[32,3968]{1,0:T(8,128)(2,1)S(1)}, u32[]{:S(2)}, u32[]{:S(2)}) collective-permute-start(bf16[32,3968]{1,0:T(8,128)(2,1)S(1)} %collective-permute-done.2.refs_0_), channel_id=1, source_target_pairs={{0,4},{4,8},{8,12},{12,14},{14,10},{10,6},{6,2},{2,0},{1,3},{5,1},... | collective-permute-start | bytes 761864 | tf_op jit(solution)/shard_map/ppermute | solution.py:429
  18.4 3.8 %copy-start = (bf16[256,256]{1,0:T(8,128)(2,1)S(1)}, bf16[256,256]{1,0:T(8,128)(2,1)}, u32[]{:S(2)}) copy-start(bf16[256,256]{1,0:T(8,128)(2,1)} %constant.21.clone.refs_8_) | copy-start | bytes 393220
  18.4 3.8 %copy-start.2 = (f32[1,512]{1,0:T(1,128)S(1)}, f32[1,512]{1,0:T(1,128)}, u32[]{:S(2)}) copy-start(f32[1,512]{1,0:T(1,128)} %refs_6_.7) | copy-start | bytes 6148
  18.4 3.8 %copy-start.3 = (f32[1,512]{1,0:T(1,128)S(1)}, f32[1,512]{1,0:T(1,128)}, u32[]{:S(2)}) copy-start(f32[1,512]{1,0:T(1,128)} %refs_7_.7) | copy-start | bytes 6148
  20.0 6.9 %collective-permute-start.13 = (bf16[32,3968]{1,0:T(8,128)(2,1)S(1)}, bf16[32,3968]{1,0:T(8,128)(2,1)S(1)}, u32[]{:S(2)}, u32[]{:S(2)}) collective-permute-start(bf16[32,3968]{1,0:T(8,128)(2,1)S(1)} %collective-permute-done.2.refs_0_), channel_id=1, source_target_pairs={{0,1},{1,0},{2,3},{3,2},{4,5},{5,4},{6,7},{7,6},{8,9},{9,8},{10,11... | collective-permute-start | bytes 761864 | tf_op jit(solution)/shard_map/ppermute | solution.py:436
  20.3 6.6 %collective-permute-start.14 = (bf16[32,3968]{1,0:T(8,128)(2,1)S(1)}, bf16[32,3968]{1,0:T(8,128)(2,1)S(1)}, u32[]{:S(2)}, u32[]{:S(2)}) collective-permute-start(bf16[32,3968]{1,0:T(8,128)(2,1)S(1)} %collective-permute-done.8.refs_2_), channel_id=1, source_target_pairs={{0,1},{1,0},{2,3},{3,2},{4,5},{5,4},{6,7},{7,6},{8,9},{9,8},{10,11... | collective-permute-start | bytes 761864 | tf_op jit(solution)/shard_map/ppermute | solution.py:436
  20.6 6.3 %collective-permute-start.9 = (bf16[32,3968]{1,0:T(8,128)(2,1)S(1)}, bf16[32,3968]{1,0:T(8,128)(2,1)S(1)}, u32[]{:S(2)}, u32[]{:S(2)}) collective-permute-start(bf16[32,3968]{1,0:T(8,128)(2,1)S(1)} %collective-permute-done.8.refs_2_), channel_id=1, source_target_pairs={{0,4},{4,8},{8,12},{12,14},{14,10},{10,6},{6,2},{2,0},{1,3},{5,1},... | collective-permute-start | bytes 761864 | tf_op jit(solution)/shard_map/ppermute | solution.py:429
  23.6 3.2 %collective-permute-start.7 = (bf16[32,3968]{1,0:T(8,128)(2,1)S(1)}, bf16[32,3968]{1,0:T(8,128)(2,1)S(1)}, u32[]{:S(2)}, u32[]{:S(2)}) collective-permute-start(bf16[32,3968]{1,0:T(8,128)(2,1)S(1)} %collective-permute-done.3.refs_0_), channel_id=1, source_target_pairs={{0,1},{1,0},{2,3},{3,2},{4,5},{5,4},{6,7},{7,6},{8,9},{9,8},{10,11... | collective-permute-start | bytes 761864 | tf_op jit(solution)/shard_map/ppermute | solution.py:436
  23.7 6.3 %collective-permute-start.12 = (bf16[32,3968]{1,0:T(8,128)(2,1)S(1)}, bf16[32,3968]{1,0:T(8,128)(2,1)S(1)}, u32[]{:S(2)}, u32[]{:S(2)}) collective-permute-start(bf16[32,3968]{1,0:T(8,128)(2,1)S(1)} %collective-permute-done.3.refs_0_), channel_id=1, source_target_pairs={{0,4},{4,8},{8,12},{12,14},{14,10},{10,6},{6,2},{2,0},{1,3},{5,1},... | collective-permute-start | bytes 761864 | tf_op jit(solution)/shard_map/ppermute | solution.py:429
  26.9 1.5 %collective-permute-start.10 = (bf16[32,3968]{1,0:T(8,128)(2,1)S(1)}, bf16[32,3968]{1,0:T(8,128)(2,1)S(1)}, u32[]{:S(2)}, u32[]{:S(2)}) collective-permute-start(bf16[32,3968]{1,0:T(8,128)(2,1)S(1)} %collective-permute-done.9.refs_2_), channel_id=1, source_target_pairs={{0,1},{1,0},{2,3},{3,2},{4,5},{5,4},{6,7},{7,6},{8,9},{9,8},{10,11... | collective-permute-start | bytes 761864 | tf_op jit(solution)/shard_map/ppermute | solution.py:436
  30.0 1.5 %collective-permute-start.15 = (bf16[32,3968]{1,0:T(8,128)(2,1)S(1)}, bf16[32,3968]{1,0:T(8,128)(2,1)S(1)}, u32[]{:S(2)}, u32[]{:S(2)}) collective-permute-start(bf16[32,3968]{1,0:T(8,128)(2,1)S(1)} %collective-permute-done.12.refs_0_), channel_id=1, source_target_pairs={{0,1},{1,0},{2,3},{3,2},{4,5},{5,4},{6,7},{7,6},{8,9},{9,8},{10,11... | collective-permute-start | bytes 761864 | tf_op jit(solution)/shard_map/ppermute | solution.py:436
  30.4 3.0 %collective-permute-start.11 = (bf16[128,512]{1,0:T(8,128)(2,1)S(1)}, bf16[128,512]{1,0:T(8,128)(2,1)S(1)}, u32[]{:S(2)}, u32[]{:S(2)}) collective-permute-start(bf16[128,512]{1,0:T(8,128)(2,1)S(1)} %get-tuple-element.56.mine), channel_id=1, source_target_pairs={{0,1},{1,0},{2,3},{3,2},{4,5},{5,4},{6,7},{7,6},{8,9},{9,8},{10,11... | collective-permute-start | bytes 393224 | tf_op jit(solution)/shard_map/ppermute | solution.py:436
  33.0 1.8 %collective-permute-start.16 = (bf16[128,512]{1,0:T(8,128)(2,1)S(1)}, bf16[128,512]{1,0:T(8,128)(2,1)S(1)}, u32[]{:S(2)}, u32[]{:S(2)}) collective-permute-start(bf16[128,512]{1,0:T(8,128)(2,1)S(1)} %get-tuple-element.70.refs_0_), channel_id=1, source_target_pairs={{0,1},{1,0},{2,3},{3,2},{4,5},{5,4},{6,7},{7,6},{8,9},{9,8},{10,11... | collective-permute-start | bytes 393224 | tf_op jit(solution)/shard_map/ppermute | solution.py:436
  36.2 5.5 %collective-permute-start.17 = (bf16[32,1920]{1,0:T(8,128)(2,1)S(1)}, bf16[32,1920]{1,0:T(8,128)(2,1)S(1)}, u32[]{:S(2)}, u32[]{:S(2)}) collective-permute-start(bf16[32,1920]{1,0:T(8,128)(2,1)S(1)} %get-tuple-element.84), channel_id=1, source_target_pairs={{0,2},{1,3},{4,0},{5,1},{8,4},{9,5},{12,8},{13,9},{14,12},{15,13},... | collective-permute-start | bytes 368648 | tf_op jit(solution)/shard_map/ppermute | solution.py:433
  36.9 8.9 %collective-permute-start.18 = (bf16[128,512]{1,0:T(8,128)(2,1)S(1)}, bf16[128,512]{1,0:T(8,128)(2,1)S(1)}, u32[]{:S(2)}, u32[]{:S(2)}) collective-permute-start(bf16[128,512]{1,0:T(8,128)(2,1)S(1)} %get-tuple-element.74.refs_0_), channel_id=1, source_target_pairs={{0,1},{1,0},{2,3},{3,2},{4,5},{5,4},{6,7},{7,6},{8,9},{9,8},{10,11... | collective-permute-start | bytes 393224 | tf_op jit(solution)/shard_map/ppermute | solution.py:436
  37.0 7.4 %collective-permute-start.19 = (bf16[128,512]{1,0:T(8,128)(2,1)S(1)}, bf16[128,512]{1,0:T(8,128)(2,1)S(1)}, u32[]{:S(2)}, u32[]{:S(2)}) collective-permute-start(bf16[128,512]{1,0:T(8,128)(2,1)S(1)} %get-tuple-element.76.refs_0_), channel_id=1, source_target_pairs={{0,1},{1,0},{2,3},{3,2},{4,5},{5,4},{6,7},{7,6},{8,9},{9,8},{10,11... | collective-permute-start | bytes 393224 | tf_op jit(solution)/shard_map/ppermute | solution.py:436
  37.4 5.4 %collective-permute-start.20 = (bf16[32,1920]{1,0:T(8,128)(2,1)S(1)}, bf16[32,1920]{1,0:T(8,128)(2,1)S(1)}, u32[]{:S(2)}, u32[]{:S(2)}) collective-permute-start(bf16[32,1920]{1,0:T(8,128)(2,1)S(1)} %get-tuple-element.83), channel_id=1, source_target_pairs={{0,4},{1,5},{4,8},{5,9},{8,12},{9,13},{12,14},{13,15},{14,10},{15,... | collective-permute-start | bytes 368648 | tf_op jit(solution)/shard_map/ppermute | solution.py:433
  41.7 7.3 %collective-permute-start.24 = (bf16[64,1920]{1,0:T(8,128)(2,1)S(1)}, bf16[64,1920]{1,0:T(8,128)(2,1)S(1)}, u32[]{:S(2)}, u32[]{:S(2)}) collective-permute-start(bf16[64,1920]{1,0:T(8,128)(2,1)S(1)} %pad_maximum_fusion.1), channel_id=1, source_target_pairs={{0,2},{1,3},{4,0},{5,1},{8,4},{9,5},{12,8},{13,9},{14,12},{15,13},... | collective-permute-start | bytes 737288 | tf_op jit(solution)/shard_map/ppermute | solution.py:433
  42.9 7.3 %collective-permute-start.21 = (bf16[64,1920]{1,0:T(8,128)(2,1)S(1)}, bf16[64,1920]{1,0:T(8,128)(2,1)S(1)}, u32[]{:S(2)}, u32[]{:S(2)}) collective-permute-start(bf16[64,1920]{1,0:T(8,128)(2,1)S(1)} %pad_maximum_fusion), channel_id=1, source_target_pairs={{0,4},{1,5},{4,8},{5,9},{8,12},{9,13},{12,14},{13,15},{14,10},{15,... | collective-permute-start | bytes 737288 | tf_op jit(solution)/shard_map/ppermute | solution.py:433
  49.0 6.4 %collective-permute-start.25 = (bf16[64,1920]{1,0:T(8,128)(2,1)S(1)}, bf16[64,1920]{1,0:T(8,128)(2,1)S(1)}, u32[]{:S(2)}, u32[]{:S(2)}) collective-permute-start(bf16[64,1920]{1,0:T(8,128)(2,1)S(1)} %add_convert_fusion.1), channel_id=1, source_target_pairs={{0,2},{1,3},{4,0},{5,1},{8,4},{9,5},{12,8},{13,9},{14,12},{15,13},... | collective-permute-start | bytes 737288 | tf_op jit(solution)/shard_map/ppermute | solution.py:433
  50.2 12.8 %copy-start.1 = (bf16[384,384]{1,0:T(8,128)(2,1)S(1)}, bf16[384,384]{1,0:T(8,128)(2,1)}, u32[]{:S(2)}) copy-start(bf16[384,384]{1,0:T(8,128)(2,1)} %constant.23.clone.order) | copy-start | bytes 884740
  50.2 6.5 %collective-permute-start.22 = (bf16[64,1920]{1,0:T(8,128)(2,1)S(1)}, bf16[64,1920]{1,0:T(8,128)(2,1)S(1)}, u32[]{:S(2)}, u32[]{:S(2)}) collective-permute-start(bf16[64,1920]{1,0:T(8,128)(2,1)S(1)} %add_convert_fusion.3), channel_id=1, source_target_pairs={{0,4},{1,5},{4,8},{5,9},{8,12},{9,13},{12,14},{13,15},{14,10},{15,... | collective-permute-start | bytes 737288 | tf_op jit(solution)/shard_map/ppermute | solution.py:433
  55.4 6.2 %collective-permute-start.26 = (bf16[64,1920]{1,0:T(8,128)(2,1)S(1)}, bf16[64,1920]{1,0:T(8,128)(2,1)S(1)}, u32[]{:S(2)}, u32[]{:S(2)}) collective-permute-start(bf16[64,1920]{1,0:T(8,128)(2,1)S(1)} %add_convert_fusion), channel_id=1, source_target_pairs={{0,2},{1,3},{4,0},{5,1},{8,4},{9,5},{12,8},{13,9},{14,12},{15,13},... | collective-permute-start | bytes 737288 | tf_op jit(solution)/shard_map/ppermute | solution.py:433
  56.8 6.2 %collective-permute-start.23 = (bf16[64,1920]{1,0:T(8,128)(2,1)S(1)}, bf16[64,1920]{1,0:T(8,128)(2,1)S(1)}, u32[]{:S(2)}, u32[]{:S(2)}) collective-permute-start(bf16[64,1920]{1,0:T(8,128)(2,1)S(1)} %add_convert_fusion.2), channel_id=1, source_target_pairs={{0,4},{1,5},{4,8},{5,9},{8,12},{9,13},{12,14},{13,15},{14,10},{15,... | collective-permute-start | bytes 737288 | tf_op jit(solution)/shard_map/ppermute | solution.py:433
  63.4 1.4 %collective-permute-start.27 = (bf16[32,1920]{1,0:T(8,128)(2,1)S(1)}, bf16[32,1920]{1,0:T(8,128)(2,1)S(1)}, u32[]{:S(2)}, u32[]{:S(2)}) collective-permute-start(bf16[32,1920]{1,0:T(8,128)(2,1)S(1)} %constant_dynamic-slice_fusion), channel_id=1, source_target_pairs={{0,1},{1,0},{2,3},{3,2},{4,5},{5,4},{6,7},{7,6},{8,9},{9,8},{10,11... | collective-permute-start | bytes 368648 | tf_op jit(solution)/shard_map/ppermute | solution.py:436

commit v2 on v1

--- a/solution.py
+++ b/solution.py
@@ -366,11 +366,32 @@
         out[...] = produced[index * rows : (index + 1) * rows]
 
 
-def close_kernel(own, ahead, behind, order, out):
-    total = own[...] + (ahead[...].astype(jnp.float32) + behind[...].astype(jnp.float32))
-    folded = fold(total.astype(jnp.bfloat16), SPAN)
-    placed = jnp.dot(folded, order[...], preferred_element_type=jnp.float32)
-    out[...] = unfold(placed, total.shape[0]).astype(jnp.bfloat16)
+def last_join_kernel(part, came, mine, other):
+    for side, out in enumerate((mine, other)):
+        at = own_rows(out.shape[0], core_of(side))
+        out[...] = (part[at, :] + came[at, :].astype(jnp.float32)).astype(jnp.bfloat16)
+
+
+def sum_rows(side, own, ahead, behind):
+    at = own_rows(ahead.shape[0], core_of(side))
+    came = ahead[...].astype(jnp.float32) + behind[...].astype(jnp.float32)
+    return (own[at, :] + came).astype(jnp.bfloat16)
+
+
+def give_kernel(own, ahead, behind, out):
+    out[...] = sum_rows(1, own, ahead, behind)
+
+
+def close_kernel(own, ahead, behind, given, order, out):
+    rows, width = ahead.shape
+    halves = (sum_rows(0, own, ahead, behind), given[...])
+    folded = jnp.concatenate([fold(values, SPAN) for values in halves], axis=0)
+    placed = jnp.dot(folded, order[...], preferred_element_type=jnp.float32).astype(jnp.bfloat16)
+    height = placed.shape[0] // 2
+    for side in range(2):
+        column = pl.multiple_of(core_of(side) * width, width)
+        part = unfold(placed[side * height : (side + 1) * height], rows)
+        out[:, pl.ds(column, width)] = part
 
 
 def on_chip(values):
@@ -595,7 +616,7 @@
     went_behind = turn_hop(edge[half:].astype(jnp.bfloat16), -1)
     behind[2], ahead[2] = expert_out(second, after=went_behind)
     behind[1], ahead[1] = expert_out(near, after=went_behind)
-    for distance in range(far - 1, 0, -1):
+    for distance in range(far - 1, 1, -1):
         if distance == far - 1:
             send_ahead = jnp.concatenate(
                 [
@@ -615,19 +636,28 @@
             send_ahead = join(ahead[distance], went_ahead)
             send_behind = join(behind[distance], went_behind)
         went_ahead, went_behind = turn_hop(send_ahead, 1), turn_hop(send_behind, -1)
+    piece = ((half, down_features), jnp.bfloat16)
+
+    def last_join(part, came):
+        return whole_call(last_join_kernel, [piece] * 2, "last_join", part, came)
+
+    mine_ahead, other_ahead = last_join(ahead[1], went_ahead)
+    mine_behind, other_behind = last_join(behind[1], went_behind)
+    other_ahead, other_behind = turn_hop(other_ahead, 1), turn_hop(other_behind, -1)
+    mine_ahead, mine_behind = turn_hop(mine_ahead, 1), turn_hop(mine_behind, -1)
+    (given,) = whole_call(give_kernel, [piece], "give", own, other_ahead, other_behind)
     (mixed,) = whole_call(
         close_kernel,
-        [(own.shape, jnp.bfloat16)],
+        [((half, features), jnp.bfloat16)],
         "close",
         own,
-        went_ahead,
-        went_behind,
+        mine_ahead,
+        mine_behind,
+        swap(given),
         back,
-    )
-    mine, theirs = own_half(mixed), swap(own_half(mixed, other=True))
-    first = jnp.where(tp_index == 0, mine, theirs)
-    second = jnp.where(tp_index == 0, theirs, mine)
-    return jnp.concatenate([first, second], axis=1)
+        plain=True,
+    )
+    return mixed
 
 
 def solution(mesh):

time: 65.8 us -> 65.3 us (level)
  waiting for transfers between devices: 19.2 us -> 16.6 us
  starting transfers between devices: 25.6 us -> 27.7 us
  Pallas kernels: 19.3 us -> 20.2 us
  other arithmetic: 1.09 us -> 0.25 us
    ppermute x8 -> x10, waiting for transfers between devices: 14 us -> 11.4 us  [turn_hop(): return lax.ppermute(values, ('ep', 'tp'), pairs)]
    ppermute x8 -> x10, starting transfers between devices: 9.19 us -> 11.8 us  [turn_hop(): return lax.ppermute(values, ('ep', 'tp'), pairs)]
    pallas_call x15 -> x18, Pallas kernels: 19.3 us -> 20.2 us  [whole_call(): pl.pallas_call(body, in_specs=specs, out_specs=[vmem] * len(outs), out_sh...]
    concatenate x1 -> x0, other arithmetic: 0.71 us -> none  [dense_shards(): return jnp.concatenate([first, second], axis=1)]
  transfers between devices with their start and end apart: 28 -> 30, of which waited for: 15 -> 18; matrix products, arithmetic and copies ran while one was open for 0% -> 0% of each run, Pallas kernels for 26% -> 26%
where the time goes in v2:
time: 65.3 us; the launch traced here: 65.1 us
  starting transfers between devices  27.7 us (42%)
  Pallas kernels  20.2 us (31%)
  waiting for transfers between devices  16.6 us (25%)
    pallas_call x18, Pallas kernels, whole_call(): pl.pallas_call(body, in_specs=specs, out_specs=[vmem] * len(outs), out_sh...  20.2 us
    ppermute x7, starting transfers between devices, hop(): return lax.ppermute(values, ('ep', 'tp'), pairs)  13.5 us
    ppermute x10, starting transfers between devices, turn_hop(): return lax.ppermute(values, ('ep', 'tp'), pairs)  11.8 us
    ppermute x10, waiting for transfers between devices, turn_hop(): return lax.ppermute(values, ('ep', 'tp'), pairs)  11.4 us
    ppermute x7, waiting for transfers between devices, hop(): return lax.ppermute(values, ('ep', 'tp'), pairs)  2.83 us
    ppermute x13, starting transfers between devices, swap(): return lax.ppermute(values, 'tp', [(0, 1), (1, 0)])  2.46 us
    ppermute x13, waiting for transfers between devices, swap(): return lax.ppermute(values, 'tp', [(0, 1), (1, 0)])  2.45 us
  transfers between devices with their start and end apart: 30, of which 18 were waited for; matrix products, arithmetic and copies ran while one was open for 0% of the time, Pallas kernels for 26%

profile of v2, /device:TPU:0, one launch (start us, length us, event | category | flops | bytes accessed | tf_op | source)
XLA Modules:
  0.0 65.1 jit_solution(15257392064221981238)
XLA Ops:
  0.0 0.5 collective-permute-start
  0.5 1.8 %first.1 = (f32[64,3840]{1,0:T(8,128)S(1)}, f32[3840]{0:T(1024)S(1)}, bf16[384,384]{1,0:T(8,128)(2,1)S(1)}, bf16[64,128]{1,0:T(8,128)(2,1)S(1)}, f32[640,512]{1,0:T(8,128)S(1)}) custom-call(bf16[64,3840]{1,0:T(8,128)(2,1)} %bitcast.8, bf16[64,3840]{1,0:T(8,128)(2,1)} %resid.1, f32[3840]{0:T(1024)} %gain.1, bf16[384,384]{1,0:T(8,128)(2,1)} %constant.8.clone.signs, ...), custom_call_target="tpu_custom_call" | custom-call | tf_op jit(solution)/shard_map/first/pallas_call | solution.py:412
  2.3 0.6 prep.2.first.refs_2_
  2.9 2.9 %collective-permute-start.1 = (bf16[32,3968]{1,0:T(8,128)(2,1)S(1)}, bf16[32,3968]{1,0:T(8,128)(2,1)S(1)}, u32[]{:S(2)}, u32[]{:S(2)}) collective-permute-start(bf16[32,3968]{1,0:T(8,128)(2,1)S(1)} %prep.2.first.refs_2_), channel_id=1, source_target_pairs={{0,4},{4,8},{8,12},{12,14},{14,10},{10,6},{6,2},{2,0},{1,3},{5,1},... | collective-permute-start | bytes 761864 | tf_op jit(solution)/shard_map/ppermute | solution.py:450
  5.8 0.6 prep.3.first.refs_3_
  6.4 1.6 %collective-permute-start.5 = (bf16[32,3968]{1,0:T(8,128)(2,1)S(1)}, bf16[32,3968]{1,0:T(8,128)(2,1)S(1)}, u32[]{:S(2)}, u32[]{:S(2)}) collective-permute-start(bf16[32,3968]{1,0:T(8,128)(2,1)S(1)} %prep.3.first.refs_3_), channel_id=1, source_target_pairs={{0,4},{4,8},{8,12},{12,14},{14,10},{10,6},{6,2},{2,0},{1,3},{5,1},... | collective-permute-start | bytes 761864 | tf_op jit(solution)/shard_map/ppermute | solution.py:450
  8.1 1.7 %unpack_gate.1 = (bf16[3840,512]{1,0:T(8,128)(2,1)S(1)}, f32[640,512]{1,0:T(8,128)S(1)}, f32[320,1024]{1,0:T(8,128)S(1)}) custom-call(bf16[32,3968]{1,0:T(8,128)(2,1)S(1)} %prep.3.first.refs_3_, f32[640,512]{1,0:T(8,128)} %bitcast.11, f32[320,1024]{1,0:T(8,128)} %bitcast.12, f32[640,512]{1,0:T(8,128)S(1)} %get-tuple-element.51.refs_2_), custom_call_target="tpu_custom_call" | custom-call | flops 10000000000 | tf_op jit(solution)/shard_map/unpack_gate/pallas_call | solution.py:412
  10.0 2.1 %collective-permute-start.2 = (bf16[32,3968]{1,0:T(8,128)(2,1)S(1)}, bf16[32,3968]{1,0:T(8,128)(2,1)S(1)}, u32[]{:S(2)}, u32[]{:S(2)}) collective-permute-start(bf16[32,3968]{1,0:T(8,128)(2,1)S(1)} %collective-permute-done.1.refs_0_), channel_id=1, source_target_pairs={{0,4},{4,8},{8,12},{12,14},{14,10},{10,6},{6,2},{2,0},{1,3},{5,1},... | collective-permute-start | bytes 761864 | tf_op jit(solution)/shard_map/ppermute | solution.py:450
  12.1 1.4 %unpack_up.1.refs_5_.first = bf16[3840,512]{1,0:T(8,128)(2,1)S(1)} custom-call(bf16[3840,512]{1,0:T(8,128)(2,1)S(1)} %get-tuple-element.52.first.refs_4_, f32[640,512]{1,0:T(8,128)S(1)} %get-tuple-element.54.refs_0_), custom_call_target="tpu_custom_call" | custom-call | flops 10000000000 | tf_op jit(solution)/shard_map/unpack_up/pallas_call | solution.py:412
  13.5 0.5 collective-permute-start.6
  14.0 1.6 %collective-permute-start.8 = (bf16[32,3968]{1,0:T(8,128)(2,1)S(1)}, bf16[32,3968]{1,0:T(8,128)(2,1)S(1)}, u32[]{:S(2)}, u32[]{:S(2)}) collective-permute-start(bf16[32,3968]{1,0:T(8,128)(2,1)S(1)} %collective-permute-done.5.refs_2_), channel_id=1, source_target_pairs={{0,4},{4,8},{8,12},{12,14},{14,10},{10,6},{6,2},{2,0},{1,3},{5,1},... | collective-permute-start | bytes 761864 | tf_op jit(solution)/shard_map/ppermute | solution.py:450
  15.6 0.6 collective-permute-done.2.refs_0_
  16.3 2.1 %collective-permute-start.3 = (bf16[32,3968]{1,0:T(8,128)(2,1)S(1)}, bf16[32,3968]{1,0:T(8,128)(2,1)S(1)}, u32[]{:S(2)}, u32[]{:S(2)}) collective-permute-start(bf16[32,3968]{1,0:T(8,128)(2,1)S(1)} %collective-permute-done.2.refs_0_), channel_id=1, source_target_pairs={{0,4},{4,8},{8,12},{12,14},{14,10},{10,6},{6,2},{2,0},{1,3},{5,1},... | collective-permute-start | bytes 761864 | tf_op jit(solution)/shard_map/ppermute | solution.py:450
  18.4 1.6 %unpack_down.1 = (bf16[1920,1024]{1,0:T(8,128)(2,1)S(1)}, f32[8,1920]{1,0:T(8,128)S(1)}) custom-call(bf16[3840,512]{1,0:T(8,128)(2,1)S(1)} %unpack_up.1.refs_5_.first, f32[320,1024]{1,0:T(8,128)S(1)} %get-tuple-element.57.refs_0_, f32[1,1920]{1,0:T(1,128)S(1)} %copy-done.4, bf16[384,384]{1,0:T(8,128)(2,1)S(1)} %copy-done.5), custom_call_target="tpu_custom_call" | custom-call | flops 10000000000 | tf_op jit(solution)/shard_map/unpack_down/pallas_call | solution.py:412
  20.6 1.6 %collective-permute-start.9 = (bf16[32,3968]{1,0:T(8,128)(2,1)S(1)}, bf16[32,3968]{1,0:T(8,128)(2,1)S(1)}, u32[]{:S(2)}, u32[]{:S(2)}) collective-permute-start(bf16[32,3968]{1,0:T(8,128)(2,1)S(1)} %collective-permute-done.8.refs_2_), channel_id=1, source_target_pairs={{0,4},{4,8},{8,12},{12,14},{14,10},{10,6},{6,2},{2,0},{1,3},{5,1},... | collective-permute-start | bytes 761864 | tf_op jit(solution)/shard_map/ppermute | solution.py:450
  22.2 1.4 %hidden_part.4 = (bf16[128,512]{1,0:T(8,128)(2,1)S(1)}, f32[128,128]{1,0:T(8,128)S(1)}) custom-call(bf16[32,3968]{1,0:T(8,128)(2,1)S(1)} %collective-permute-done.1.refs_0_, bf16[32,3968]{1,0:T(8,128)(2,1)S(1)} %collective-permute-done.4.refs_1_, bf16[32,3968]{1,0:T(8,128)(2,1)S(1)} %collective-permute-done.5.refs_2_, ...), custom_call_target="tpu_custom_call" | custom-call | flops 1000000000 | tf_op jit(solution)/shard_map/hidden_part/pallas_call | solution.py:412
  23.7 1.6 %collective-permute-start.12 = (bf16[32,3968]{1,0:T(8,128)(2,1)S(1)}, bf16[32,3968]{1,0:T(8,128)(2,1)S(1)}, u32[]{:S(2)}, u32[]{:S(2)}) collective-permute-start(bf16[32,3968]{1,0:T(8,128)(2,1)S(1)} %collective-permute-done.3.refs_0_), channel_id=1, source_target_pairs={{0,4},{4,8},{8,12},{12,14},{14,10},{10,6},{6,2},{2,0},{1,3},{5,1},... | collective-permute-start | bytes 761864 | tf_op jit(solution)/shard_map/ppermute | solution.py:450
  25.3 1.5 %collective-permute-done.9.refs_2_ = bf16[32,3968]{1,0:T(8,128)(2,1)S(1)} collective-permute-done((bf16[32,3968]{1,0:T(8,128)(2,1)S(1)}, bf16[32,3968]{1,0:T(8,128)(2,1)S(1)}, u32[]{:S(2)}, u32[]{:S(2)}) %collective-permute-start.9) | collective-permute-done | bytes 253984 | tf_op jit(solution)/shard_map/ppermute | solution.py:450
  26.9 1.4 %hidden_part.6 = (bf16[128,512]{1,0:T(8,128)(2,1)S(1)}, f32[128,128]{1,0:T(8,128)S(1)}) custom-call(bf16[32,3968]{1,0:T(8,128)(2,1)S(1)} %collective-permute-done.2.refs_0_, bf16[32,3968]{1,0:T(8,128)(2,1)S(1)} %collective-permute-done.13.refs_1_, bf16[32,3968]{1,0:T(8,128)(2,1)S(1)} %collective-permute-done.8.refs_2_, ...), custom_call_target="tpu_custom_call" | custom-call | flops 10000000000 | tf_op jit(solution)/shard_map/hidden_part/pallas_call | solution.py:412
  28.4 1.4 %hidden_part.5 = (bf16[128,512]{1,0:T(8,128)(2,1)S(1)}, f32[128,128]{1,0:T(8,128)S(1)}) custom-call(bf16[32,3968]{1,0:T(8,128)(2,1)S(1)} %collective-permute-done.3.refs_0_, bf16[32,3968]{1,0:T(8,128)(2,1)S(1)} %collective-permute-done.7.refs_1_, bf16[32,3968]{1,0:T(8,128)(2,1)S(1)} %collective-permute-done.9.refs_2_, ...), custom_call_target="tpu_custom_call" | custom-call | flops 1000000000 | tf_op jit(solution)/shard_map/hidden_part/pallas_call | solution.py:412
  30.0 0.3 collective-permute-start.15
  30.5 1.0 %collective-permute-done.15.refs_1_ = bf16[32,3968]{1,0:T(8,128)(2,1)S(1)} collective-permute-done((bf16[32,3968]{1,0:T(8,128)(2,1)S(1)}, bf16[32,3968]{1,0:T(8,128)(2,1)S(1)}, u32[]{:S(2)}, u32[]{:S(2)}) %collective-permute-start.15) | collective-permute-done | bytes 253984 | tf_op jit(solution)/shard_map/ppermute | solution.py:457
  31.6 1.4 %hidden_part.7 = (bf16[128,512]{1,0:T(8,128)(2,1)S(1)}, f32[128,128]{1,0:T(8,128)S(1)}) custom-call(bf16[32,3968]{1,0:T(8,128)(2,1)S(1)} %collective-permute-done.12.refs_0_, bf16[32,3968]{1,0:T(8,128)(2,1)S(1)} %collective-permute-done.15.refs_1_, bf16[32,3968]{1,0:T(8,128)(2,1)S(1)} %prep.2.first.refs_2_, bf16[32,3968]{1,0:T(8,128)(2,1)S(1)} %prep.3.first.refs_3_, ...), custom_call_target="tpu_custom_call" | custom-call | flops 1000000000 | tf_op jit(solution)/shard_map/hidden_part/pallas_call | solution.py:412
  33.0 0.4 collective-permute-start.16
  33.4 1.4 %down_part.4 = (f32[64,1920]{1,0:T(8,128)S(1)}, f32[64,1920]{1,0:T(8,128)S(1)}) custom-call(bf16[128,512]{1,0:T(8,128)(2,1)S(1)} %get-tuple-element.60.mine, bf16[128,512]{1,0:T(8,128)(2,1)S(1)} %collective-permute-done.11.theirs, bf16[1920,1024]{1,0:T(8,128)(2,1)S(1)} %get-tuple-element.61.levels.refs_2_, f32[8,1920]{1,0:T(8,128)S(1)} %get-tuple-element.58.down_row.refs_3_, ...), custom_call_target="tpu_custom_call" | custom-call | flops 503316480 | tf_op jit(solution)/shard_map/down_part/pallas_call | solution.py:412
  34.8 1.4 %down_part.5 = (f32[64,1920]{1,0:T(8,128)S(1)}, f32[64,1920]{1,0:T(8,128)S(1)}) custom-call(f32[64,1920]{1,0:T(8,128)S(1)} %get-tuple-element.63.first, bf16[128,512]{1,0:T(8,128)(2,1)S(1)} %get-tuple-element.74.refs_0_, bf16[128,512]{1,0:T(8,128)(2,1)S(1)} %collective-permute-done.16.refs_1_, bf16[1920,1024]{1,0:T(8,128)(2,1)S(1)} %get-tuple-element.61.levels.refs_2_, ...), custom_call_target="tpu_custom_call" | custom-call | flops 503316480 | tf_op jit(solution)/shard_map/down_part/pallas_call | solution.py:412
  36.2 0.7 %collective-permute-start.17 = (bf16[32,1920]{1,0:T(8,128)(2,1)S(1)}, bf16[32,1920]{1,0:T(8,128)(2,1)S(1)}, u32[]{:S(2)}, u32[]{:S(2)}) collective-permute-start(bf16[32,1920]{1,0:T(8,128)(2,1)S(1)} %get-tuple-element.90), channel_id=1, source_target_pairs={{0,2},{1,3},{4,0},{5,1},{8,4},{9,5},{12,8},{13,9},{14,12},{15,13},... | collective-permute-start | bytes 368648 | tf_op jit(solution)/shard_map/ppermute | solution.py:454
  37.0 1.4 %collective-permute-start.20 = (bf16[32,1920]{1,0:T(8,128)(2,1)S(1)}, bf16[32,1920]{1,0:T(8,128)(2,1)S(1)}, u32[]{:S(2)}, u32[]{:S(2)}) collective-permute-start(bf16[32,1920]{1,0:T(8,128)(2,1)S(1)} %get-tuple-element.89), channel_id=1, source_target_pairs={{0,4},{1,5},{4,8},{5,9},{8,12},{9,13},{12,14},{13,15},{14,10},{15,... | collective-permute-start | bytes 368648 | tf_op jit(solution)/shard_map/ppermute | solution.py:454
  38.4 3.3 %collective-permute-done.17.first = bf16[32,1920]{1,0:T(8,128)(2,1)S(1)} collective-permute-done((bf16[32,1920]{1,0:T(8,128)(2,1)S(1)}, bf16[32,1920]{1,0:T(8,128)(2,1)S(1)}, u32[]{:S(2)}, u32[]{:S(2)}) %collective-permute-start.17) | collective-permute-done | bytes 122912 | tf_op jit(solution)/shard_map/ppermute | solution.py:454
  41.7 0.9 %collective-permute-start.24 = (bf16[64,1920]{1,0:T(8,128)(2,1)S(1)}, bf16[64,1920]{1,0:T(8,128)(2,1)S(1)}, u32[]{:S(2)}, u32[]{:S(2)}) collective-permute-start(bf16[64,1920]{1,0:T(8,128)(2,1)S(1)} %pad_maximum_fusion.1), channel_id=1, source_target_pairs={{0,2},{1,3},{4,0},{5,1},{8,4},{9,5},{12,8},{13,9},{14,12},{15,13},... | collective-permute-start | bytes 737288 | tf_op jit(solution)/shard_map/ppermute | solution.py:454
  42.8 1.4 %collective-permute-start.21 = (bf16[64,1920]{1,0:T(8,128)(2,1)S(1)}, bf16[64,1920]{1,0:T(8,128)(2,1)S(1)}, u32[]{:S(2)}, u32[]{:S(2)}) collective-permute-start(bf16[64,1920]{1,0:T(8,128)(2,1)S(1)} %pad_maximum_fusion), channel_id=1, source_target_pairs={{0,4},{1,5},{4,8},{5,9},{8,12},{9,13},{12,14},{13,15},{14,10},{15,... | collective-permute-start | bytes 737288 | tf_op jit(solution)/shard_map/ppermute | solution.py:454
  44.2 1.4 %down_part.7 = (f32[64,1920]{1,0:T(8,128)S(1)}, f32[64,1920]{1,0:T(8,128)S(1)}) custom-call(bf16[32,1920]{1,0:T(8,128)(2,1)S(1)} %collective-permute-done.17.first, bf16[128,512]{1,0:T(8,128)(2,1)S(1)} %get-tuple-element.80.refs_0_, bf16[128,512]{1,0:T(8,128)(2,1)S(1)} %collective-permute-done.19.refs_1_, ...), custom_call_target="tpu_custom_call" | custom-call | flops 503316480 | tf_op jit(solution)/shard_map/down_part/pallas_call | solution.py:412
  45.6 3.4 %collective-permute-done.24 = bf16[64,1920]{1,0:T(8,128)(2,1)S(1)} collective-permute-done((bf16[64,1920]{1,0:T(8,128)(2,1)S(1)}, bf16[64,1920]{1,0:T(8,128)(2,1)S(1)}, u32[]{:S(2)}, u32[]{:S(2)}) %collective-permute-start.24) | collective-permute-done | bytes 245792 | tf_op jit(solution)/shard_map/ppermute | solution.py:454
  49.1 1.1 %collective-permute-start.25 = (bf16[64,1920]{1,0:T(8,128)(2,1)S(1)}, bf16[64,1920]{1,0:T(8,128)(2,1)S(1)}, u32[]{:S(2)}, u32[]{:S(2)}) collective-permute-start(bf16[64,1920]{1,0:T(8,128)(2,1)S(1)} %add_convert_fusion), channel_id=1, source_target_pairs={{0,2},{1,3},{4,0},{5,1},{8,4},{9,5},{12,8},{13,9},{14,12},{15,13},... | collective-permute-start | bytes 737288 | tf_op jit(solution)/shard_map/ppermute | solution.py:454
  50.4 1.5 %collective-permute-start.22 = (bf16[64,1920]{1,0:T(8,128)(2,1)S(1)}, bf16[64,1920]{1,0:T(8,128)(2,1)S(1)}, u32[]{:S(2)}, u32[]{:S(2)}) collective-permute-start(bf16[64,1920]{1,0:T(8,128)(2,1)S(1)} %add_convert_fusion.1), channel_id=1, source_target_pairs={{0,4},{1,5},{4,8},{5,9},{8,12},{9,13},{12,14},{13,15},{14,10},{15,... | collective-permute-start | bytes 737288 | tf_op jit(solution)/shard_map/ppermute | solution.py:454
  51.9 1.3 %collective-permute-done.18.refs_1_ = bf16[128,512]{1,0:T(8,128)(2,1)S(1)} collective-permute-done((bf16[128,512]{1,0:T(8,128)(2,1)S(1)}, bf16[128,512]{1,0:T(8,128)(2,1)S(1)}, u32[]{:S(2)}, u32[]{:S(2)}) %collective-permute-start.18) | collective-permute-done | bytes 131104 | tf_op jit(solution)/shard_map/ppermute | solution.py:457
  53.3 1.4 %down_part.6 = (f32[64,1920]{1,0:T(8,128)S(1)}, f32[64,1920]{1,0:T(8,128)S(1)}) custom-call(bf16[32,1920]{1,0:T(8,128)(2,1)S(1)} %collective-permute-done.17.first, bf16[128,512]{1,0:T(8,128)(2,1)S(1)} %get-tuple-element.78.refs_0_, bf16[128,512]{1,0:T(8,128)(2,1)S(1)} %collective-permute-done.18.refs_1_, ...), custom_call_target="tpu_custom_call" | custom-call | flops 503316480 | tf_op jit(solution)/shard_map/down_part/pallas_call | solution.py:412
  54.7 0.8 %collective-permute-done.25.came = bf16[64,1920]{1,0:T(8,128)(2,1)S(1)} collective-permute-done((bf16[64,1920]{1,0:T(8,128)(2,1)S(1)}, bf16[64,1920]{1,0:T(8,128)(2,1)S(1)}, u32[]{:S(2)}, u32[]{:S(2)}) %collective-permute-start.25) | collective-permute-done | bytes 245792 | tf_op jit(solution)/shard_map/ppermute | solution.py:454
  55.5 1.3 %collective-permute-start.28 = (bf16[32,1920]{1,0:T(8,128)(2,1)S(1)}, bf16[32,1920]{1,0:T(8,128)(2,1)S(1)}, u32[]{:S(2)}, u32[]{:S(2)}) collective-permute-start(bf16[32,1920]{1,0:T(8,128)(2,1)S(1)} %get-tuple-element.88), channel_id=1, source_target_pairs={{0,2},{1,3},{4,0},{5,1},{8,4},{9,5},{12,8},{13,9},{14,12},{15,13},... | collective-permute-start | bytes 368648 | tf_op jit(solution)/shard_map/ppermute | solution.py:454
  56.8 0.3 collective-permute-done.22.came
  57.1 1.6 %collective-permute-start.27 = (bf16[32,1920]{1,0:T(8,128)(2,1)S(1)}, bf16[32,1920]{1,0:T(8,128)(2,1)S(1)}, u32[]{:S(2)}, u32[]{:S(2)}) collective-permute-start(bf16[32,1920]{1,0:T(8,128)(2,1)S(1)} %get-tuple-element.87), channel_id=1, source_target_pairs={{0,4},{1,5},{4,8},{5,9},{8,12},{9,13},{12,14},{13,15},{14,10},{15,... | collective-permute-start | bytes 368648 | tf_op jit(solution)/shard_map/ppermute | solution.py:454
  58.7 0.5 collective-permute-start.26
  59.2 1.5 %collective-permute-start.23 = (bf16[32,1920]{1,0:T(8,128)(2,1)S(1)}, bf16[32,1920]{1,0:T(8,128)(2,1)S(1)}, u32[]{:S(2)}, u32[]{:S(2)}) collective-permute-start(bf16[32,1920]{1,0:T(8,128)(2,1)S(1)} %get-tuple-element.82), channel_id=1, source_target_pairs={{0,4},{1,5},{4,8},{5,9},{8,12},{9,13},{12,14},{13,15},{14,10},{15,... | collective-permute-start | bytes 368648 | tf_op jit(solution)/shard_map/ppermute | solution.py:454
  60.8 1.0 %collective-permute-done.28.behind = bf16[32,1920]{1,0:T(8,128)(2,1)S(1)} collective-permute-done((bf16[32,1920]{1,0:T(8,128)(2,1)S(1)}, bf16[32,1920]{1,0:T(8,128)(2,1)S(1)}, u32[]{:S(2)}, u32[]{:S(2)}) %collective-permute-start.28) | collective-permute-done | bytes 122912 | tf_op jit(solution)/shard_map/ppermute | solution.py:454
  61.7 0.4 collective-permute-done.27.ahead
  62.2 1.4 %collective-permute-done.26.behind = bf16[32,1920]{1,0:T(8,128)(2,1)S(1)} collective-permute-done((bf16[32,1920]{1,0:T(8,128)(2,1)S(1)}, bf16[32,1920]{1,0:T(8,128)(2,1)S(1)}, u32[]{:S(2)}, u32[]{:S(2)}) %collective-permute-start.26) | collective-permute-done | bytes 122912 | tf_op jit(solution)/shard_map/ppermute | solution.py:454
  63.6 0.5 collective-permute-done.23.ahead
  64.1 1.0 %close.1 = bf16[32,3840]{1,0:T(8,128)(2,1)} custom-call(f32[64,1920]{1,0:T(8,128)S(1)} %get-tuple-element.76.own, bf16[32,1920]{1,0:T(8,128)(2,1)S(1)} %collective-permute-done.23.ahead, bf16[32,1920]{1,0:T(8,128)(2,1)S(1)} %collective-permute-done.26.behind, bf16[32,1920]{1,0:T(8,128)(2,1)S(1)} %collective-permute-done.29.given, bf16[384,384]{1,0:T(8,128)(2,1)S(1)} %copy-done.1), custom_call_target="tpu_custom_call" | custom-call | tf_op jit(solution)/shard_map/close/pallas_call | solution.py:412
  (52 shorter events, 2.4 us)
Async XLA Ops:
  0.0 2.3 %collective-permute-start = (bf16[64,3840]{1,0:T(8,128)(2,1)}, bf16[64,3840]{1,0:T(8,128)(2,1)S(1)}, u32[]{:S(2)}, u32[]{:S(2)}) collective-permute-start(bf16[64,3840]{1,0:T(8,128)(2,1)} %bitcast.7), channel_id=1, source_target_pairs={{0,1},{1,0},{2,3},{3,2},{4,5},{5,4},{6,7},{7,6},{8,9},{9,8},{10,11... | collective-permute-start | bytes 1474568 | tf_op jit(solution)/shard_map/ppermute | solution.py:457
  2.9 7.0 %collective-permute-start.1 = (bf16[32,3968]{1,0:T(8,128)(2,1)S(1)}, bf16[32,3968]{1,0:T(8,128)(2,1)S(1)}, u32[]{:S(2)}, u32[]{:S(2)}) collective-permute-start(bf16[32,3968]{1,0:T(8,128)(2,1)S(1)} %prep.2.first.refs_2_), channel_id=1, source_target_pairs={{0,4},{4,8},{8,12},{12,14},{14,10},{10,6},{6,2},{2,0},{1,3},{5,1},... | collective-permute-start | bytes 761864 | tf_op jit(solution)/shard_map/ppermute | solution.py:450
  6.4 7.1 %collective-permute-start.5 = (bf16[32,3968]{1,0:T(8,128)(2,1)S(1)}, bf16[32,3968]{1,0:T(8,128)(2,1)S(1)}, u32[]{:S(2)}, u32[]{:S(2)}) collective-permute-start(bf16[32,3968]{1,0:T(8,128)(2,1)S(1)} %prep.3.first.refs_3_), channel_id=1, source_target_pairs={{0,4},{4,8},{8,12},{12,14},{14,10},{10,6},{6,2},{2,0},{1,3},{5,1},... | collective-permute-start | bytes 761864 | tf_op jit(solution)/shard_map/ppermute | solution.py:450
  10.0 6.3 %collective-permute-start.2 = (bf16[32,3968]{1,0:T(8,128)(2,1)S(1)}, bf16[32,3968]{1,0:T(8,128)(2,1)S(1)}, u32[]{:S(2)}, u32[]{:S(2)}) collective-permute-start(bf16[32,3968]{1,0:T(8,128)(2,1)S(1)} %collective-permute-done.1.refs_0_), channel_id=1, source_target_pairs={{0,4},{4,8},{8,12},{12,14},{14,10},{10,6},{6,2},{2,0},{1,3},{5,1},... | collective-permute-start | bytes 761864 | tf_op jit(solution)/shard_map/ppermute | solution.py:450
  12.1 6.3 %copy-start.4 = (f32[1,1920]{1,0:T(1,128)S(1)}, f32[1,1920]{1,0:T(1,128)}, u32[]{:S(2)}) copy-start(f32[1,1920]{1,0:T(1,128)} %refs_1_.1) | copy-start | bytes 23044
  12.1 6.3 %copy-start.5 = (bf16[384,384]{1,0:T(8,128)(2,1)S(1)}, bf16[384,384]{1,0:T(8,128)(2,1)}, u32[]{:S(2)}) copy-start(bf16[384,384]{1,0:T(8,128)(2,1)} %constant.10.clone.refs_2_) | copy-start | bytes 884740
  13.4 7.1 %collective-permute-start.4 = (bf16[32,3968]{1,0:T(8,128)(2,1)S(1)}, bf16[32,3968]{1,0:T(8,128)(2,1)S(1)}, u32[]{:S(2)}, u32[]{:S(2)}) collective-permute-start(bf16[32,3968]{1,0:T(8,128)(2,1)S(1)} %collective-permute-done.1.refs_0_), channel_id=1, source_target_pairs={{0,1},{1,0},{2,3},{3,2},{4,5},{5,4},{6,7},{7,6},{8,9},{9,8},{10,11... | collective-permute-start | bytes 761864 | tf_op jit(solution)/shard_map/ppermute | solution.py:457
  13.5 8.6 %collective-permute-start.6 = (bf16[32,3968]{1,0:T(8,128)(2,1)S(1)}, bf16[32,3968]{1,0:T(8,128)(2,1)S(1)}, u32[]{:S(2)}, u32[]{:S(2)}) collective-permute-start(bf16[32,3968]{1,0:T(8,128)(2,1)S(1)} %collective-permute-done.5.refs_2_), channel_id=1, source_target_pairs={{0,1},{1,0},{2,3},{3,2},{4,5},{5,4},{6,7},{7,6},{8,9},{9,8},{10,11... | collective-permute-start | bytes 761864 | tf_op jit(solution)/shard_map/ppermute | solution.py:457
  14.0 6.3 %collective-permute-start.8 = (bf16[32,3968]{1,0:T(8,128)(2,1)S(1)}, bf16[32,3968]{1,0:T(8,128)(2,1)S(1)}, u32[]{:S(2)}, u32[]{:S(2)}) collective-permute-start(bf16[32,3968]{1,0:T(8,128)(2,1)S(1)} %collective-permute-done.5.refs_2_), channel_id=1, source_target_pairs={{0,4},{4,8},{8,12},{12,14},{14,10},{10,6},{6,2},{2,0},{1,3},{5,1},... | collective-permute-start | bytes 761864 | tf_op jit(solution)/shard_map/ppermute | solution.py:450
  16.3 7.4 %collective-permute-start.3 = (bf16[32,3968]{1,0:T(8,128)(2,1)S(1)}, bf16[32,3968]{1,0:T(8,128)(2,1)S(1)}, u32[]{:S(2)}, u32[]{:S(2)}) collective-permute-start(bf16[32,3968]{1,0:T(8,128)(2,1)S(1)} %collective-permute-done.2.refs_0_), channel_id=1, source_target_pairs={{0,4},{4,8},{8,12},{12,14},{14,10},{10,6},{6,2},{2,0},{1,3},{5,1},... | collective-permute-start | bytes 761864 | tf_op jit(solution)/shard_map/ppermute | solution.py:450
  18.4 3.8 %copy-start = (bf16[256,256]{1,0:T(8,128)(2,1)S(1)}, bf16[256,256]{1,0:T(8,128)(2,1)}, u32[]{:S(2)}) copy-start(bf16[256,256]{1,0:T(8,128)(2,1)} %constant.9.clone.refs_8_) | copy-start | bytes 393220
  18.4 3.8 %copy-start.2 = (f32[1,512]{1,0:T(1,128)S(1)}, f32[1,512]{1,0:T(1,128)}, u32[]{:S(2)}) copy-start(f32[1,512]{1,0:T(1,128)} %refs_6_.7) | copy-start | bytes 6148
  18.4 3.8 %copy-start.3 = (f32[1,512]{1,0:T(1,128)S(1)}, f32[1,512]{1,0:T(1,128)}, u32[]{:S(2)}) copy-start(f32[1,512]{1,0:T(1,128)} %refs_7_.7) | copy-start | bytes 6148
  20.0 6.9 %collective-permute-start.13 = (bf16[32,3968]{1,0:T(8,128)(2,1)S(1)}, bf16[32,3968]{1,0:T(8,128)(2,1)S(1)}, u32[]{:S(2)}, u32[]{:S(2)}) collective-permute-start(bf16[32,3968]{1,0:T(8,128)(2,1)S(1)} %collective-permute-done.2.refs_0_), channel_id=1, source_target_pairs={{0,1},{1,0},{2,3},{3,2},{4,5},{5,4},{6,7},{7,6},{8,9},{9,8},{10,11... | collective-permute-start | bytes 761864 | tf_op jit(solution)/shard_map/ppermute | solution.py:457
  20.3 6.6 %collective-permute-start.14 = (bf16[32,3968]{1,0:T(8,128)(2,1)S(1)}, bf16[32,3968]{1,0:T(8,128)(2,1)S(1)}, u32[]{:S(2)}, u32[]{:S(2)}) collective-permute-start(bf16[32,3968]{1,0:T(8,128)(2,1)S(1)} %collective-permute-done.8.refs_2_), channel_id=1, source_target_pairs={{0,1},{1,0},{2,3},{3,2},{4,5},{5,4},{6,7},{7,6},{8,9},{9,8},{10,11... | collective-permute-start | bytes 761864 | tf_op jit(solution)/shard_map/ppermute | solution.py:457
  20.6 6.3 %collective-permute-start.9 = (bf16[32,3968]{1,0:T(8,128)(2,1)S(1)}, bf16[32,3968]{1,0:T(8,128)(2,1)S(1)}, u32[]{:S(2)}, u32[]{:S(2)}) collective-permute-start(bf16[32,3968]{1,0:T(8,128)(2,1)S(1)} %collective-permute-done.8.refs_2_), channel_id=1, source_target_pairs={{0,4},{4,8},{8,12},{12,14},{14,10},{10,6},{6,2},{2,0},{1,3},{5,1},... | collective-permute-start | bytes 761864 | tf_op jit(solution)/shard_map/ppermute | solution.py:450
  23.6 3.3 %collective-permute-start.7 = (bf16[32,3968]{1,0:T(8,128)(2,1)S(1)}, bf16[32,3968]{1,0:T(8,128)(2,1)S(1)}, u32[]{:S(2)}, u32[]{:S(2)}) collective-permute-start(bf16[32,3968]{1,0:T(8,128)(2,1)S(1)} %collective-permute-done.3.refs_0_), channel_id=1, source_target_pairs={{0,1},{1,0},{2,3},{3,2},{4,5},{5,4},{6,7},{7,6},{8,9},{9,8},{10,11... | collective-permute-start | bytes 761864 | tf_op jit(solution)/shard_map/ppermute | solution.py:457
  23.7 6.3 %collective-permute-start.12 = (bf16[32,3968]{1,0:T(8,128)(2,1)S(1)}, bf16[32,3968]{1,0:T(8,128)(2,1)S(1)}, u32[]{:S(2)}, u32[]{:S(2)}) collective-permute-start(bf16[32,3968]{1,0:T(8,128)(2,1)S(1)} %collective-permute-done.3.refs_0_), channel_id=1, source_target_pairs={{0,4},{4,8},{8,12},{12,14},{14,10},{10,6},{6,2},{2,0},{1,3},{5,1},... | collective-permute-start | bytes 761864 | tf_op jit(solution)/shard_map/ppermute | solution.py:450
  26.9 1.5 %collective-permute-start.10 = (bf16[32,3968]{1,0:T(8,128)(2,1)S(1)}, bf16[32,3968]{1,0:T(8,128)(2,1)S(1)}, u32[]{:S(2)}, u32[]{:S(2)}) collective-permute-start(bf16[32,3968]{1,0:T(8,128)(2,1)S(1)} %collective-permute-done.9.refs_2_), channel_id=1, source_target_pairs={{0,1},{1,0},{2,3},{3,2},{4,5},{5,4},{6,7},{7,6},{8,9},{9,8},{10,11... | collective-permute-start | bytes 761864 | tf_op jit(solution)/shard_map/ppermute | solution.py:457
  30.0 1.5 %collective-permute-start.15 = (bf16[32,3968]{1,0:T(8,128)(2,1)S(1)}, bf16[32,3968]{1,0:T(8,128)(2,1)S(1)}, u32[]{:S(2)}, u32[]{:S(2)}) collective-permute-start(bf16[32,3968]{1,0:T(8,128)(2,1)S(1)} %collective-permute-done.12.refs_0_), channel_id=1, source_target_pairs={{0,1},{1,0},{2,3},{3,2},{4,5},{5,4},{6,7},{7,6},{8,9},{9,8},{10,11... | collective-permute-start | bytes 761864 | tf_op jit(solution)/shard_map/ppermute | solution.py:457
  30.4 3.0 %collective-permute-start.11 = (bf16[128,512]{1,0:T(8,128)(2,1)S(1)}, bf16[128,512]{1,0:T(8,128)(2,1)S(1)}, u32[]{:S(2)}, u32[]{:S(2)}) collective-permute-start(bf16[128,512]{1,0:T(8,128)(2,1)S(1)} %get-tuple-element.60.mine), channel_id=1, source_target_pairs={{0,1},{1,0},{2,3},{3,2},{4,5},{5,4},{6,7},{7,6},{8,9},{9,8},{10,11... | collective-permute-start | bytes 393224 | tf_op jit(solution)/shard_map/ppermute | solution.py:457
  33.0 1.8 %collective-permute-start.16 = (bf16[128,512]{1,0:T(8,128)(2,1)S(1)}, bf16[128,512]{1,0:T(8,128)(2,1)S(1)}, u32[]{:S(2)}, u32[]{:S(2)}) collective-permute-start(bf16[128,512]{1,0:T(8,128)(2,1)S(1)} %get-tuple-element.74.refs_0_), channel_id=1, source_target_pairs={{0,1},{1,0},{2,3},{3,2},{4,5},{5,4},{6,7},{7,6},{8,9},{9,8},{10,11... | collective-permute-start | bytes 393224 | tf_op jit(solution)/shard_map/ppermute | solution.py:457
  36.2 5.5 %collective-permute-start.17 = (bf16[32,1920]{1,0:T(8,128)(2,1)S(1)}, bf16[32,1920]{1,0:T(8,128)(2,1)S(1)}, u32[]{:S(2)}, u32[]{:S(2)}) collective-permute-start(bf16[32,1920]{1,0:T(8,128)(2,1)S(1)} %get-tuple-element.90), channel_id=1, source_target_pairs={{0,2},{1,3},{4,0},{5,1},{8,4},{9,5},{12,8},{13,9},{14,12},{15,13},... | collective-permute-start | bytes 368648 | tf_op jit(solution)/shard_map/ppermute | solution.py:454
  36.9 7.3 %collective-permute-start.19 = (bf16[128,512]{1,0:T(8,128)(2,1)S(1)}, bf16[128,512]{1,0:T(8,128)(2,1)S(1)}, u32[]{:S(2)}, u32[]{:S(2)}) collective-permute-start(bf16[128,512]{1,0:T(8,128)(2,1)S(1)} %get-tuple-element.80.refs_0_), channel_id=1, source_target_pairs={{0,1},{1,0},{2,3},{3,2},{4,5},{5,4},{6,7},{7,6},{8,9},{9,8},{10,11... | collective-permute-start | bytes 393224 | tf_op jit(solution)/shard_map/ppermute | solution.py:457
  37.0 5.7 %collective-permute-start.20 = (bf16[32,1920]{1,0:T(8,128)(2,1)S(1)}, bf16[32,1920]{1,0:T(8,128)(2,1)S(1)}, u32[]{:S(2)}, u32[]{:S(2)}) collective-permute-start(bf16[32,1920]{1,0:T(8,128)(2,1)S(1)} %get-tuple-element.89), channel_id=1, source_target_pairs={{0,4},{1,5},{4,8},{5,9},{8,12},{9,13},{12,14},{13,15},{14,10},{15,... | collective-permute-start | bytes 368648 | tf_op jit(solution)/shard_map/ppermute | solution.py:454
  41.7 7.3 %collective-permute-start.24 = (bf16[64,1920]{1,0:T(8,128)(2,1)S(1)}, bf16[64,1920]{1,0:T(8,128)(2,1)S(1)}, u32[]{:S(2)}, u32[]{:S(2)}) collective-permute-start(bf16[64,1920]{1,0:T(8,128)(2,1)S(1)} %pad_maximum_fusion.1), channel_id=1, source_target_pairs={{0,2},{1,3},{4,0},{5,1},{8,4},{9,5},{12,8},{13,9},{14,12},{15,13},... | collective-permute-start | bytes 737288 | tf_op jit(solution)/shard_map/ppermute | solution.py:454
  42.8 7.6 %collective-permute-start.21 = (bf16[64,1920]{1,0:T(8,128)(2,1)S(1)}, bf16[64,1920]{1,0:T(8,128)(2,1)S(1)}, u32[]{:S(2)}, u32[]{:S(2)}) collective-permute-start(bf16[64,1920]{1,0:T(8,128)(2,1)S(1)} %pad_maximum_fusion), channel_id=1, source_target_pairs={{0,4},{1,5},{4,8},{5,9},{8,12},{9,13},{12,14},{13,15},{14,10},{15,... | collective-permute-start | bytes 737288 | tf_op jit(solution)/shard_map/ppermute | solution.py:454
  49.1 6.4 %collective-permute-start.25 = (bf16[64,1920]{1,0:T(8,128)(2,1)S(1)}, bf16[64,1920]{1,0:T(8,128)(2,1)S(1)}, u32[]{:S(2)}, u32[]{:S(2)}) collective-permute-start(bf16[64,1920]{1,0:T(8,128)(2,1)S(1)} %add_convert_fusion), channel_id=1, source_target_pairs={{0,2},{1,3},{4,0},{5,1},{8,4},{9,5},{12,8},{13,9},{14,12},{15,13},... | collective-permute-start | bytes 737288 | tf_op jit(solution)/shard_map/ppermute | solution.py:454
  50.4 6.7 %collective-permute-start.22 = (bf16[64,1920]{1,0:T(8,128)(2,1)S(1)}, bf16[64,1920]{1,0:T(8,128)(2,1)S(1)}, u32[]{:S(2)}, u32[]{:S(2)}) collective-permute-start(bf16[64,1920]{1,0:T(8,128)(2,1)S(1)} %add_convert_fusion.1), channel_id=1, source_target_pairs={{0,4},{1,5},{4,8},{5,9},{8,12},{9,13},{12,14},{13,15},{14,10},{15,... | collective-permute-start | bytes 737288 | tf_op jit(solution)/shard_map/ppermute | solution.py:454
  51.9 1.3 %collective-permute-start.18 = (bf16[128,512]{1,0:T(8,128)(2,1)S(1)}, bf16[128,512]{1,0:T(8,128)(2,1)S(1)}, u32[]{:S(2)}, u32[]{:S(2)}) collective-permute-start(bf16[128,512]{1,0:T(8,128)(2,1)S(1)} %get-tuple-element.78.refs_0_), channel_id=1, source_target_pairs={{0,1},{1,0},{2,3},{3,2},{4,5},{5,4},{6,7},{7,6},{8,9},{9,8},{10,11... | collective-permute-start | bytes 393224 | tf_op jit(solution)/shard_map/ppermute | solution.py:457
  54.7 9.5 %copy-start.1 = (bf16[384,384]{1,0:T(8,128)(2,1)S(1)}, bf16[384,384]{1,0:T(8,128)(2,1)}, u32[]{:S(2)}) copy-start(bf16[384,384]{1,0:T(8,128)(2,1)} %constant.11.clone.order) | copy-start | bytes 884740
  55.5 6.2 %collective-permute-start.28 = (bf16[32,1920]{1,0:T(8,128)(2,1)S(1)}, bf16[32,1920]{1,0:T(8,128)(2,1)S(1)}, u32[]{:S(2)}, u32[]{:S(2)}) collective-permute-start(bf16[32,1920]{1,0:T(8,128)(2,1)S(1)} %get-tuple-element.88), channel_id=1, source_target_pairs={{0,2},{1,3},{4,0},{5,1},{8,4},{9,5},{12,8},{13,9},{14,12},{15,13},... | collective-permute-start | bytes 368648 | tf_op jit(solution)/shard_map/ppermute | solution.py:454
  57.1 4.9 %collective-permute-start.27 = (bf16[32,1920]{1,0:T(8,128)(2,1)S(1)}, bf16[32,1920]{1,0:T(8,128)(2,1)S(1)}, u32[]{:S(2)}, u32[]{:S(2)}) collective-permute-start(bf16[32,1920]{1,0:T(8,128)(2,1)S(1)} %get-tuple-element.87), channel_id=1, source_target_pairs={{0,4},{1,5},{4,8},{5,9},{8,12},{9,13},{12,14},{13,15},{14,10},{15,... | collective-permute-start | bytes 368648 | tf_op jit(solution)/shard_map/ppermute | solution.py:454
  58.7 4.9 %collective-permute-start.26 = (bf16[32,1920]{1,0:T(8,128)(2,1)S(1)}, bf16[32,1920]{1,0:T(8,128)(2,1)S(1)}, u32[]{:S(2)}, u32[]{:S(2)}) collective-permute-start(bf16[32,1920]{1,0:T(8,128)(2,1)S(1)} %get-tuple-element.86), channel_id=1, source_target_pairs={{0,2},{1,3},{4,0},{5,1},{8,4},{9,5},{12,8},{13,9},{14,12},{15,13},... | collective-permute-start | bytes 368648 | tf_op jit(solution)/shard_map/ppermute | solution.py:454
  59.2 4.9 %collective-permute-start.23 = (bf16[32,1920]{1,0:T(8,128)(2,1)S(1)}, bf16[32,1920]{1,0:T(8,128)(2,1)S(1)}, u32[]{:S(2)}, u32[]{:S(2)}) collective-permute-start(bf16[32,1920]{1,0:T(8,128)(2,1)S(1)} %get-tuple-element.82), channel_id=1, source_target_pairs={{0,4},{1,5},{4,8},{5,9},{8,12},{9,13},{12,14},{13,15},{14,10},{15,... | collective-permute-start | bytes 368648 | tf_op jit(solution)/shard_map/ppermute | solution.py:454
  62.1 2.0 %collective-permute-start.29 = (bf16[32,1920]{1,0:T(8,128)(2,1)S(1)}, bf16[32,1920]{1,0:T(8,128)(2,1)S(1)}, u32[]{:S(2)}, u32[]{:S(2)}) collective-permute-start(bf16[32,1920]{1,0:T(8,128)(2,1)S(1)} %give.1), channel_id=1, source_target_pairs={{0,1},{1,0},{2,3},{3,2},{4,5},{5,4},{6,7},{7,6},{8,9},{9,8},{10,11... | collective-permute-start | bytes 368648 | tf_op jit(solution)/shard_map/ppermute | solution.py:457

commit v3 on v2

--- a/solution.py
+++ b/solution.py
@@ -361,9 +361,10 @@
     )
     scale = 1.0 / math.sqrt(level_variance * 2 * half)
     produced = produced * (down_row[:1, :] * scale) * weight[:, :1]
-    rows = outs[0].shape[0]
-    for index, out in enumerate(outs):
-        out[...] = produced[index * rows : (index + 1) * rows]
+    start = 0
+    for out in outs:
+        out[...] = produced[start : start + out.shape[0]].astype(out.dtype)
+        start += out.shape[0]
 
 
 def last_join_kernel(part, came, mine, other):
@@ -552,12 +553,12 @@
         )
         return hidden, weight, swap(hidden)
 
-    def expert_out(stage, after=None):
+    def expert_out(stage, after=None, outs=None):
         hidden, weight, theirs = stage
         count = hidden.shape[0] // block_rows
         return whole_call(
             down_kernel,
-            [((block_rows, down_features), jnp.float32)] * count,
+            outs or [((block_rows, down_features), jnp.float32)] * count,
             "down_part",
             hidden,
             theirs,
@@ -611,9 +612,12 @@
 
     ahead, behind = {}, {}
     behind[3], ahead[3] = expert_out(third)
-    edge, own = expert_out(edge, after=ahead[3])
-    went_ahead = turn_hop(edge[:half].astype(jnp.bfloat16), 1)
-    went_behind = turn_hop(edge[half:].astype(jnp.bfloat16), -1)
+    piece = ((half, down_features), jnp.bfloat16)
+    edge_ahead, edge_behind, own = expert_out(
+        edge, after=ahead[3], outs=[piece, piece, ((block_rows, down_features), jnp.float32)]
+    )
+    went_ahead = turn_hop(edge_ahead, 1)
+    went_behind = turn_hop(edge_behind, -1)
     behind[2], ahead[2] = expert_out(second, after=went_behind)
     behind[1], ahead[1] = expert_out(near, after=went_behind)
     for distance in range(far - 1, 1, -1):

time: 65.3 us -> 65.3 us (level)
  no operation moved by 1% of the time
where the time goes in v3:
time: 65.3 us; the launch traced here: 65.1 us
  starting transfers between devices  27.7 us (42%)
  Pallas kernels  20.2 us (31%)
  waiting for transfers between devices  16.6 us (25%)
    pallas_call x18, Pallas kernels, whole_call(): pl.pallas_call(body, in_specs=specs, out_specs=[vmem] * len(outs), out_sh...  20.2 us
    ppermute x7, starting transfers between devices, hop(): return lax.ppermute(values, ('ep', 'tp'), pairs)  13.5 us
    ppermute x10, starting transfers between devices, turn_hop(): return lax.ppermute(values, ('ep', 'tp'), pairs)  11.8 us
    ppermute x10, waiting for transfers between devices, turn_hop(): return lax.ppermute(values, ('ep', 'tp'), pairs)  11.4 us
    ppermute x7, waiting for transfers between devices, hop(): return lax.ppermute(values, ('ep', 'tp'), pairs)  2.83 us
    ppermute x13, starting transfers between devices, swap(): return lax.ppermute(values, 'tp', [(0, 1), (1, 0)])  2.46 us
    ppermute x13, waiting for transfers between devices, swap(): return lax.ppermute(values, 'tp', [(0, 1), (1, 0)])  2.45 us
  transfers between devices with their start and end apart: 30, of which 18 were waited for; matrix products, arithmetic and copies ran while one was open for 0% of the time, Pallas kernels for 26%

profile of v3, /device:TPU:0, one launch (start us, length us, event | category | flops | bytes accessed | tf_op | source)
XLA Modules:
  0.0 65.1 jit_solution(2533776173180715825)
XLA Ops:
  0.0 0.5 collective-permute-start
  0.5 1.8 %first.1 = (f32[64,3840]{1,0:T(8,128)S(1)}, f32[3840]{0:T(1024)S(1)}, bf16[384,384]{1,0:T(8,128)(2,1)S(1)}, bf16[64,128]{1,0:T(8,128)(2,1)S(1)}, f32[640,512]{1,0:T(8,128)S(1)}) custom-call(bf16[64,3840]{1,0:T(8,128)(2,1)} %bitcast.8, bf16[64,3840]{1,0:T(8,128)(2,1)} %resid.1, f32[3840]{0:T(1024)} %gain.1, bf16[384,384]{1,0:T(8,128)(2,1)} %constant.8.clone.signs, ...), custom_call_target="tpu_custom_call" | custom-call | tf_op jit(solution)/shard_map/first/pallas_call | solution.py:413
  2.3 0.6 prep.2.first.refs_2_
  2.9 2.9 %collective-permute-start.1 = (bf16[32,3968]{1,0:T(8,128)(2,1)S(1)}, bf16[32,3968]{1,0:T(8,128)(2,1)S(1)}, u32[]{:S(2)}, u32[]{:S(2)}) collective-permute-start(bf16[32,3968]{1,0:T(8,128)(2,1)S(1)} %prep.2.first.refs_2_), channel_id=1, source_target_pairs={{0,4},{4,8},{8,12},{12,14},{14,10},{10,6},{6,2},{2,0},{1,3},{5,1},... | collective-permute-start | bytes 761864 | tf_op jit(solution)/shard_map/ppermute | solution.py:451
  5.8 0.6 prep.3.first.refs_3_
  6.4 1.6 %collective-permute-start.5 = (bf16[32,3968]{1,0:T(8,128)(2,1)S(1)}, bf16[32,3968]{1,0:T(8,128)(2,1)S(1)}, u32[]{:S(2)}, u32[]{:S(2)}) collective-permute-start(bf16[32,3968]{1,0:T(8,128)(2,1)S(1)} %prep.3.first.refs_3_), channel_id=1, source_target_pairs={{0,4},{4,8},{8,12},{12,14},{14,10},{10,6},{6,2},{2,0},{1,3},{5,1},... | collective-permute-start | bytes 761864 | tf_op jit(solution)/shard_map/ppermute | solution.py:451
  8.1 1.7 %unpack_gate.1 = (bf16[3840,512]{1,0:T(8,128)(2,1)S(1)}, f32[640,512]{1,0:T(8,128)S(1)}, f32[320,1024]{1,0:T(8,128)S(1)}) custom-call(bf16[32,3968]{1,0:T(8,128)(2,1)S(1)} %prep.3.first.refs_3_, f32[640,512]{1,0:T(8,128)} %bitcast.11, f32[320,1024]{1,0:T(8,128)} %bitcast.12, f32[640,512]{1,0:T(8,128)S(1)} %get-tuple-element.52.refs_2_), custom_call_target="tpu_custom_call" | custom-call | flops 10000000000 | tf_op jit(solution)/shard_map/unpack_gate/pallas_call | solution.py:413
  10.0 2.1 %collective-permute-start.2 = (bf16[32,3968]{1,0:T(8,128)(2,1)S(1)}, bf16[32,3968]{1,0:T(8,128)(2,1)S(1)}, u32[]{:S(2)}, u32[]{:S(2)}) collective-permute-start(bf16[32,3968]{1,0:T(8,128)(2,1)S(1)} %collective-permute-done.1.refs_0_), channel_id=1, source_target_pairs={{0,4},{4,8},{8,12},{12,14},{14,10},{10,6},{6,2},{2,0},{1,3},{5,1},... | collective-permute-start | bytes 761864 | tf_op jit(solution)/shard_map/ppermute | solution.py:451
  12.1 1.4 %unpack_up.1.refs_5_.first = bf16[3840,512]{1,0:T(8,128)(2,1)S(1)} custom-call(bf16[3840,512]{1,0:T(8,128)(2,1)S(1)} %get-tuple-element.53.first.refs_4_, f32[640,512]{1,0:T(8,128)S(1)} %get-tuple-element.55.refs_0_), custom_call_target="tpu_custom_call" | custom-call | flops 10000000000 | tf_op jit(solution)/shard_map/unpack_up/pallas_call | solution.py:413
  13.5 0.5 collective-permute-start.6
  14.0 1.6 %collective-permute-start.8 = (bf16[32,3968]{1,0:T(8,128)(2,1)S(1)}, bf16[32,3968]{1,0:T(8,128)(2,1)S(1)}, u32[]{:S(2)}, u32[]{:S(2)}) collective-permute-start(bf16[32,3968]{1,0:T(8,128)(2,1)S(1)} %collective-permute-done.5.refs_2_), channel_id=1, source_target_pairs={{0,4},{4,8},{8,12},{12,14},{14,10},{10,6},{6,2},{2,0},{1,3},{5,1},... | collective-permute-start | bytes 761864 | tf_op jit(solution)/shard_map/ppermute | solution.py:451
  15.6 0.6 collective-permute-done.2.refs_0_
  16.3 2.1 %collective-permute-start.3 = (bf16[32,3968]{1,0:T(8,128)(2,1)S(1)}, bf16[32,3968]{1,0:T(8,128)(2,1)S(1)}, u32[]{:S(2)}, u32[]{:S(2)}) collective-permute-start(bf16[32,3968]{1,0:T(8,128)(2,1)S(1)} %collective-permute-done.2.refs_0_), channel_id=1, source_target_pairs={{0,4},{4,8},{8,12},{12,14},{14,10},{10,6},{6,2},{2,0},{1,3},{5,1},... | collective-permute-start | bytes 761864 | tf_op jit(solution)/shard_map/ppermute | solution.py:451
  18.4 1.6 %unpack_down.1 = (bf16[1920,1024]{1,0:T(8,128)(2,1)S(1)}, f32[8,1920]{1,0:T(8,128)S(1)}) custom-call(bf16[3840,512]{1,0:T(8,128)(2,1)S(1)} %unpack_up.1.refs_5_.first, f32[320,1024]{1,0:T(8,128)S(1)} %get-tuple-element.58.refs_0_, f32[1,1920]{1,0:T(1,128)S(1)} %copy-done.4, bf16[384,384]{1,0:T(8,128)(2,1)S(1)} %copy-done.5), custom_call_target="tpu_custom_call" | custom-call | flops 10000000000 | tf_op jit(solution)/shard_map/unpack_down/pallas_call | solution.py:413
  20.6 1.6 %collective-permute-start.9 = (bf16[32,3968]{1,0:T(8,128)(2,1)S(1)}, bf16[32,3968]{1,0:T(8,128)(2,1)S(1)}, u32[]{:S(2)}, u32[]{:S(2)}) collective-permute-start(bf16[32,3968]{1,0:T(8,128)(2,1)S(1)} %collective-permute-done.8.refs_2_), channel_id=1, source_target_pairs={{0,4},{4,8},{8,12},{12,14},{14,10},{10,6},{6,2},{2,0},{1,3},{5,1},... | collective-permute-start | bytes 761864 | tf_op jit(solution)/shard_map/ppermute | solution.py:451
  22.2 1.4 %hidden_part.4 = (bf16[128,512]{1,0:T(8,128)(2,1)S(1)}, f32[128,128]{1,0:T(8,128)S(1)}) custom-call(bf16[32,3968]{1,0:T(8,128)(2,1)S(1)} %collective-permute-done.1.refs_0_, bf16[32,3968]{1,0:T(8,128)(2,1)S(1)} %collective-permute-done.4.refs_1_, bf16[32,3968]{1,0:T(8,128)(2,1)S(1)} %collective-permute-done.5.refs_2_, ...), custom_call_target="tpu_custom_call" | custom-call | flops 1000000000 | tf_op jit(solution)/shard_map/hidden_part/pallas_call | solution.py:413
  23.7 1.6 %collective-permute-start.12 = (bf16[32,3968]{1,0:T(8,128)(2,1)S(1)}, bf16[32,3968]{1,0:T(8,128)(2,1)S(1)}, u32[]{:S(2)}, u32[]{:S(2)}) collective-permute-start(bf16[32,3968]{1,0:T(8,128)(2,1)S(1)} %collective-permute-done.3.refs_0_), channel_id=1, source_target_pairs={{0,4},{4,8},{8,12},{12,14},{14,10},{10,6},{6,2},{2,0},{1,3},{5,1},... | collective-permute-start | bytes 761864 | tf_op jit(solution)/shard_map/ppermute | solution.py:451
  25.3 1.5 %collective-permute-done.9.refs_2_ = bf16[32,3968]{1,0:T(8,128)(2,1)S(1)} collective-permute-done((bf16[32,3968]{1,0:T(8,128)(2,1)S(1)}, bf16[32,3968]{1,0:T(8,128)(2,1)S(1)}, u32[]{:S(2)}, u32[]{:S(2)}) %collective-permute-start.9) | collective-permute-done | bytes 253984 | tf_op jit(solution)/shard_map/ppermute | solution.py:451
  26.9 1.4 %hidden_part.6 = (bf16[128,512]{1,0:T(8,128)(2,1)S(1)}, f32[128,128]{1,0:T(8,128)S(1)}) custom-call(bf16[32,3968]{1,0:T(8,128)(2,1)S(1)} %collective-permute-done.2.refs_0_, bf16[32,3968]{1,0:T(8,128)(2,1)S(1)} %collective-permute-done.13.refs_1_, bf16[32,3968]{1,0:T(8,128)(2,1)S(1)} %collective-permute-done.8.refs_2_, ...), custom_call_target="tpu_custom_call" | custom-call | flops 10000000000 | tf_op jit(solution)/shard_map/hidden_part/pallas_call | solution.py:413
  28.4 1.4 %hidden_part.5 = (bf16[128,512]{1,0:T(8,128)(2,1)S(1)}, f32[128,128]{1,0:T(8,128)S(1)}) custom-call(bf16[32,3968]{1,0:T(8,128)(2,1)S(1)} %collective-permute-done.3.refs_0_, bf16[32,3968]{1,0:T(8,128)(2,1)S(1)} %collective-permute-done.7.refs_1_, bf16[32,3968]{1,0:T(8,128)(2,1)S(1)} %collective-permute-done.9.refs_2_, ...), custom_call_target="tpu_custom_call" | custom-call | flops 1000000000 | tf_op jit(solution)/shard_map/hidden_part/pallas_call | solution.py:413
  30.0 0.3 collective-permute-start.15
  30.5 1.0 %collective-permute-done.15.refs_1_ = bf16[32,3968]{1,0:T(8,128)(2,1)S(1)} collective-permute-done((bf16[32,3968]{1,0:T(8,128)(2,1)S(1)}, bf16[32,3968]{1,0:T(8,128)(2,1)S(1)}, u32[]{:S(2)}, u32[]{:S(2)}) %collective-permute-start.15) | collective-permute-done | bytes 253984 | tf_op jit(solution)/shard_map/ppermute | solution.py:458
  31.6 1.4 %hidden_part.7 = (bf16[128,512]{1,0:T(8,128)(2,1)S(1)}, f32[128,128]{1,0:T(8,128)S(1)}) custom-call(bf16[32,3968]{1,0:T(8,128)(2,1)S(1)} %collective-permute-done.12.refs_0_, bf16[32,3968]{1,0:T(8,128)(2,1)S(1)} %collective-permute-done.15.refs_1_, bf16[32,3968]{1,0:T(8,128)(2,1)S(1)} %prep.2.first.refs_2_, bf16[32,3968]{1,0:T(8,128)(2,1)S(1)} %prep.3.first.refs_3_, ...), custom_call_target="tpu_custom_call" | custom-call | flops 1000000000 | tf_op jit(solution)/shard_map/hidden_part/pallas_call | solution.py:413
  33.0 0.4 collective-permute-start.16
  33.4 1.4 %down_part.4 = (f32[64,1920]{1,0:T(8,128)S(1)}, f32[64,1920]{1,0:T(8,128)S(1)}) custom-call(bf16[128,512]{1,0:T(8,128)(2,1)S(1)} %get-tuple-element.61.mine, bf16[128,512]{1,0:T(8,128)(2,1)S(1)} %collective-permute-done.11.theirs, bf16[1920,1024]{1,0:T(8,128)(2,1)S(1)} %get-tuple-element.62.levels.refs_2_, f32[8,1920]{1,0:T(8,128)S(1)} %get-tuple-element.59.down_row.refs_3_, ...), custom_call_target="tpu_custom_call" | custom-call | flops 503316480 | tf_op jit(solution)/shard_map/down_part/pallas_call | solution.py:413
  34.8 1.4 %down_part.5 = (bf16[32,1920]{1,0:T(8,128)(2,1)S(1)}, bf16[32,1920]{1,0:T(8,128)(2,1)S(1)}, f32[64,1920]{1,0:T(8,128)S(1)}) custom-call(f32[64,1920]{1,0:T(8,128)S(1)} %get-tuple-element.64.first, bf16[128,512]{1,0:T(8,128)(2,1)S(1)} %get-tuple-element.75.refs_0_, bf16[128,512]{1,0:T(8,128)(2,1)S(1)} %collective-permute-done.16.refs_1_, ...), custom_call_target="tpu_custom_call" | custom-call | flops 503316480 | tf_op jit(solution)/shard_map/down_part/pallas_call | solution.py:413
  36.1 0.7 %collective-permute-start.17 = (bf16[32,1920]{1,0:T(8,128)(2,1)S(1)}, bf16[32,1920]{1,0:T(8,128)(2,1)S(1)}, u32[]{:S(2)}, u32[]{:S(2)}) collective-permute-start(bf16[32,1920]{1,0:T(8,128)(2,1)S(1)} %get-tuple-element.78), channel_id=1, source_target_pairs={{0,2},{1,3},{4,0},{5,1},{8,4},{9,5},{12,8},{13,9},{14,12},{15,13},... | collective-permute-start | bytes 368648 | tf_op jit(solution)/shard_map/ppermute | solution.py:455
  37.0 1.4 %collective-permute-start.20 = (bf16[32,1920]{1,0:T(8,128)(2,1)S(1)}, bf16[32,1920]{1,0:T(8,128)(2,1)S(1)}, u32[]{:S(2)}, u32[]{:S(2)}) collective-permute-start(bf16[32,1920]{1,0:T(8,128)(2,1)S(1)} %get-tuple-element.83), channel_id=1, source_target_pairs={{0,4},{1,5},{4,8},{5,9},{8,12},{9,13},{12,14},{13,15},{14,10},{15,... | collective-permute-start | bytes 368648 | tf_op jit(solution)/shard_map/ppermute | solution.py:455
  38.3 3.3 %collective-permute-done.17.first = bf16[32,1920]{1,0:T(8,128)(2,1)S(1)} collective-permute-done((bf16[32,1920]{1,0:T(8,128)(2,1)S(1)}, bf16[32,1920]{1,0:T(8,128)(2,1)S(1)}, u32[]{:S(2)}, u32[]{:S(2)}) %collective-permute-start.17) | collective-permute-done | bytes 122912 | tf_op jit(solution)/shard_map/ppermute | solution.py:455
  41.7 0.9 %collective-permute-start.24 = (bf16[64,1920]{1,0:T(8,128)(2,1)S(1)}, bf16[64,1920]{1,0:T(8,128)(2,1)S(1)}, u32[]{:S(2)}, u32[]{:S(2)}) collective-permute-start(bf16[64,1920]{1,0:T(8,128)(2,1)S(1)} %pad_maximum_fusion.1), channel_id=1, source_target_pairs={{0,2},{1,3},{4,0},{5,1},{8,4},{9,5},{12,8},{13,9},{14,12},{15,13},... | collective-permute-start | bytes 737288 | tf_op jit(solution)/shard_map/ppermute | solution.py:455
  42.7 1.4 %collective-permute-start.21 = (bf16[64,1920]{1,0:T(8,128)(2,1)S(1)}, bf16[64,1920]{1,0:T(8,128)(2,1)S(1)}, u32[]{:S(2)}, u32[]{:S(2)}) collective-permute-start(bf16[64,1920]{1,0:T(8,128)(2,1)S(1)} %pad_maximum_fusion), channel_id=1, source_target_pairs={{0,4},{1,5},{4,8},{5,9},{8,12},{9,13},{12,14},{13,15},{14,10},{15,... | collective-permute-start | bytes 737288 | tf_op jit(solution)/shard_map/ppermute | solution.py:455
  44.2 1.4 %down_part.7 = (f32[64,1920]{1,0:T(8,128)S(1)}, f32[64,1920]{1,0:T(8,128)S(1)}) custom-call(bf16[32,1920]{1,0:T(8,128)(2,1)S(1)} %collective-permute-done.17.first, bf16[128,512]{1,0:T(8,128)(2,1)S(1)} %get-tuple-element.81.refs_0_, bf16[128,512]{1,0:T(8,128)(2,1)S(1)} %collective-permute-done.19.refs_1_, ...), custom_call_target="tpu_custom_call" | custom-call | flops 503316480 | tf_op jit(solution)/shard_map/down_part/pallas_call | solution.py:413
  45.5 3.4 %collective-permute-done.24 = bf16[64,1920]{1,0:T(8,128)(2,1)S(1)} collective-permute-done((bf16[64,1920]{1,0:T(8,128)(2,1)S(1)}, bf16[64,1920]{1,0:T(8,128)(2,1)S(1)}, u32[]{:S(2)}, u32[]{:S(2)}) %collective-permute-start.24) | collective-permute-done | bytes 245792 | tf_op jit(solution)/shard_map/ppermute | solution.py:455
  49.0 1.1 %collective-permute-start.25 = (bf16[64,1920]{1,0:T(8,128)(2,1)S(1)}, bf16[64,1920]{1,0:T(8,128)(2,1)S(1)}, u32[]{:S(2)}, u32[]{:S(2)}) collective-permute-start(bf16[64,1920]{1,0:T(8,128)(2,1)S(1)} %add_convert_fusion), channel_id=1, source_target_pairs={{0,2},{1,3},{4,0},{5,1},{8,4},{9,5},{12,8},{13,9},{14,12},{15,13},... | collective-permute-start | bytes 737288 | tf_op jit(solution)/shard_map/ppermute | solution.py:455
  50.4 1.5 %collective-permute-start.22 = (bf16[64,1920]{1,0:T(8,128)(2,1)S(1)}, bf16[64,1920]{1,0:T(8,128)(2,1)S(1)}, u32[]{:S(2)}, u32[]{:S(2)}) collective-permute-start(bf16[64,1920]{1,0:T(8,128)(2,1)S(1)} %add_convert_fusion.1), channel_id=1, source_target_pairs={{0,4},{1,5},{4,8},{5,9},{8,12},{9,13},{12,14},{13,15},{14,10},{15,... | collective-permute-start | bytes 737288 | tf_op jit(solution)/shard_map/ppermute | solution.py:455
  51.9 1.3 %collective-permute-done.18.refs_1_ = bf16[128,512]{1,0:T(8,128)(2,1)S(1)} collective-permute-done((bf16[128,512]{1,0:T(8,128)(2,1)S(1)}, bf16[128,512]{1,0:T(8,128)(2,1)S(1)}, u32[]{:S(2)}, u32[]{:S(2)}) %collective-permute-start.18) | collective-permute-done | bytes 131104 | tf_op jit(solution)/shard_map/ppermute | solution.py:458
  53.2 1.4 %down_part.6 = (f32[64,1920]{1,0:T(8,128)S(1)}, f32[64,1920]{1,0:T(8,128)S(1)}) custom-call(bf16[32,1920]{1,0:T(8,128)(2,1)S(1)} %collective-permute-done.17.first, bf16[128,512]{1,0:T(8,128)(2,1)S(1)} %get-tuple-element.79.refs_0_, bf16[128,512]{1,0:T(8,128)(2,1)S(1)} %collective-permute-done.18.refs_1_, ...), custom_call_target="tpu_custom_call" | custom-call | flops 503316480 | tf_op jit(solution)/shard_map/down_part/pallas_call | solution.py:413
  54.6 0.7 %collective-permute-done.25.came = bf16[64,1920]{1,0:T(8,128)(2,1)S(1)} collective-permute-done((bf16[64,1920]{1,0:T(8,128)(2,1)S(1)}, bf16[64,1920]{1,0:T(8,128)(2,1)S(1)}, u32[]{:S(2)}, u32[]{:S(2)}) %collective-permute-start.25) | collective-permute-done | bytes 245792 | tf_op jit(solution)/shard_map/ppermute | solution.py:455
  55.4 1.3 %collective-permute-start.28 = (bf16[32,1920]{1,0:T(8,128)(2,1)S(1)}, bf16[32,1920]{1,0:T(8,128)(2,1)S(1)}, u32[]{:S(2)}, u32[]{:S(2)}) collective-permute-start(bf16[32,1920]{1,0:T(8,128)(2,1)S(1)} %get-tuple-element.90), channel_id=1, source_target_pairs={{0,2},{1,3},{4,0},{5,1},{8,4},{9,5},{12,8},{13,9},{14,12},{15,13},... | collective-permute-start | bytes 368648 | tf_op jit(solution)/shard_map/ppermute | solution.py:455
  56.7 0.3 collective-permute-done.22.came
  57.1 1.6 %collective-permute-start.27 = (bf16[32,1920]{1,0:T(8,128)(2,1)S(1)}, bf16[32,1920]{1,0:T(8,128)(2,1)S(1)}, u32[]{:S(2)}, u32[]{:S(2)}) collective-permute-start(bf16[32,1920]{1,0:T(8,128)(2,1)S(1)} %get-tuple-element.89), channel_id=1, source_target_pairs={{0,4},{1,5},{4,8},{5,9},{8,12},{9,13},{12,14},{13,15},{14,10},{15,... | collective-permute-start | bytes 368648 | tf_op jit(solution)/shard_map/ppermute | solution.py:455
  58.7 0.5 collective-permute-start.26
  59.2 1.5 %collective-permute-start.23 = (bf16[32,1920]{1,0:T(8,128)(2,1)S(1)}, bf16[32,1920]{1,0:T(8,128)(2,1)S(1)}, u32[]{:S(2)}, u32[]{:S(2)}) collective-permute-start(bf16[32,1920]{1,0:T(8,128)(2,1)S(1)} %get-tuple-element.84), channel_id=1, source_target_pairs={{0,4},{1,5},{4,8},{5,9},{8,12},{9,13},{12,14},{13,15},{14,10},{15,... | collective-permute-start | bytes 368648 | tf_op jit(solution)/shard_map/ppermute | solution.py:455
  60.7 0.9 %collective-permute-done.28.behind = bf16[32,1920]{1,0:T(8,128)(2,1)S(1)} collective-permute-done((bf16[32,1920]{1,0:T(8,128)(2,1)S(1)}, bf16[32,1920]{1,0:T(8,128)(2,1)S(1)}, u32[]{:S(2)}, u32[]{:S(2)}) %collective-permute-start.28) | collective-permute-done | bytes 122912 | tf_op jit(solution)/shard_map/ppermute | solution.py:455
  61.6 0.4 collective-permute-done.27.ahead
  62.1 1.4 %collective-permute-done.26.behind = bf16[32,1920]{1,0:T(8,128)(2,1)S(1)} collective-permute-done((bf16[32,1920]{1,0:T(8,128)(2,1)S(1)}, bf16[32,1920]{1,0:T(8,128)(2,1)S(1)}, u32[]{:S(2)}, u32[]{:S(2)}) %collective-permute-start.26) | collective-permute-done | bytes 122912 | tf_op jit(solution)/shard_map/ppermute | solution.py:455
  63.5 0.5 collective-permute-done.23.ahead
  64.0 1.0 %close.1 = bf16[32,3840]{1,0:T(8,128)(2,1)} custom-call(f32[64,1920]{1,0:T(8,128)S(1)} %get-tuple-element.77.own, bf16[32,1920]{1,0:T(8,128)(2,1)S(1)} %collective-permute-done.23.ahead, bf16[32,1920]{1,0:T(8,128)(2,1)S(1)} %collective-permute-done.26.behind, bf16[32,1920]{1,0:T(8,128)(2,1)S(1)} %collective-permute-done.29.given, bf16[384,384]{1,0:T(8,128)(2,1)S(1)} %copy-done.1), custom_call_target="tpu_custom_call" | custom-call | tf_op jit(solution)/shard_map/close/pallas_call | solution.py:413
  (50 shorter events, 2.4 us)
Async XLA Ops:
  0.0 2.3 %collective-permute-start = (bf16[64,3840]{1,0:T(8,128)(2,1)}, bf16[64,3840]{1,0:T(8,128)(2,1)S(1)}, u32[]{:S(2)}, u32[]{:S(2)}) collective-permute-start(bf16[64,3840]{1,0:T(8,128)(2,1)} %bitcast.7), channel_id=1, source_target_pairs={{0,1},{1,0},{2,3},{3,2},{4,5},{5,4},{6,7},{7,6},{8,9},{9,8},{10,11... | collective-permute-start | bytes 1474568 | tf_op jit(solution)/shard_map/ppermute | solution.py:458
  2.9 7.0 %collective-permute-start.1 = (bf16[32,3968]{1,0:T(8,128)(2,1)S(1)}, bf16[32,3968]{1,0:T(8,128)(2,1)S(1)}, u32[]{:S(2)}, u32[]{:S(2)}) collective-permute-start(bf16[32,3968]{1,0:T(8,128)(2,1)S(1)} %prep.2.first.refs_2_), channel_id=1, source_target_pairs={{0,4},{4,8},{8,12},{12,14},{14,10},{10,6},{6,2},{2,0},{1,3},{5,1},... | collective-permute-start | bytes 761864 | tf_op jit(solution)/shard_map/ppermute | solution.py:451
  6.4 7.1 %collective-permute-start.5 = (bf16[32,3968]{1,0:T(8,128)(2,1)S(1)}, bf16[32,3968]{1,0:T(8,128)(2,1)S(1)}, u32[]{:S(2)}, u32[]{:S(2)}) collective-permute-start(bf16[32,3968]{1,0:T(8,128)(2,1)S(1)} %prep.3.first.refs_3_), channel_id=1, source_target_pairs={{0,4},{4,8},{8,12},{12,14},{14,10},{10,6},{6,2},{2,0},{1,3},{5,1},... | collective-permute-start | bytes 761864 | tf_op jit(solution)/shard_map/ppermute | solution.py:451
  10.0 6.3 %collective-permute-start.2 = (bf16[32,3968]{1,0:T(8,128)(2,1)S(1)}, bf16[32,3968]{1,0:T(8,128)(2,1)S(1)}, u32[]{:S(2)}, u32[]{:S(2)}) collective-permute-start(bf16[32,3968]{1,0:T(8,128)(2,1)S(1)} %collective-permute-done.1.refs_0_), channel_id=1, source_target_pairs={{0,4},{4,8},{8,12},{12,14},{14,10},{10,6},{6,2},{2,0},{1,3},{5,1},... | collective-permute-start | bytes 761864 | tf_op jit(solution)/shard_map/ppermute | solution.py:451
  12.1 6.3 %copy-start.4 = (f32[1,1920]{1,0:T(1,128)S(1)}, f32[1,1920]{1,0:T(1,128)}, u32[]{:S(2)}) copy-start(f32[1,1920]{1,0:T(1,128)} %refs_1_.1) | copy-start | bytes 23044
  12.1 6.3 %copy-start.5 = (bf16[384,384]{1,0:T(8,128)(2,1)S(1)}, bf16[384,384]{1,0:T(8,128)(2,1)}, u32[]{:S(2)}) copy-start(bf16[384,384]{1,0:T(8,128)(2,1)} %constant.10.clone.refs_2_) | copy-start | bytes 884740
  13.4 7.1 %collective-permute-start.4 = (bf16[32,3968]{1,0:T(8,128)(2,1)S(1)}, bf16[32,3968]{1,0:T(8,128)(2,1)S(1)}, u32[]{:S(2)}, u32[]{:S(2)}) collective-permute-start(bf16[32,3968]{1,0:T(8,128)(2,1)S(1)} %collective-permute-done.1.refs_0_), channel_id=1, source_target_pairs={{0,1},{1,0},{2,3},{3,2},{4,5},{5,4},{6,7},{7,6},{8,9},{9,8},{10,11... | collective-permute-start | bytes 761864 | tf_op jit(solution)/shard_map/ppermute | solution.py:458
  13.5 8.6 %collective-permute-start.6 = (bf16[32,3968]{1,0:T(8,128)(2,1)S(1)}, bf16[32,3968]{1,0:T(8,128)(2,1)S(1)}, u32[]{:S(2)}, u32[]{:S(2)}) collective-permute-start(bf16[32,3968]{1,0:T(8,128)(2,1)S(1)} %collective-permute-done.5.refs_2_), channel_id=1, source_target_pairs={{0,1},{1,0},{2,3},{3,2},{4,5},{5,4},{6,7},{7,6},{8,9},{9,8},{10,11... | collective-permute-start | bytes 761864 | tf_op jit(solution)/shard_map/ppermute | solution.py:458
  14.0 6.3 %collective-permute-start.8 = (bf16[32,3968]{1,0:T(8,128)(2,1)S(1)}, bf16[32,3968]{1,0:T(8,128)(2,1)S(1)}, u32[]{:S(2)}, u32[]{:S(2)}) collective-permute-start(bf16[32,3968]{1,0:T(8,128)(2,1)S(1)} %collective-permute-done.5.refs_2_), channel_id=1, source_target_pairs={{0,4},{4,8},{8,12},{12,14},{14,10},{10,6},{6,2},{2,0},{1,3},{5,1},... | collective-permute-start | bytes 761864 | tf_op jit(solution)/shard_map/ppermute | solution.py:451
  16.3 7.4 %collective-permute-start.3 = (bf16[32,3968]{1,0:T(8,128)(2,1)S(1)}, bf16[32,3968]{1,0:T(8,128)(2,1)S(1)}, u32[]{:S(2)}, u32[]{:S(2)}) collective-permute-start(bf16[32,3968]{1,0:T(8,128)(2,1)S(1)} %collective-permute-done.2.refs_0_), channel_id=1, source_target_pairs={{0,4},{4,8},{8,12},{12,14},{14,10},{10,6},{6,2},{2,0},{1,3},{5,1},... | collective-permute-start | bytes 761864 | tf_op jit(solution)/shard_map/ppermute | solution.py:451
  18.4 3.8 %copy-start = (bf16[256,256]{1,0:T(8,128)(2,1)S(1)}, bf16[256,256]{1,0:T(8,128)(2,1)}, u32[]{:S(2)}) copy-start(bf16[256,256]{1,0:T(8,128)(2,1)} %constant.9.clone.refs_8_) | copy-start | bytes 393220
  18.4 3.8 %copy-start.2 = (f32[1,512]{1,0:T(1,128)S(1)}, f32[1,512]{1,0:T(1,128)}, u32[]{:S(2)}) copy-start(f32[1,512]{1,0:T(1,128)} %refs_6_.7) | copy-start | bytes 6148
  18.4 3.8 %copy-start.3 = (f32[1,512]{1,0:T(1,128)S(1)}, f32[1,512]{1,0:T(1,128)}, u32[]{:S(2)}) copy-start(f32[1,512]{1,0:T(1,128)} %refs_7_.7) | copy-start | bytes 6148
  20.0 6.9 %collective-permute-start.13 = (bf16[32,3968]{1,0:T(8,128)(2,1)S(1)}, bf16[32,3968]{1,0:T(8,128)(2,1)S(1)}, u32[]{:S(2)}, u32[]{:S(2)}) collective-permute-start(bf16[32,3968]{1,0:T(8,128)(2,1)S(1)} %collective-permute-done.2.refs_0_), channel_id=1, source_target_pairs={{0,1},{1,0},{2,3},{3,2},{4,5},{5,4},{6,7},{7,6},{8,9},{9,8},{10,11... | collective-permute-start | bytes 761864 | tf_op jit(solution)/shard_map/ppermute | solution.py:458
  20.3 6.6 %collective-permute-start.14 = (bf16[32,3968]{1,0:T(8,128)(2,1)S(1)}, bf16[32,3968]{1,0:T(8,128)(2,1)S(1)}, u32[]{:S(2)}, u32[]{:S(2)}) collective-permute-start(bf16[32,3968]{1,0:T(8,128)(2,1)S(1)} %collective-permute-done.8.refs_2_), channel_id=1, source_target_pairs={{0,1},{1,0},{2,3},{3,2},{4,5},{5,4},{6,7},{7,6},{8,9},{9,8},{10,11... | collective-permute-start | bytes 761864 | tf_op jit(solution)/shard_map/ppermute | solution.py:458
  20.6 6.3 %collective-permute-start.9 = (bf16[32,3968]{1,0:T(8,128)(2,1)S(1)}, bf16[32,3968]{1,0:T(8,128)(2,1)S(1)}, u32[]{:S(2)}, u32[]{:S(2)}) collective-permute-start(bf16[32,3968]{1,0:T(8,128)(2,1)S(1)} %collective-permute-done.8.refs_2_), channel_id=1, source_target_pairs={{0,4},{4,8},{8,12},{12,14},{14,10},{10,6},{6,2},{2,0},{1,3},{5,1},... | collective-permute-start | bytes 761864 | tf_op jit(solution)/shard_map/ppermute | solution.py:451
  23.6 3.3 %collective-permute-start.7 = (bf16[32,3968]{1,0:T(8,128)(2,1)S(1)}, bf16[32,3968]{1,0:T(8,128)(2,1)S(1)}, u32[]{:S(2)}, u32[]{:S(2)}) collective-permute-start(bf16[32,3968]{1,0:T(8,128)(2,1)S(1)} %collective-permute-done.3.refs_0_), channel_id=1, source_target_pairs={{0,1},{1,0},{2,3},{3,2},{4,5},{5,4},{6,7},{7,6},{8,9},{9,8},{10,11... | collective-permute-start | bytes 761864 | tf_op jit(solution)/shard_map/ppermute | solution.py:458
  23.7 6.3 %collective-permute-start.12 = (bf16[32,3968]{1,0:T(8,128)(2,1)S(1)}, bf16[32,3968]{1,0:T(8,128)(2,1)S(1)}, u32[]{:S(2)}, u32[]{:S(2)}) collective-permute-start(bf16[32,3968]{1,0:T(8,128)(2,1)S(1)} %collective-permute-done.3.refs_0_), channel_id=1, source_target_pairs={{0,4},{4,8},{8,12},{12,14},{14,10},{10,6},{6,2},{2,0},{1,3},{5,1},... | collective-permute-start | bytes 761864 | tf_op jit(solution)/shard_map/ppermute | solution.py:451
  26.9 1.5 %collective-permute-start.10 = (bf16[32,3968]{1,0:T(8,128)(2,1)S(1)}, bf16[32,3968]{1,0:T(8,128)(2,1)S(1)}, u32[]{:S(2)}, u32[]{:S(2)}) collective-permute-start(bf16[32,3968]{1,0:T(8,128)(2,1)S(1)} %collective-permute-done.9.refs_2_), channel_id=1, source_target_pairs={{0,1},{1,0},{2,3},{3,2},{4,5},{5,4},{6,7},{7,6},{8,9},{9,8},{10,11... | collective-permute-start | bytes 761864 | tf_op jit(solution)/shard_map/ppermute | solution.py:458
  30.0 1.5 %collective-permute-start.15 = (bf16[32,3968]{1,0:T(8,128)(2,1)S(1)}, bf16[32,3968]{1,0:T(8,128)(2,1)S(1)}, u32[]{:S(2)}, u32[]{:S(2)}) collective-permute-start(bf16[32,3968]{1,0:T(8,128)(2,1)S(1)} %collective-permute-done.12.refs_0_), channel_id=1, source_target_pairs={{0,1},{1,0},{2,3},{3,2},{4,5},{5,4},{6,7},{7,6},{8,9},{9,8},{10,11... | collective-permute-start | bytes 761864 | tf_op jit(solution)/shard_map/ppermute | solution.py:458
  30.4 3.0 %collective-permute-start.11 = (bf16[128,512]{1,0:T(8,128)(2,1)S(1)}, bf16[128,512]{1,0:T(8,128)(2,1)S(1)}, u32[]{:S(2)}, u32[]{:S(2)}) collective-permute-start(bf16[128,512]{1,0:T(8,128)(2,1)S(1)} %get-tuple-element.61.mine), channel_id=1, source_target_pairs={{0,1},{1,0},{2,3},{3,2},{4,5},{5,4},{6,7},{7,6},{8,9},{9,8},{10,11... | collective-permute-start | bytes 393224 | tf_op jit(solution)/shard_map/ppermute | solution.py:458
  33.0 1.8 %collective-permute-start.16 = (bf16[128,512]{1,0:T(8,128)(2,1)S(1)}, bf16[128,512]{1,0:T(8,128)(2,1)S(1)}, u32[]{:S(2)}, u32[]{:S(2)}) collective-permute-start(bf16[128,512]{1,0:T(8,128)(2,1)S(1)} %get-tuple-element.75.refs_0_), channel_id=1, source_target_pairs={{0,1},{1,0},{2,3},{3,2},{4,5},{5,4},{6,7},{7,6},{8,9},{9,8},{10,11... | collective-permute-start | bytes 393224 | tf_op jit(solution)/shard_map/ppermute | solution.py:458
  36.1 5.5 %collective-permute-start.17 = (bf16[32,1920]{1,0:T(8,128)(2,1)S(1)}, bf16[32,1920]{1,0:T(8,128)(2,1)S(1)}, u32[]{:S(2)}, u32[]{:S(2)}) collective-permute-start(bf16[32,1920]{1,0:T(8,128)(2,1)S(1)} %get-tuple-element.78), channel_id=1, source_target_pairs={{0,2},{1,3},{4,0},{5,1},{8,4},{9,5},{12,8},{13,9},{14,12},{15,13},... | collective-permute-start | bytes 368648 | tf_op jit(solution)/shard_map/ppermute | solution.py:455
  36.8 7.3 %collective-permute-start.19 = (bf16[128,512]{1,0:T(8,128)(2,1)S(1)}, bf16[128,512]{1,0:T(8,128)(2,1)S(1)}, u32[]{:S(2)}, u32[]{:S(2)}) collective-permute-start(bf16[128,512]{1,0:T(8,128)(2,1)S(1)} %get-tuple-element.81.refs_0_), channel_id=1, source_target_pairs={{0,1},{1,0},{2,3},{3,2},{4,5},{5,4},{6,7},{7,6},{8,9},{9,8},{10,11... | collective-permute-start | bytes 393224 | tf_op jit(solution)/shard_map/ppermute | solution.py:458
  37.0 5.7 %collective-permute-start.20 = (bf16[32,1920]{1,0:T(8,128)(2,1)S(1)}, bf16[32,1920]{1,0:T(8,128)(2,1)S(1)}, u32[]{:S(2)}, u32[]{:S(2)}) collective-permute-start(bf16[32,1920]{1,0:T(8,128)(2,1)S(1)} %get-tuple-element.83), channel_id=1, source_target_pairs={{0,4},{1,5},{4,8},{5,9},{8,12},{9,13},{12,14},{13,15},{14,10},{15,... | collective-permute-start | bytes 368648 | tf_op jit(solution)/shard_map/ppermute | solution.py:455
  41.7 7.3 %collective-permute-start.24 = (bf16[64,1920]{1,0:T(8,128)(2,1)S(1)}, bf16[64,1920]{1,0:T(8,128)(2,1)S(1)}, u32[]{:S(2)}, u32[]{:S(2)}) collective-permute-start(bf16[64,1920]{1,0:T(8,128)(2,1)S(1)} %pad_maximum_fusion.1), channel_id=1, source_target_pairs={{0,2},{1,3},{4,0},{5,1},{8,4},{9,5},{12,8},{13,9},{14,12},{15,13},... | collective-permute-start | bytes 737288 | tf_op jit(solution)/shard_map/ppermute | solution.py:455
  42.7 7.6 %collective-permute-start.21 = (bf16[64,1920]{1,0:T(8,128)(2,1)S(1)}, bf16[64,1920]{1,0:T(8,128)(2,1)S(1)}, u32[]{:S(2)}, u32[]{:S(2)}) collective-permute-start(bf16[64,1920]{1,0:T(8,128)(2,1)S(1)} %pad_maximum_fusion), channel_id=1, source_target_pairs={{0,4},{1,5},{4,8},{5,9},{8,12},{9,13},{12,14},{13,15},{14,10},{15,... | collective-permute-start | bytes 737288 | tf_op jit(solution)/shard_map/ppermute | solution.py:455
  49.0 6.4 %collective-permute-start.25 = (bf16[64,1920]{1,0:T(8,128)(2,1)S(1)}, bf16[64,1920]{1,0:T(8,128)(2,1)S(1)}, u32[]{:S(2)}, u32[]{:S(2)}) collective-permute-start(bf16[64,1920]{1,0:T(8,128)(2,1)S(1)} %add_convert_fusion), channel_id=1, source_target_pairs={{0,2},{1,3},{4,0},{5,1},{8,4},{9,5},{12,8},{13,9},{14,12},{15,13},... | collective-permute-start | bytes 737288 | tf_op jit(solution)/shard_map/ppermute | solution.py:455
  50.4 6.7 %collective-permute-start.22 = (bf16[64,1920]{1,0:T(8,128)(2,1)S(1)}, bf16[64,1920]{1,0:T(8,128)(2,1)S(1)}, u32[]{:S(2)}, u32[]{:S(2)}) collective-permute-start(bf16[64,1920]{1,0:T(8,128)(2,1)S(1)} %add_convert_fusion.1), channel_id=1, source_target_pairs={{0,4},{1,5},{4,8},{5,9},{8,12},{9,13},{12,14},{13,15},{14,10},{15,... | collective-permute-start | bytes 737288 | tf_op jit(solution)/shard_map/ppermute | solution.py:455
  51.9 1.3 %collective-permute-start.18 = (bf16[128,512]{1,0:T(8,128)(2,1)S(1)}, bf16[128,512]{1,0:T(8,128)(2,1)S(1)}, u32[]{:S(2)}, u32[]{:S(2)}) collective-permute-start(bf16[128,512]{1,0:T(8,128)(2,1)S(1)} %get-tuple-element.79.refs_0_), channel_id=1, source_target_pairs={{0,1},{1,0},{2,3},{3,2},{4,5},{5,4},{6,7},{7,6},{8,9},{9,8},{10,11... | collective-permute-start | bytes 393224 | tf_op jit(solution)/shard_map/ppermute | solution.py:458
  54.6 9.4 %copy-start.1 = (bf16[384,384]{1,0:T(8,128)(2,1)S(1)}, bf16[384,384]{1,0:T(8,128)(2,1)}, u32[]{:S(2)}) copy-start(bf16[384,384]{1,0:T(8,128)(2,1)} %constant.11.clone.order) | copy-start | bytes 884740
  55.4 6.2 %collective-permute-start.28 = (bf16[32,1920]{1,0:T(8,128)(2,1)S(1)}, bf16[32,1920]{1,0:T(8,128)(2,1)S(1)}, u32[]{:S(2)}, u32[]{:S(2)}) collective-permute-start(bf16[32,1920]{1,0:T(8,128)(2,1)S(1)} %get-tuple-element.90), channel_id=1, source_target_pairs={{0,2},{1,3},{4,0},{5,1},{8,4},{9,5},{12,8},{13,9},{14,12},{15,13},... | collective-permute-start | bytes 368648 | tf_op jit(solution)/shard_map/ppermute | solution.py:455
  57.1 4.9 %collective-permute-start.27 = (bf16[32,1920]{1,0:T(8,128)(2,1)S(1)}, bf16[32,1920]{1,0:T(8,128)(2,1)S(1)}, u32[]{:S(2)}, u32[]{:S(2)}) collective-permute-start(bf16[32,1920]{1,0:T(8,128)(2,1)S(1)} %get-tuple-element.89), channel_id=1, source_target_pairs={{0,4},{1,5},{4,8},{5,9},{8,12},{9,13},{12,14},{13,15},{14,10},{15,... | collective-permute-start | bytes 368648 | tf_op jit(solution)/shard_map/ppermute | solution.py:455
  58.7 4.9 %collective-permute-start.26 = (bf16[32,1920]{1,0:T(8,128)(2,1)S(1)}, bf16[32,1920]{1,0:T(8,128)(2,1)S(1)}, u32[]{:S(2)}, u32[]{:S(2)}) collective-permute-start(bf16[32,1920]{1,0:T(8,128)(2,1)S(1)} %get-tuple-element.88), channel_id=1, source_target_pairs={{0,2},{1,3},{4,0},{5,1},{8,4},{9,5},{12,8},{13,9},{14,12},{15,13},... | collective-permute-start | bytes 368648 | tf_op jit(solution)/shard_map/ppermute | solution.py:455
  59.2 4.9 %collective-permute-start.23 = (bf16[32,1920]{1,0:T(8,128)(2,1)S(1)}, bf16[32,1920]{1,0:T(8,128)(2,1)S(1)}, u32[]{:S(2)}, u32[]{:S(2)}) collective-permute-start(bf16[32,1920]{1,0:T(8,128)(2,1)S(1)} %get-tuple-element.84), channel_id=1, source_target_pairs={{0,4},{1,5},{4,8},{5,9},{8,12},{9,13},{12,14},{13,15},{14,10},{15,... | collective-permute-start | bytes 368648 | tf_op jit(solution)/shard_map/ppermute | solution.py:455
  62.1 2.0 %collective-permute-start.29 = (bf16[32,1920]{1,0:T(8,128)(2,1)S(1)}, bf16[32,1920]{1,0:T(8,128)(2,1)S(1)}, u32[]{:S(2)}, u32[]{:S(2)}) collective-permute-start(bf16[32,1920]{1,0:T(8,128)(2,1)S(1)} %give.1), channel_id=1, source_target_pairs={{0,1},{1,0},{2,3},{3,2},{4,5},{5,4},{6,7},{7,6},{8,9},{9,8},{10,11... | collective-permute-start | bytes 368648 | tf_op jit(solution)/shard_map/ppermute | solution.py:458
